TPU v7x, 32 devices: a whole 2x2x4 slice. The times are simulated.
32 devices in a mesh: expert: 16 (over z, y, x), tensor: 2 (over core).
Axes of the slice: x: 2, y: 2, z: 4, core: 2. Of those that a mesh axis runs over, the one named last changes fastest.
Arguments:
- tokens: bfloat16 [36864, 768], P(('expert', 'tensor')), may hold values from -6 to 6
- gains: float32 [768], replicated, may hold values from 0.5 to 1.5
- shifts: float32 [768], replicated, may hold values from -1 to 1
- projection: bfloat16 [768, 2304], replicated, may hold values from -0.21875 to 0.21875
- mixing: bfloat16 [768, 768], replicated, may hold values from -0.875 to 0.875
- factors: float32 [768], replicated, may hold values from 0.5 to 1.5
- biases: float32 [768], replicated, may hold values from -1 to 1
- centroids: bfloat16 [4, 768], replicated, may hold values from -0.15625 to 0.15625
- expanding: bfloat16 [16, 768, 768], P('expert', None, 'tensor'), may hold values from -0.21875 to 0.21875
- contracting: bfloat16 [16, 768, 768], P('expert', 'tensor'), may hold values from -0.21875 to 0.21875
- routes: int32 [36864, 1], P(('expert', 'tensor')), may hold values from 0 to 3; in each aligned block of 1152 rows (0 to 1151, 1152 to 2303, ...) at most 576 rows name the same one
- lengths: int32 [32, 4], P(('expert', 'tensor')), may hold values from 1 to 1024, 1152 in all within a row
- cotangent: bfloat16 [36864, 768], P(('expert', 'tensor')), may hold values from -6 to 6
Outputs:
- layer_output: bfloat16 [36864, 768], P(('expert', 'tensor'))
- balance: float32 [], replicated
- grad_tokens: float32 [36864, 768], P(('expert', 'tensor'))
- grad_gains: float32 [768], replicated
- grad_shifts: float32 [768], replicated
- grad_projection: float32 [768, 2304], replicated
- grad_mixing: float32 [768, 768], replicated
- grad_factors: float32 [768], replicated
- grad_biases: float32 [768], replicated
- grad_centroids: float32 [4, 768], replicated
- grad_expanding: float32 [16, 768, 768], P('expert', None, 'tensor')
- grad_contracting: float32 [16, 768, 768], P('expert', 'tensor')
Inputs may be any that keep to these rules, and one draw needn't show every extreme that they name: `routes`: in each device's block of 1152 rows no expert is named more than 576 times, a bound that some block reaches. `lengths`: each row sums to 1152; its largest entry is 1024.
All inputs are finite; a program needn't handle non-finite values.
Results may differ from a plain program's by a relative error of at most 0.014.
Values may be sent and summed in bfloat16 or wider, within the bound.
A program may use at most 384 MiB of HBM per device.

v0:
```python
from functools import partial

import jax
import jax.numpy as jnp
from jax import lax
from jax.sharding import PartitionSpec as P

HEADS = 12


highest = lax.Precision.HIGHEST
epsilon = 1e-05


def norm_parts(values, gain, shift):
    centered = values - jnp.mean(values, axis=1, keepdims=True)
    scale = lax.rsqrt(jnp.mean(centered * centered, axis=1, keepdims=True) + epsilon)
    normal = centered * scale
    return (normal * gain + shift, normal, scale)


def norm_back(upstream, normal, scale, gain):
    scaled = upstream * gain
    inner = (
        scaled
        - jnp.mean(scaled, axis=1, keepdims=True)
        - normal * jnp.mean(scaled * normal, axis=1, keepdims=True)
    )
    return (inner * scale, jnp.sum(upstream * normal, axis=0), jnp.sum(upstream, axis=0))


def gelu_slope(values):
    return (
        0.5 * (1.0 + lax.erf(values * 0.7071067811865476))
        + values * jnp.exp(-0.5 * values * values) * 0.3989422804014327
    )


def expert_forward(gathered, upward, downward):
    before = jnp.dot(gathered, upward, preferred_element_type=jnp.float32)
    active = jax.nn.gelu(before, approximate=False).astype(jnp.bfloat16)
    return jnp.dot(active, downward, preferred_element_type=jnp.float32)


def expert_backward(gathered, incoming, upward, downward):
    before = jnp.dot(gathered, upward, preferred_element_type=jnp.float32)
    active = jax.nn.gelu(before, approximate=False).astype(jnp.bfloat16)
    down_grad = jnp.einsum("rf,rd->fd", active, incoming, preferred_element_type=jnp.float32)
    through = jnp.einsum("rd,fd->rf", incoming, downward, preferred_element_type=jnp.float32)
    hidden_grad = (through * gelu_slope(before)).astype(jnp.bfloat16)
    up_grad = jnp.einsum("rd,rf->df", gathered, hidden_grad, preferred_element_type=jnp.float32)
    return (up_grad, down_grad, hidden_grad)


def head_forward(allowed, item):
    query, keys, values = item
    factor = query.shape[1] ** (-0.5)
    scores = jnp.einsum("qd,kd->qk", query, keys, preferred_element_type=jnp.float32) * factor
    scores = jnp.where(allowed, scores, -1000000000.0)
    peak = jnp.max(scores, axis=1, keepdims=True)
    weights = jnp.exp(scores - peak)
    total = jnp.sum(weights, axis=1, keepdims=True)
    mixed = jnp.dot(
        (weights / total).astype(jnp.bfloat16), values, preferred_element_type=jnp.float32
    )
    return (mixed.astype(jnp.bfloat16), (peak + jnp.log(total))[:, 0])


def head_backward(allowed, item):
    query, keys, values, upstream, log_total = item
    factor = query.shape[1] ** (-0.5)
    scores = jnp.einsum("qd,kd->qk", query, keys, preferred_element_type=jnp.float32) * factor
    scores = jnp.where(allowed, scores, -1000000000.0)
    probs = jnp.exp(scores - log_total[:, None])
    value_grad = jnp.einsum(
        "qk,qd->kd", probs.astype(jnp.bfloat16), upstream, preferred_element_type=jnp.float32
    )
    prob_grad = jnp.einsum("qd,kd->qk", upstream, values, preferred_element_type=jnp.float32)
    inner = jnp.sum(prob_grad * probs, axis=1, keepdims=True)
    score_grad = (probs * (prob_grad - inner)).astype(jnp.bfloat16)
    query_grad = (
        jnp.einsum("qk,kd->qd", score_grad, keys, preferred_element_type=jnp.float32) * factor
    )
    key_grad = (
        jnp.einsum("qk,qd->kd", score_grad, query, preferred_element_type=jnp.float32) * factor
    )
    return (query_grad, key_grad, value_grad)


def per_device(
    tokens,
    gains,
    shifts,
    projection,
    mixing,
    factors,
    biases,
    centroids,
    expanding,
    contracting,
    routes,
    lengths,
    cotangent,
):
    count, width = tokens.shape
    experts = centroids.shape[0]
    groups = lax.axis_size("expert")
    slab_count = groups // experts
    capacity = max(2, 2 * count // experts)
    total_tokens = count * groups * lax.axis_size("tensor")
    average = total_tokens / experts
    route = routes[:, 0]
    picks = route[:, None] == jnp.arange(experts, dtype=jnp.int32)[None, :]
    picks_int = picks.astype(jnp.int32)
    picks_float = picks.astype(jnp.float32)
    loads = lax.psum(jnp.sum(picks_float, axis=0), ("expert", "tensor"))
    spread = (loads - average) / average
    token_spread = jnp.sum(jnp.where(picks, spread[None, :], 0.0), axis=1)
    ranks = jnp.sum((jnp.cumsum(picks_int, axis=0) - picks_int) * picks_int, axis=1)
    slots = route * capacity + ranks
    places = jnp.arange(count, dtype=jnp.int32)
    documents = jnp.sum(
        (places[:, None] >= jnp.cumsum(lengths[0])[None, :]).astype(jnp.int32), axis=1
    )
    allowed = (places[:, None] >= places[None, :]) & (documents[:, None] == documents[None, :])
    inputs = tokens.astype(jnp.float32)
    entry, entry_normal, entry_scale = norm_parts(inputs, gains, shifts)
    entry = entry.astype(jnp.bfloat16)
    joint = jnp.dot(entry, projection, preferred_element_type=jnp.float32).astype(jnp.bfloat16)
    heads = joint.reshape(count, 3, HEADS, width // HEADS).transpose(1, 2, 0, 3)
    mixed, log_total = lax.map(partial(head_forward, allowed), (heads[0], heads[1], heads[2]))
    mixed_rows = mixed.transpose(1, 0, 2).reshape(count, width)
    residual = inputs + jnp.dot(mixed_rows, mixing, preferred_element_type=jnp.float32)
    normed, mixer_normal, mixer_scale = norm_parts(residual, factors, biases)
    chosen = jnp.dot(picks.astype(jnp.bfloat16), centroids, preferred_element_type=jnp.float32)
    gates = jax.nn.sigmoid(jnp.sum(normed * chosen, axis=1))
    outgoing = (
        jnp.zeros((experts * capacity, width), jnp.bfloat16)
        .at[slots]
        .set(normed.astype(jnp.bfloat16))
    )
    copies = jnp.broadcast_to(
        outgoing.reshape(experts, 1, capacity, width), (experts, slab_count, capacity, width)
    ).reshape(groups, capacity, width)
    arrived = lax.all_to_all(copies, "expert", split_axis=0, concat_axis=0, tiled=True)
    sources = groups * capacity
    own_rows = arrived.reshape(sources, width)
    gathered = lax.all_gather(own_rows, "tensor", axis=0, tiled=True)
    produced = lax.psum_scatter(
        expert_forward(gathered, expanding[0], contracting[0]).astype(jnp.bfloat16),
        "tensor",
        scatter_dimension=0,
        tiled=True,
    )
    returned = lax.all_to_all(
        produced.reshape(arrived.shape), "expert", split_axis=0, concat_axis=0, tiled=True
    )
    combined = jnp.sum(
        returned.reshape(experts, slab_count, capacity, width).astype(jnp.float32), axis=1
    ).reshape(experts * capacity, width)
    picked = combined[slots]
    layer_output = (residual + gates[:, None] * picked).astype(jnp.bfloat16)
    balance_part = jnp.sum(token_spread * gates) / total_tokens
    upstream = cotangent.astype(jnp.float32)
    gate_grad = jnp.sum(upstream * picked, axis=1)
    logit_grad = (gate_grad + token_spread / total_tokens) * gates * (1.0 - gates)
    scaled_rows = (gates[:, None] * upstream).astype(jnp.bfloat16)
    grad_slots = jnp.zeros((experts * capacity, width), jnp.bfloat16).at[slots].set(scaled_rows)
    grad_copies = jnp.broadcast_to(
        grad_slots.reshape(experts, 1, capacity, width), (experts, slab_count, capacity, width)
    ).reshape(groups, capacity, width)
    incoming = lax.all_to_all(
        grad_copies, "expert", split_axis=0, concat_axis=0, tiled=True
    ).reshape(sources, width)
    incoming_pair = lax.all_gather(incoming, "tensor", axis=0, tiled=True)
    up_share, down_share, hidden_grad = expert_backward(
        gathered, incoming_pair, expanding[0], contracting[0]
    )
    back_rows = lax.psum_scatter(
        jnp.einsum(
            "rf,df->rd", hidden_grad, expanding[0], preferred_element_type=jnp.float32
        ).astype(jnp.bfloat16),
        "tensor",
        scatter_dimension=0,
        tiled=True,
    )
    back = lax.all_to_all(
        back_rows.reshape(arrived.shape), "expert", split_axis=0, concat_axis=0, tiled=True
    )
    back_sum = jnp.sum(
        back.reshape(experts, slab_count, capacity, width).astype(jnp.float32), axis=1
    ).reshape(experts * capacity, width)
    normed_grad = back_sum[slots] + logit_grad[:, None] * chosen
    centroid_grad = jnp.einsum(
        "te,td->ed", picks_float, logit_grad[:, None] * normed, precision=highest
    )
    mixer_back, factor_grad, bias_grad = norm_back(normed_grad, mixer_normal, mixer_scale, factors)
    residual_grad = upstream + mixer_back
    branch_grad = residual_grad.astype(jnp.bfloat16)
    mixing_grad = jnp.einsum(
        "td,te->de", mixed_rows, branch_grad, preferred_element_type=jnp.float32
    )
    mixed_grad = jnp.einsum(
        "te,de->td", branch_grad, mixing, preferred_element_type=jnp.float32
    ).astype(jnp.bfloat16)
    head_grads = mixed_grad.reshape(count, HEADS, width // HEADS).transpose(1, 0, 2)
    query_grad, key_grad, value_grad = lax.map(
        partial(head_backward, allowed), (heads[0], heads[1], heads[2], head_grads, log_total)
    )
    joint_grad = (
        jnp.stack((query_grad, key_grad, value_grad))
        .transpose(2, 0, 1, 3)
        .reshape(count, 3 * width)
        .astype(jnp.bfloat16)
    )
    projection_grad = jnp.einsum("td,te->de", entry, joint_grad, preferred_element_type=jnp.float32)
    entry_back = jnp.einsum("te,de->td", joint_grad, projection, preferred_element_type=jnp.float32)
    entry_input, gain_grad, shift_grad = norm_back(entry_back, entry_normal, entry_scale, gains)
    token_grad = residual_grad + entry_input
    summed = lax.psum(
        (
            gain_grad,
            shift_grad,
            projection_grad,
            mixing_grad,
            factor_grad,
            bias_grad,
            centroid_grad,
            balance_part,
        ),
        ("expert", "tensor"),
    )
    return (
        layer_output,
        summed[7],
        token_grad,
        summed[0],
        summed[1],
        summed[2],
        summed[3],
        summed[4],
        summed[5],
        summed[6],
        up_share[None],
        down_share[None],
    )


def solution(mesh):
    placed = (
        P(("expert", "tensor"), None),
        P(),
        P(),
        P(),
        P(),
        P(),
        P(),
        P(),
        P("expert", None, "tensor"),
        P("expert", "tensor", None),
        P(("expert", "tensor"), None),
        P(("expert", "tensor"), None),
        P(("expert", "tensor"), None),
    )
    return jax.shard_map(
        per_device,
        mesh=mesh,
        in_specs=placed,
        out_specs=(
            P(("expert", "tensor"), None),
            P(),
            P(("expert", "tensor"), None),
            P(),
            P(),
            P(),
            P(),
            P(),
            P(),
            P(),
            P("expert", None, "tensor"),
            P("expert", "tensor", None),
        ),
        check_vma=False,
    )
```

profile of v0, /device:TPU:0, one launch (start us, length us, event | category | flops | bytes accessed | tf_op | source)
XLA Modules:
  0.0 2327.0 jit_solution(5649885159985938230)
XLA Ops:
  25.1 7.0 convolution_convert_fusion.2
  32.2 8.6 copy.56
  40.7 5.0 slice_bitcast_fusion
  45.8 4.5 copy.59
  50.3 4.5 copy.58
  54.9 4.5 copy.57
  59.4 93.0 %while.28 = (s32[]{:T(128)}, bf16[12,1152,64]{1,2,0:T(8,128)(2,1)}, f32[12,1152]{1,0:T(8,128)}, bf16[12,1152,64]{2,1,0:T(8,128)(2,1)}, bf16[12,1152,64]{2,1,0:T(...) while((s32[]{:T(128)}, bf16[12,1152,64]{1,2,0:T(8,128)(2,1)}, ...), condition=%wide.region_7.8_spmd.clone, body=%wide.region_4.7_spmd.clone.sunk | while | flops 354409344 | bytes 17031272 | solution.py:131
  152.3 4.3 fusion.117
  161.4 4.1 copy.60
  165.5 11.0 scatter_custom_fusion
  180.5 315.5 %all_to_all.20 = bf16[16,576,768]{2,1,0:T(8,128)(2,1)} all-to-all(bf16[16,576,768]{2,1,0:T(8,128)(2,1)S(1)} %bitcast.188), channel_id=1, replica_groups=mesh['expert'=16,'tensor'=2] {'expert'}, dimensions={0} | all-to-all | bytes 28311552 | tf_op jit(solution)/shard_map/all_to_all | solution.py:145
  496.1 44.2 %all-gather.3.cloned.1.call-done = bf16[18432,768]{1,0:T(8,128)(2,1)} async-done(((bf16[9216,768]{1,0:T(8,128)(2,1)}), bf16[18432,768]{1,0:T(8,128)(2,1)}) %all-gather.3.cloned.1.call-update) | async-done | bytes 28311568 | tf_op jit(solution)/shard_map/all_gather | solution.py:148
  540.3 76.4 %fusion.57 = (bf16[18432,384]{1,0:T(8,128)(2,1)}, f32[18432,384]{1,0:T(8,128)}) fusion(bf16[18432,768]{1,0:T(8,128)(2,1)} %all-gather.3.cloned.1.call-done, bf16[1,768,384]{2,1,0:T(8,128)(2,1)} %param.25), kind=kOutput, calls=%fused_computation.71 | convolution fusion | flops 11331698688 | bytes 71368704 | tf_op jit(solution)/shard_map/dot_general | solution.py:40
  616.7 24.3 %convolution_convert_fusion.1 = bf16[18432,768]{1,0:T(8,128)(2,1)} fusion(bf16[18432,384]{1,0:T(8,128)(2,1)} %get-tuple-element.287, bf16[1,384,768]{2,1,0:T(8,128)(2,1)} %param.26), kind=kOutput, calls=%fused_computation.68 | convolution fusion | flops 10885791744 | bytes 43057152 | tf_op jit(solution)/shard_map/dot_general | solution.py:42
  641.0 40.3 %reduce-scatter.3.cloned.1.call-done = bf16[9216,768]{1,0:T(8,128)(2,1)} async-done(((bf16[18432,768]{1,0:T(8,128)(2,1)}), bf16[9216,768]{1,0:T(8,128)(2,1)}) %reduce-scatter.3.cloned.1.call-update) | async-done | bytes 14155792 | tf_op jit(solution)/shard_map/reduce_scatter | solution.py:149
  681.3 6.8 all-to-all-start.1
  688.2 4.3 copy.62
  693.2 261.9 %all-to-all-done.1 = bf16[16,576,768]{2,1,0:T(8,128)(2,1)} async-done(((bf16[16,576,768]{2,1,0:T(8,128)(2,1)}), bf16[16,576,768]{2,1,0:T(8,128)(2,1)}, u32[]{:S(2)}, u32[]{:S(2)}) %all-to-all-start.1) | async-done | bytes 14155808 | tf_op jit(solution)/shard_map/all_to_all | solution.py:155
  955.1 10.7 convert_reduce_fusion.1
  965.8 8.8 gather_fusion
  974.5 5.2 copy.61
  979.7 4.9 fusion.86
  988.5 11.0 scatter_custom_fusion.1
  1003.5 369.4 %all_to_all.21 = bf16[16,576,768]{2,1,0:T(8,128)(2,1)} all-to-all(bf16[16,576,768]{2,1,0:T(8,128)(2,1)S(1)} %bitcast.189), channel_id=1, replica_groups=mesh['expert'=16,'tensor'=2] {'expert'}, dimensions={0} | all-to-all | bytes 28311552 | tf_op jit(solution)/shard_map/all_to_all | solution.py:172
  1373.0 45.2 %all-gather.5.cloned.1.call-done = bf16[18432,768]{1,0:T(8,128)(2,1)} async-done(((bf16[9216,768]{1,0:T(8,128)(2,1)}), bf16[18432,768]{1,0:T(8,128)(2,1)}) %all-gather.5.cloned.1.call-update) | async-done | bytes 28311568 | tf_op jit(solution)/shard_map/all_gather | solution.py:175
  1418.2 30.3 %fusion.63 = bf16[18432,384]{1,0:T(8,128)(2,1)} fusion(f32[18432,384]{1,0:T(8,128)} %get-tuple-element.288, bf16[18432,768]{1,0:T(8,128)(2,1)} %all-gather.5.cloned.1.call-done, bf16[1,384,768]{2,1,0:T(8,128)(2,1)} %param.26), kind=kOutput, calls=%fused_computation.77 | convolution fusion | flops 10942414848 | bytes 71368704 | tf_op jit(solution)/shard_map/rd,fd->rf/dot_general | solution.py:49
  1448.5 24.4 %convolution_convert_fusion = bf16[18432,768]{1,0:T(8,128)(2,1)} fusion(bf16[18432,384]{1,0:T(8,128)(2,1)} %fusion.63, bf16[1,768,384]{2,1,0:T(8,128)(2,1)} %param.25), kind=kOutput, calls=%fused_computation.67 | convolution fusion | flops 10885791744 | bytes 43057152 | tf_op jit(solution)/shard_map/rf,df->rd/dot_general | solution.py:180
  1473.0 40.3 %reduce-scatter.5.cloned.1.call-done = bf16[9216,768]{1,0:T(8,128)(2,1)} async-done(((bf16[18432,768]{1,0:T(8,128)(2,1)}), bf16[9216,768]{1,0:T(8,128)(2,1)}) %reduce-scatter.5.cloned.1.call-update) | async-done | bytes 14155792 | tf_op jit(solution)/shard_map/reduce_scatter | solution.py:179
  1513.3 7.0 all-to-all-start.3
  1520.9 343.0 %psum.63 = f32[4]{0:T(128)} all-reduce(f32[4]{0:T(128)} %convert_reduce_fusion.3), channel_id=1, replica_groups=mesh['expert'=16,'tensor'=2] {'expert','tensor'}, use_global_device_ids=true, to_apply=%region_18.19 | all-reduce | flops 4 | bytes 32 | tf_op jit(solution)/shard_map/psum | solution.py:116
  1867.3 5.0 fusion.87
  1872.3 21.2 convolution_bitcast_fusion.1
  1893.5 10.7 convert_reduce_fusion
  1904.2 8.8 gather_fusion.1
  1913.0 5.2 copy.65
  1918.2 5.8 multiply_reduce_fusion.1
  1934.0 4.5 copy.66
  1938.5 168.2 %while.29 = (s32[]{:T(128)}, bf16[12,1152,64]{1,2,0:T(8,128)(2,1)}, bf16[12,1152,64]{1,2,0:T(8,128)(2,1)}, bf16[12,1152,64]{1,2,0:T(8,128)(2,1)}, bf16[12,1152,6...) while((s32[]{:T(128)}, bf16[12,1152,64]{1,2,0:T(8,128)(2,1)}, ...), condition=%wide.region_30.31_spmd.clone, body=%wide.region_28.30_spmd.clone.sunk | while | flops 865418112 | bytes 42806904 | solution.py:207
  2112.6 7.3 fusion.113
  2119.9 21.5 convolution_bitcast_fusion
  2141.4 9.4 fusion.118
  2150.8 5.2 copy.70
  2156.0 4.3 fusion.83
  2160.3 42.5 %all-reduce = (f32[]{:T(128)}, f32[768]{0:T(1024)}, f32[768]{0:T(1024)}, f32[768]{0:T(1024)}, f32[768]{0:T(1024)}, /*index=5*/f32[4,768]{1,0:T(4,128)}) all-reduce(f32[]{:T(128)S(6)} %div.60, f32[768]{0:T(1024)} %get-tuple-element.221, f32[768]{0:T(1024)} %get-tuple-element.289, ...), channel_id=1, replica_groups=mesh['expert'=16,'tensor'=2] {'expert','tensor'}, use_global_device_ids=true, to_apply=%region_21.22 | all-reduce | flops 6145 | bytes 49160 | tf_op jit(solution)/shard_map/psum | solution.py:220
  2208.1 6.5 fusion.82
  2214.6 5.2 copy.73
  2219.8 92.5 %all-reduce.4.cloned.1.call-done = (f32[768,2304]{1,0:T(8,128)}, f32[768,768]{1,0:T(8,128)}) async-done(((f32[768,2304]{1,0:T(8,128)}, f32[768,768]{1,0:T(8,128)}), (f32[768,2304]{1,0:T(8,128)}, f32[768,768]{1,0:T(8,128)})) %all-reduce.4.cloned.1.call-update) | async-done | bytes 9437200 | tf_op jit(solution)/shard_map/psum | solution.py:220
  2312.3 6.6 copy.106
  (279 shorter events, 322.2 us)
Async XLA Ops:
  7.2 18.0 copy-start
  7.2 533.1 %all-gather.3.cloned.1.call-start = ((), (), s32[]{:S(2)}) async-start(), calls=%async_computation.6 | async-start | bytes 42467328 | tf_op jit(solution)/shard_map/all_gather | solution.py:148
  9.6 147.5 %copy-start.10 = (s32[1152]{0:T(1024)}, s32[1152]{0:T(1024)S(1)}, u32[]{:S(2)}) copy-start(s32[1152]{0:T(1024)S(1)} %reduce.1) | copy-start | bytes 13828
  16.7 8.4 copy-start.27
  16.7 8.4 copy-start.32
  20.6 4.5 copy-start.3
  22.5 2.0 copy-start.14
  24.5 0.6 copy-start.22
  156.6 4.8 copy-start.1
  156.6 0.7 copy-start.24
  156.6 0.8 copy-start.29
  156.6 0.8 copy-start.30
  156.7 4.8 copy-start.12
  157.4 4.0 copy-start.16
  496.0 185.3 %reduce-scatter.3.cloned.1.call-start = ((), (), s32[]{:S(2)}) async-start(), calls=%async_computation.7 | async-start | bytes 42467328 | tf_op jit(solution)/shard_map/reduce_scatter | solution.py:149
  681.3 273.8 %all-to-all-start.1 = ((bf16[16,576,768]{2,1,0:T(8,128)(2,1)}), bf16[16,576,768]{2,1,0:T(8,128)(2,1)}, u32[]{:S(2)}, u32[]{:S(2)}) async-start(bf16[16,576,768]{2,1,0:T(8,128)(2,1)} %bitcast.192), calls=%async_computation.2 | async-start | bytes 28311552 | tf_op jit(solution)/shard_map/all_to_all | solution.py:155
  688.1 4.3 copy-start.26
  688.2 730.0 %all-gather.5.cloned.1.call-start = ((), (), s32[]{:S(2)}) async-start(), calls=%async_computation.8 | async-start | bytes 42467328 | tf_op jit(solution)/shard_map/all_gather | solution.py:175
  692.5 273.3 %copy-start.20 = (s32[2048]{0:T(1024)}, s32[2048]{0:T(1024)S(1)}, u32[]{:S(2)}) copy-start(s32[2048]{0:T(1024)S(1)} %pad_clamp_fusion) | copy-start | bytes 24580
  693.2 286.5 %copy-start.18 = (f32[1152]{0:T(1024)}, f32[1152]{0:T(1024)S(1)}, u32[]{:S(2)}) copy-start(f32[1152]{0:T(1024)S(1)} %add_divide_fusion) | copy-start | bytes 13828
  1372.9 140.4 %reduce-scatter.5.cloned.1.call-start = ((), (), s32[]{:S(2)}) async-start(), calls=%async_computation.9 | async-start | bytes 42467328 | tf_op jit(solution)/shard_map/reduce_scatter | solution.py:179
  1513.3 7.0 copy-start.11
  1513.3 354.0 %copy-start.13 = (f32[1152]{0:T(1024)S(1)}, f32[1152]{0:T(1024)}, u32[]{:S(2)}) copy-start(f32[1152]{0:T(1024)} %copy-done.12) | copy-start | bytes 13828
  1513.3 380.2 %all-to-all-start.3 = ((bf16[16,576,768]{2,1,0:T(8,128)(2,1)}), bf16[16,576,768]{2,1,0:T(8,128)(2,1)}, u32[]{:S(2)}, u32[]{:S(2)}) async-start(bf16[16,576,768]{2,1,0:T(8,128)(2,1)} %bitcast.191), calls=%async_computation.5 | async-start | bytes 28311552 | tf_op jit(solution)/shard_map/all_to_all | solution.py:187
  1520.2 792.0 %all-reduce.4.cloned.1.call-start = ((), (), s32[]{:S(2)}) async-start(), calls=%async_computation.10 | async-start | bytes 18874368 | tf_op jit(solution)/shard_map/psum | solution.py:220
  1893.5 10.7 copy-start.21
  1913.0 5.2 copy-start.17
  1918.1 5.8 copy-start.2
  1918.1 6.2 copy-start.5
  1918.1 6.7 copy-start.6
  1918.1 6.7 copy-start.19
  1918.1 6.7 copy-start.25
  1924.8 3.1 copy-start.34
  1927.9 3.2 copy-start.7
  1927.9 3.2 copy-start.31
  2106.7 5.9 copy-start.4
  2106.7 5.9 copy-start.15
  2106.7 5.9 copy-start.23
  2106.7 5.9 copy-start.28
  2106.7 5.9 copy-start.33
  2110.3 2.3 copy-start.8
  2312.3 6.6 copy-start.9
Sparse Core Ops, SparseCore 0:
  496.2 44.0 all-gather.2
  641.1 40.1 reduce-scatter.2
  1373.0 45.1 all-gather.4
  1473.1 40.1 reduce-scatter.4
  2120.0 192.2 all-reduce.3
where the time goes:
time: 2350 us; the launch traced here: 2330 us
  blocking collectives  1070 us (46%)
  waiting for transfers between devices  525 us (22%)
  matrix products  458 us (19%)
  local copies, waits for them, and re-layouts  159 us (7%)
  other arithmetic  85.3 us (4%)
    all_to_all x1, blocking collectives, per_device(): lax.all_to_all(grad_copies, 'expert', split_axis=0, concat_axis=0, tiled=...  369 us
    psum x1, blocking collectives, per_device(): loads = lax.psum(jnp.sum(picks_float, axis=0), ('expert', 'tensor'))  343 us
    all_to_all x1, blocking collectives, per_device(): lax.all_to_all(copies, 'expert', split_axis=0, concat_axis=0, tiled=True)  315 us
    all_to_all x1, waiting for transfers between devices, per_device(): lax.all_to_all(produced.reshape(arrived.shape), 'expert', split_axis=0, c...  262 us
    psum x1, waiting for transfers between devices, per_device(): lax.psum((gain_grad, shift_grad, projection_grad, mixing_grad, factor_gra...  92.5 us
    dot_general x1, matrix products, expert_forward(): before = jnp.dot(gathered, upward, preferred_element_type=jnp.float32)  76.4 us
  transfers between devices with their start and end apart: 7, of which 6 were waited for; matrix products, arithmetic and copies ran while one was open for 4% of the time, Pallas kernels for 0%

commit v1 on v0

--- a/solution.py
+++ b/solution.py
@@ -3,6 +3,8 @@
 import jax
 import jax.numpy as jnp
 from jax import lax
+from jax.experimental import pallas as pl
+from jax.experimental.pallas import tpu as pltpu
 from jax.sharding import PartitionSpec as P
 
 HEADS = 12
@@ -10,6 +12,19 @@
 
 highest = lax.Precision.HIGHEST
 epsilon = 1e-05
+
+
+def running(values):
+    places = jnp.arange(values.shape[0])
+    return jnp.sum(jnp.where(places[:, None] >= places[None, :], values[None, :], 0), axis=1)
+
+
+def earlier(picks):
+    places = jnp.arange(picks.shape[0])
+    before = (places[:, None] > places[None, :]).astype(jnp.bfloat16)
+    return jnp.dot(
+        before, picks.astype(jnp.bfloat16), preferred_element_type=jnp.float32
+    ).astype(jnp.int32)
 
 
 def norm_parts(values, gain, shift):
@@ -87,7 +102,7 @@
     return (query_grad, key_grad, value_grad)
 
 
-def per_device(
+def moving_tokens(
     tokens,
     gains,
     shifts,
@@ -116,11 +131,11 @@
     loads = lax.psum(jnp.sum(picks_float, axis=0), ("expert", "tensor"))
     spread = (loads - average) / average
     token_spread = jnp.sum(jnp.where(picks, spread[None, :], 0.0), axis=1)
-    ranks = jnp.sum((jnp.cumsum(picks_int, axis=0) - picks_int) * picks_int, axis=1)
+    ranks = jnp.sum(earlier(picks) * picks_int, axis=1)
     slots = route * capacity + ranks
     places = jnp.arange(count, dtype=jnp.int32)
     documents = jnp.sum(
-        (places[:, None] >= jnp.cumsum(lengths[0])[None, :]).astype(jnp.int32), axis=1
+        (places[:, None] >= running(lengths[0])[None, :]).astype(jnp.int32), axis=1
     )
     allowed = (places[:, None] >= places[None, :]) & (documents[:, None] == documents[None, :])
     inputs = tokens.astype(jnp.float32)
@@ -246,6 +261,664 @@
     )
 
 
+HALF_LOG = 1.4426950408889634
+LN2 = 0.6931471805599453
+NT = (((1,), (1,)), ((), ()))
+TN = (((0,), (0,)), ((), ()))
+VMEM_LIMIT = 60 * 1024 * 1024
+
+
+def query_blocks(count):
+    step = 256 if count > 256 else count
+    return [(i, min(i + step, count)) for i in range(0, count, step)]
+
+
+def document_starts(lengths_ref, places):
+    starts = jnp.zeros_like(places)
+    end = 0
+    for d in range(lengths_ref.shape[0]):
+        end = end + lengths_ref[d]
+        starts = jnp.where(places >= end, end, starts)
+    return starts
+
+
+def attend_forward(joint, lengths):
+    count, width = joint.shape[0], joint.shape[1] // 3
+    pairs = width // 128
+    factor = (width // HEADS) ** (-0.5) * HALF_LOG
+
+    def kernel(lengths_ref, q_ref, k_ref, v_ref, o_ref, l_ref, bias_ref):
+        @pl.when(pl.program_id(0) == 0)
+        def _():
+            rows = lax.broadcasted_iota(jnp.int32, (count, 1), 0)
+            starts = document_starts(lengths_ref, rows)
+            for s, e in query_blocks(count):
+                column = lax.broadcasted_iota(jnp.int32, (count, e - s), 1) + s
+                seen = (column <= rows) & (column >= starts)
+                bias_ref[:, s:e] = jnp.where(seen, 0.0, -1e9)
+
+        first = lax.broadcasted_iota(jnp.int32, (1, 128), 1) < 64
+        for s, e in query_blocks(count):
+            outs, logs = [], []
+            for half in range(2):
+                q = jnp.where(first == (half == 0), q_ref[s:e, :], jnp.bfloat16(0))
+                scores = lax.dot_general(
+                    q, k_ref[0:e, :], NT, preferred_element_type=jnp.float32
+                )
+                scores = scores * factor + bias_ref[s:e, 0:e]
+                peak = jnp.max(scores, axis=1, keepdims=True)
+                weights = jnp.exp2(scores - peak)
+                total = jnp.sum(weights, axis=1, keepdims=True)
+                mixed = jnp.dot(
+                    weights.astype(jnp.bfloat16),
+                    v_ref[0:e, :],
+                    preferred_element_type=jnp.float32,
+                )
+                outs.append(mixed / total)
+                logs.append(peak + jnp.log2(total))
+            o_ref[s:e, :] = jnp.where(first, outs[0], outs[1]).astype(jnp.bfloat16)
+            spread = jnp.transpose(jnp.where(first, logs[0], logs[1]))
+            l_ref[0, 0:1, s:e] = spread[0:1, :]
+            l_ref[0, 1:2, s:e] = spread[64:65, :]
+
+    return pl.pallas_call(
+        kernel,
+        out_shape=(
+            jax.ShapeDtypeStruct((count, width), jnp.bfloat16),
+            jax.ShapeDtypeStruct((pairs, 2, count), jnp.float32),
+        ),
+        grid_spec=pltpu.PrefetchScalarGridSpec(
+            num_scalar_prefetch=1,
+            grid=(pairs,),
+            in_specs=[
+                pl.BlockSpec((count, 128), lambda p, _: (0, p)),
+                pl.BlockSpec((count, 128), lambda p, _: (0, pairs + p)),
+                pl.BlockSpec((count, 128), lambda p, _: (0, 2 * pairs + p)),
+            ],
+            out_specs=(
+                pl.BlockSpec((count, 128), lambda p, _: (0, p)),
+                pl.BlockSpec((1, 2, count), lambda p, _: (p, 0, 0)),
+            ),
+            scratch_shapes=[pltpu.VMEM((count, count), jnp.float32)],
+        ),
+        compiler_params=pltpu.CompilerParams(vmem_limit_bytes=VMEM_LIMIT),
+        cost_estimate=pl.CostEstimate(
+            flops=4 * count * count * width, bytes_accessed=8 * count * width, transcendentals=count * count * HEADS
+        ),
+    )(lengths, joint, joint, joint)
+
+
+def attend_backward(joint, mixed, upstream, logs, lengths):
+    count, width = joint.shape[0], joint.shape[1] // 3
+    pairs = width // 128
+    scale = (width // HEADS) ** (-0.5)
+    factor = scale * HALF_LOG
+
+    def kernel(
+        lengths_ref, q_ref, k_ref, v_ref, o_ref, u_ref, l_ref, dq_ref, dk_ref, dv_ref, bias_ref, ka_ref, va_ref
+    ):
+        @pl.when(pl.program_id(0) == 0)
+        def _():
+            places = lax.broadcasted_iota(jnp.int32, (1, count), 1)
+            starts = document_starts(lengths_ref, places)
+            for s, e in query_blocks(count):
+                row = lax.broadcasted_iota(jnp.int32, (e - s, count), 0) + s
+                seen = (row <= places) & (row >= starts)
+                bias_ref[s:e, :] = jnp.where(seen, 0.0, -1e9)
+
+        first = lax.broadcasted_iota(jnp.int32, (1, 128), 1) < 64
+        ka_ref[...] = jnp.zeros_like(ka_ref)
+        va_ref[...] = jnp.zeros_like(va_ref)
+        for s, e in query_blocks(count):
+            both = jnp.transpose(
+                u_ref[s:e, :].astype(jnp.float32) * o_ref[s:e, :].astype(jnp.float32)
+            )
+            found = []
+            for half in range(2):
+                mine = first == (half == 0)
+                inner = jnp.sum(both[64 * half : 64 * half + 64, :], axis=0, keepdims=True)
+                q = jnp.where(mine, q_ref[s:e, :], jnp.bfloat16(0))
+                u = jnp.where(mine, u_ref[s:e, :], jnp.bfloat16(0))
+                scores = lax.dot_general(
+                    k_ref[0:e, :], q, NT, preferred_element_type=jnp.float32
+                )
+                probs = jnp.exp2(
+                    scores * factor + bias_ref[0:e, s:e] - l_ref[0, half : half + 1, s:e]
+                )
+                prob_grad = lax.dot_general(
+                    v_ref[0:e, :], u, NT, preferred_element_type=jnp.float32
+                )
+                score_grad = (probs * (prob_grad - inner)).astype(jnp.bfloat16)
+                va_ref[0:e, :] += jnp.dot(
+                    probs.astype(jnp.bfloat16), u, preferred_element_type=jnp.float32
+                )
+                ka_ref[0:e, :] += jnp.dot(score_grad, q, preferred_element_type=jnp.float32)
+                found.append(
+                    lax.dot_general(
+                        score_grad, k_ref[0:e, :], TN, preferred_element_type=jnp.float32
+                    )
+                )
+            dq_ref[s:e, :] = (jnp.where(first, found[0], found[1]) * scale).astype(jnp.bfloat16)
+        dk_ref[...] = (ka_ref[...] * scale).astype(jnp.bfloat16)
+        dv_ref[...] = va_ref[...].astype(jnp.bfloat16)
+
+    column = lambda shift: pl.BlockSpec((count, 128), lambda p, _: (0, shift + p))
+    return pl.pallas_call(
+        kernel,
+        out_shape=(jax.ShapeDtypeStruct((count, width), jnp.bfloat16),) * 3,
+        grid_spec=pltpu.PrefetchScalarGridSpec(
+            num_scalar_prefetch=1,
+            grid=(pairs,),
+            in_specs=[
+                column(0),
+                column(pairs),
+                column(2 * pairs),
+                column(0),
+                column(0),
+                pl.BlockSpec((1, 2, count), lambda p, _: (p, 0, 0)),
+            ],
+            out_specs=(column(0),) * 3,
+            scratch_shapes=[
+                pltpu.VMEM((count, count), jnp.float32),
+                pltpu.VMEM((count, 128), jnp.float32),
+                pltpu.VMEM((count, 128), jnp.float32),
+            ],
+        ),
+        compiler_params=pltpu.CompilerParams(vmem_limit_bytes=VMEM_LIMIT),
+        cost_estimate=pl.CostEstimate(
+            flops=10 * count * count * width, bytes_accessed=16 * count * width, transcendentals=count * count * HEADS
+        ),
+    )(lengths, joint, joint, joint, mixed, upstream, logs)
+
+
+TILE = 256
+ALIGN = 16
+
+
+def aligned_rows(count, experts):
+    return -(-(count + experts * (ALIGN - 1)) // ALIGN) * ALIGN
+
+
+def gelu_pair(values):
+    bell = jnp.exp2(values * values * (-0.5 * HALF_LOG))
+    near = 1.0 / (1.0 + (0.3275911 * 0.7071067811865476) * jnp.abs(values))
+    series = 1.061405429 * 0.5 * near - 1.453152027 * 0.5
+    series = series * near + 1.421413741 * 0.5
+    series = series * near - 0.284496736 * 0.5
+    series = series * near + 0.254829592 * 0.5
+    tail = series * near * bell
+    below = jnp.where(values >= 0.0, 1.0 - tail, tail)
+    return values * below, below + values * bell * 0.3989422804014327
+
+
+def expert_kernel_body(
+    experts,
+    sources,
+    rows,
+    limit,
+    width,
+    hidden,
+    meta_ref,
+    *refs,
+):
+    sent_refs, refs = refs[:sources], refs[sources:]
+    cot_refs, refs = refs[:sources], refs[sources:]
+    gate_refs, refs = refs[:sources], refs[sources:]
+    near_refs, refs = refs[: 2 * experts - 1], refs[2 * experts - 1 :]
+    far_refs, refs = refs[: 2 * experts - 1], refs[2 * experts - 1 :]
+    back_outs, refs = refs[:sources], refs[sources:]
+    made_outs, refs = refs[:sources], refs[sources:]
+    dot_outs, refs = refs[:sources], refs[sources:]
+    near_out, far_out = refs[:2]
+    (x_ref, c_ref, g_ref, column_ref, up_ref, down_ref, gu_ref, gd_ref, pack_ref, zero_ref) = refs[2:12]
+    weight_sem, row_sem, out_sem, grad_sem, zero_sem = refs[12:]
+    half = hidden // 2
+    own = meta_ref[0]
+
+    def size_of(s, e):
+        return meta_ref[1 + s * experts + e]
+
+    source_at, joined_at, tiles = {}, {}, []
+    first = []
+    base = 0
+    for s in range(sources):
+        at = 0
+        for e in range(experts):
+            source_at[s, e] = at
+            at = at + size_of(s, e)
+        source_at[s, experts] = at
+    for e in range(experts):
+        first.append(base)
+        at = base
+        for s in range(sources):
+            joined_at[s, e] = at
+            at = at + size_of(s, e)
+        number = (at - base + (TILE - 1)) // TILE
+        tiles.append(number)
+        base = base + number * TILE
+
+    bits = [1 << b for b in range(limit.bit_length()) if ALIGN <= (1 << b)]
+
+    def pieces(s, e):
+        size = size_of(s, e)
+        for i, piece in enumerate(bits):
+            yield i, piece, (size & piece) != 0, size & (piece - 1)
+
+    def move_in(s, e, act):
+        for i, piece, taken, offset in pieces(s, e):
+            @pl.when(taken)
+            def _(i=i, piece=piece, offset=offset):
+                src = pl.ds(pl.multiple_of(source_at[s, e] + offset, ALIGN), piece)
+                dst = pl.ds(pl.multiple_of(joined_at[s, e] + offset, ALIGN), piece)
+                k = s * experts + e
+                act(pltpu.make_async_copy(sent_refs[s].at[src], x_ref.at[dst], row_sem.at[0, k, i]))
+                act(pltpu.make_async_copy(cot_refs[s].at[src], c_ref.at[dst], row_sem.at[1, k, i]))
+
+    def move_out(s, e, act):
+        for i, piece, taken, offset in pieces(s, e):
+            @pl.when(taken)
+            def _(i=i, piece=piece, offset=offset):
+                src = pl.ds(pl.multiple_of(source_at[s, e] + offset, ALIGN), piece)
+                dst = pl.ds(pl.multiple_of(joined_at[s, e] + offset, ALIGN), piece)
+                k = s * experts + e
+                act(pltpu.make_async_copy(x_ref.at[dst], made_outs[s].at[src], out_sem.at[0, k, i]))
+                act(pltpu.make_async_copy(c_ref.at[dst], back_outs[s].at[src], out_sem.at[1, k, i]))
+
+    def move_weights(e, act):
+        step = e - own
+        for k in range(2 * experts - 1):
+            @pl.when(step == k - (experts - 1))
+            def _(k=k):
+                for j, ref in enumerate((near_refs[k], far_refs[k])):
+                    lanes = pl.ds(j * half, half)
+                    act(pltpu.make_async_copy(ref.at[pl.ds(0, width)], up_ref.at[e, :, lanes], weight_sem.at[e, j, 0]))
+                    for part in range(2):
+                        act(
+                            pltpu.make_async_copy(
+                                ref.at[pl.ds(width + part * half, half)],
+                                down_ref.at[e, lanes, pl.ds(part * half, half)],
+                                weight_sem.at[e, j, 1 + part],
+                            )
+                        )
+
+    zero_ref[...] = jnp.zeros_like(zero_ref)
+    for e in range(experts):
+        @pl.when(tiles[e] > 0)
+        def _(e=e):
+            last = pl.ds(pl.multiple_of(first[e] + (tiles[e] - 1) * TILE, TILE), TILE)
+            x_ref[last, :] = jnp.zeros((TILE, width), jnp.bfloat16)
+            c_ref[last, :] = jnp.zeros((TILE, width), jnp.bfloat16)
+            g_ref[last, :] = jnp.zeros((TILE, 128), jnp.float32)
+
+    for e in range(experts):
+        move_weights(e, lambda copy: copy.start())
+        for s in range(sources):
+            move_in(s, e, lambda copy: copy.start())
+
+    tail_chunks = rows // ALIGN
+
+    def tail(s, act):
+        def one(i, _):
+            @pl.when(i * ALIGN >= source_at[s, experts])
+            def _():
+                dst = pl.ds(pl.multiple_of(i * ALIGN, ALIGN), ALIGN)
+                act(pltpu.make_async_copy(zero_ref, made_outs[s].at[dst], zero_sem.at[0, s, i]))
+                act(pltpu.make_async_copy(zero_ref, back_outs[s].at[dst], zero_sem.at[1, s, i]))
+            return 0
+        lax.fori_loop(tail_chunks - 5, tail_chunks, one, 0)
+
+    for s in range(sources):
+        tail(s, lambda copy: copy.start())
+
+    for s in range(sources):
+        column_ref[...] = jnp.broadcast_to(
+            jnp.transpose(jnp.broadcast_to(gate_refs[s][0:1, :], (128, rows)))[:, 0:128], (rows, 128)
+        )
+        for e in range(experts):
+            def one(i, _, s=s, e=e):
+                src = pl.ds(pl.multiple_of(source_at[s, e] + i * ALIGN, ALIGN), ALIGN)
+                dst = pl.ds(pl.multiple_of(joined_at[s, e] + i * ALIGN, ALIGN), ALIGN)
+                g_ref[dst, :] = column_ref[src, :]
+                return 0
+            lax.fori_loop(0, size_of(s, e) // ALIGN, one, 0)
+
+    for e in range(experts):
+        move_weights(e, lambda copy: copy.wait())
+        for s in range(sources):
+            move_in(s, e, lambda copy: copy.wait())
+        gu_ref[...] = jnp.zeros_like(gu_ref)
+        gd_ref[...] = jnp.zeros_like(gd_ref)
+
+        def tile(t, _, e=e):
+            at = pl.ds(pl.multiple_of(first[e] + t * TILE, TILE), TILE)
+            x, c, gate = x_ref[at, :], c_ref[at, :], g_ref[at, 0:1]
+            before = jnp.dot(x, up_ref[e], preferred_element_type=jnp.float32)
+            active, slope = gelu_pair(before)
+            through = lax.dot_general(c, down_ref[e], NT, preferred_element_type=jnp.float32)
+            grad = (through * (slope * gate)).astype(jnp.bfloat16)
+            gated = (active * gate).astype(jnp.bfloat16)
+            made = jnp.dot(active.astype(jnp.bfloat16), down_ref[e], preferred_element_type=jnp.float32)
+            g_ref[at, :] = jnp.broadcast_to(
+                jnp.sum(made * c.astype(jnp.float32), axis=1, keepdims=True), (TILE, 128)
+            )
+            gd_ref[...] += lax.dot_general(gated, c, TN, preferred_element_type=jnp.float32)
+            gu_ref[...] += lax.dot_general(x, grad, TN, preferred_element_type=jnp.float32)
+            back = lax.dot_general(grad, up_ref[e], NT, preferred_element_type=jnp.float32)
+            x_ref[at, :] = made.astype(jnp.bfloat16)
+            c_ref[at, :] = back.astype(jnp.bfloat16)
+            return 0
+
+        lax.fori_loop(0, tiles[e], tile, 0)
+        for s in range(sources):
+            move_out(s, e, lambda copy: copy.start())
+
+        slot = e % 2
+        grads = lambda e, slot: [
+            pltpu.make_async_copy(pack_ref.at[slot, j], ref.at[e - own + experts - 1], grad_sem.at[slot, j])
+            for j, ref in enumerate((near_out, far_out))
+        ]
+        if e >= 2:
+            for copy in grads(e - 2, slot):
+                copy.wait()
+        for j in range(2):
+            pack_ref[slot, j, 0:width, :] = gu_ref[:, j * half : (j + 1) * half].astype(jnp.bfloat16)
+            for part in range(2):
+                pack_ref[slot, j, width + part * half : width + (part + 1) * half, :] = gd_ref[
+                    j * half : (j + 1) * half, part * half : (part + 1) * half
+                ].astype(jnp.bfloat16)
+        for copy in grads(e, slot):
+            copy.start()
+
+    for s in range(sources):
+        for e in range(experts):
+            def one(i, _, s=s, e=e):
+                src = pl.ds(pl.multiple_of(source_at[s, e] + i * ALIGN, ALIGN), ALIGN)
+                dst = pl.ds(pl.multiple_of(joined_at[s, e] + i * ALIGN, ALIGN), ALIGN)
+                column_ref[src, :] = g_ref[dst, :]
+                return 0
+            lax.fori_loop(0, size_of(s, e) // ALIGN, one, 0)
+        dot_outs[s][...] = jnp.transpose(column_ref[...])[0:8, :]
+
+    for e in range(experts):
+        for s in range(sources):
+            move_out(s, e, lambda copy: copy.wait())
+    for s in range(sources):
+        tail(s, lambda copy: copy.wait())
+    for e in range(max(0, experts - 2), experts):
+        for copy in grads(e, e % 2):
+            copy.wait()
+
+
+def expert_stage(meta, sent, cot, gates, near, far, experts, limit):
+    sources = len(sent)
+    rows, width = sent[0].shape
+    half = near[0].shape[1]
+    hidden = 2 * half
+    joined = -(-(sources * rows + experts * (TILE - 1)) // TILE) * TILE
+    limit = -(-limit // ALIGN) * ALIGN
+    pieces = limit.bit_length() - ALIGN.bit_length() + 1
+    anywhere = pl.BlockSpec(memory_space=pl.ANY)
+    local = pl.BlockSpec(memory_space=pltpu.VMEM)
+    slots = 2 * experts - 1
+    dma = pltpu.SemaphoreType.DMA
+    outs = pl.pallas_call(
+        partial(expert_kernel_body, experts, sources, rows, limit, width, hidden),
+        out_shape=(
+            [jax.ShapeDtypeStruct((rows, width), jnp.bfloat16)] * (2 * sources)
+            + [jax.ShapeDtypeStruct((8, rows), jnp.float32)] * sources
+            + [jax.ShapeDtypeStruct((slots,) + near[0].shape, jnp.bfloat16)] * 2
+        ),
+        in_specs=[pl.BlockSpec(memory_space=pltpu.SMEM)]
+        + [anywhere] * (2 * sources)
+        + [local] * sources
+        + [anywhere] * (2 * slots),
+        out_specs=[anywhere] * (2 * sources) + [local] * sources + [anywhere] * 2,
+        scratch_shapes=[
+            pltpu.VMEM((joined, width), jnp.bfloat16),
+            pltpu.VMEM((joined, width), jnp.bfloat16),
+            pltpu.VMEM((joined, 128), jnp.float32),
+            pltpu.VMEM((rows, 128), jnp.float32),
+            pltpu.VMEM((experts, width, hidden), jnp.bfloat16),
+            pltpu.VMEM((experts, hidden, width), jnp.bfloat16),
+            pltpu.VMEM((width, hidden), jnp.float32),
+            pltpu.VMEM((hidden, width), jnp.float32),
+            pltpu.VMEM((2, 2) + near[0].shape, jnp.bfloat16),
+            pltpu.VMEM((ALIGN, width), jnp.bfloat16),
+            dma((experts, 2, 3)),
+            dma((2, sources * experts, pieces)),
+            dma((2, sources * experts, pieces)),
+            dma((2, 2)),
+            dma((2, sources, rows // ALIGN)),
+        ],
+        compiler_params=pltpu.CompilerParams(vmem_limit_bytes=VMEM_LIMIT),
+        cost_estimate=pl.CostEstimate(
+            flops=12 * sources * rows * width * hidden, bytes_accessed=100_000_000, transcendentals=sources * rows * hidden
+        ),
+    )(meta, *sent, *cot, *gates, *near, *far)
+    back, made, dots = outs[:sources], outs[sources : 2 * sources], outs[2 * sources : 3 * sources]
+    return back, made, dots, outs[-2], outs[-1]
+
+
+def swap(value, bit):
+    groups = lax.axis_size("expert")
+    return lax.ppermute(value, "expert", [(i, i ^ bit) for i in range(groups)])
+
+
+def across(value):
+    return lax.ppermute(value, "tensor", [(0, 1), (1, 0)])
+
+
+def spread_out(value):
+    other = swap(value, 2)
+    return [value, across(value), other, across(other)]
+
+
+def line(value, step, planes, slabs, least):
+    pairs = []
+    for i in range(planes * slabs):
+        plane = i // slabs
+        source = plane if step > 0 else planes - 1 - plane
+        if source >= least and 0 <= plane + step < planes:
+            pairs.append((i, i + step * slabs))
+    return lax.ppermute(value, "expert", pairs)
+
+
+def beside(value, planes, slabs, shift):
+    pairs = [
+        (i, i ^ 1) for i in range(planes * slabs) if 0 <= i // slabs + shift < planes
+    ]
+    return lax.ppermute(value, "expert", pairs)
+
+
+def gather_weights(packed, planes, slabs):
+    near = [None] * (2 * planes - 1)
+    near[planes - 1] = packed
+    for k in range(1, planes):
+        near[planes - 1 - k] = line(near[planes - k], 1, planes, slabs, k - 1)
+        near[planes - 1 + k] = line(near[planes - 2 + k], -1, planes, slabs, k - 1)
+    far = [None] * (2 * planes - 1)
+    for k in range(planes):
+        for sign in (1, -1):
+            if k or sign > 0:
+                at = planes - 1 + sign * k
+                far[at] = beside(near[at], planes, slabs, sign * k)
+    return near, far
+
+
+def reduce_weights(near, far, planes, slabs):
+    sums = {}
+    for k in range(planes - 1, -1, -1):
+        for sign in (1, -1):
+            if k or sign > 0:
+                at = planes - 1 + sign * k
+                came = beside(far[at], planes, slabs, sign * k)
+                sums[sign * k] = near[at].astype(jnp.float32) + came.astype(jnp.float32)
+    arrived = []
+    for sign in (1, -1):
+        came = None
+        for k in range(planes - 1, 0, -1):
+            total = sums[sign * k]
+            if came is not None:
+                total = total + came.astype(jnp.float32)
+            pairs = [
+                (i, i + sign * slabs)
+                for i in range(planes * slabs)
+                if 0 <= i // slabs + sign * k < planes
+            ]
+            came = lax.ppermute(total.astype(jnp.bfloat16), "expert", pairs)
+        arrived.append(came.astype(jnp.float32))
+    return sums[0] + arrived[0] + arrived[1]
+
+
+def per_device(
+    tokens,
+    gains,
+    shifts,
+    projection,
+    mixing,
+    factors,
+    biases,
+    centroids,
+    expanding,
+    contracting,
+    routes,
+    lengths,
+    cotangent,
+):
+    count, width = tokens.shape
+    experts = centroids.shape[0]
+    groups = lax.axis_size("expert")
+    slabs = groups // experts
+    half = expanding.shape[2]
+    limit = 2 * count // experts
+    total_tokens = count * groups * lax.axis_size("tensor")
+    average = total_tokens / experts
+    rows = aligned_rows(count, experts)
+    me, core = lax.axis_index("expert"), lax.axis_index("tensor")
+
+    packed = jnp.concatenate(
+        (expanding[0], contracting[0, :, :half], contracting[0, :, half:]), axis=0
+    )
+    near, far = gather_weights(packed, experts, slabs)
+
+    route = routes[:, 0]
+    picks = route[:, None] == jnp.arange(experts, dtype=jnp.int32)[None, :]
+    picks_int = picks.astype(jnp.int32)
+    counts = jnp.sum(picks_int, axis=0)
+    all_counts = lax.all_gather(counts, ("expert", "tensor"))
+    loads = jnp.sum(all_counts, axis=0).astype(jnp.float32)
+    spread = (loads - average) / average
+    token_spread = jnp.sum(jnp.where(picks, spread[None, :], 0.0), axis=1)
+    sizes = (all_counts + (ALIGN - 1)) // ALIGN * ALIGN
+    mine = sizes[me * 2 + core]
+    starts = running(mine) - mine
+    ranks = earlier(picks)
+    position = jnp.sum((ranks + starts[None, :]) * picks_int, axis=1)
+    order = (jnp.arange(rows, dtype=jnp.int32)[:, None] == position[None, :]).astype(jnp.bfloat16)
+    back_order = (position[:, None] == jnp.arange(rows, dtype=jnp.int32)[None, :]).astype(jnp.bfloat16)
+    group = [me * 2 + core, me * 2 + 1 - core, (me ^ 2) * 2 + core, (me ^ 2) * 2 + 1 - core]
+    meta = jnp.concatenate(
+        [(me // slabs).astype(jnp.int32)[None]] + [sizes[g] for g in group]
+    )
+    sorted_cot = jnp.dot(order, cotangent, preferred_element_type=jnp.float32).astype(jnp.bfloat16)
+    group_cot = spread_out(sorted_cot)
+
+    inputs = tokens.astype(jnp.float32)
+    entry, entry_normal, entry_scale = norm_parts(inputs, gains, shifts)
+    entry = entry.astype(jnp.bfloat16)
+    joint = jnp.dot(entry, projection, preferred_element_type=jnp.float32).astype(jnp.bfloat16)
+    mixed_rows, logs = attend_forward(joint, lengths[0])
+    residual = inputs + jnp.dot(mixed_rows, mixing, preferred_element_type=jnp.float32)
+    normed, mixer_normal, mixer_scale = norm_parts(residual, factors, biases)
+    chosen = jnp.dot(picks.astype(jnp.bfloat16), centroids, preferred_element_type=jnp.float32)
+    gates = jax.nn.sigmoid(jnp.sum(normed * chosen, axis=1))
+    sorted_sent = jnp.dot(
+        order, normed.astype(jnp.bfloat16), preferred_element_type=jnp.float32
+    ).astype(jnp.bfloat16)
+    sorted_gates = jnp.sum(
+        jnp.where(position[:, None] == jnp.arange(rows, dtype=jnp.int32)[None, :], gates[:, None], 0.0),
+        axis=0,
+    )
+    group_gates = spread_out(jnp.broadcast_to(sorted_gates[None, :], (8, rows)))
+    group_sent = spread_out(sorted_sent)
+    back, made, dots, near_grads, far_grads = expert_stage(
+        meta, group_sent, group_cot, group_gates, near, far, experts, limit
+    )
+
+    def collect(parts, narrow):
+        own = parts[0].astype(jnp.float32) + across(parts[1]).astype(jnp.float32)
+        other = parts[2].astype(jnp.float32) + across(parts[3]).astype(jnp.float32)
+        return own, swap(other.astype(narrow), 2)
+
+    def unsort(own, came):
+        high = own.astype(jnp.bfloat16)
+        return jnp.dot(
+            back_order, high, preferred_element_type=jnp.float32
+        ) + jnp.dot(back_order, came, preferred_element_type=jnp.float32)
+
+    dot_own, dot_came = collect(dots, jnp.float32)
+    gate_rows = (dot_own + dot_came)[0]
+    gate_grad = jnp.sum(
+        jnp.where(position[:, None] == jnp.arange(rows, dtype=jnp.int32)[None, :], gate_rows[None, :], 0.0),
+        axis=1,
+    )
+    sent_grad = unsort(*collect(back, jnp.bfloat16))
+    made_own, made_came = collect(made, jnp.bfloat16)
+    up_down = reduce_weights(near_grads, far_grads, experts, slabs)
+
+    upstream = cotangent.astype(jnp.float32)
+    balance_part = jnp.sum(token_spread * gates) / total_tokens
+    logit_grad = (gate_grad + token_spread / total_tokens) * gates * (1.0 - gates)
+    normed_grad = sent_grad + logit_grad[:, None] * chosen
+    centroid_grad = jnp.einsum(
+        "te,td->ed", picks.astype(jnp.float32), logit_grad[:, None] * normed, precision=highest
+    )
+    mixer_back, factor_grad, bias_grad = norm_back(normed_grad, mixer_normal, mixer_scale, factors)
+    residual_grad = upstream + mixer_back
+    branch_grad = residual_grad.astype(jnp.bfloat16)
+    mixing_grad = jnp.einsum(
+        "td,te->de", mixed_rows, branch_grad, preferred_element_type=jnp.float32
+    )
+    mixed_grad = jnp.einsum(
+        "te,de->td", branch_grad, mixing, preferred_element_type=jnp.float32
+    ).astype(jnp.bfloat16)
+    joint_grad = jnp.concatenate(
+        attend_backward(joint, mixed_rows, mixed_grad, logs, lengths[0]), axis=1
+    )
+    projection_grad = jnp.einsum("td,te->de", entry, joint_grad, preferred_element_type=jnp.float32)
+    entry_back = jnp.einsum("te,de->td", joint_grad, projection, preferred_element_type=jnp.float32)
+    entry_input, gain_grad, shift_grad = norm_back(entry_back, entry_normal, entry_scale, gains)
+    token_grad = residual_grad + entry_input
+    layer_output = (residual + gates[:, None] * unsort(made_own, made_came)).astype(jnp.bfloat16)
+    summed = lax.psum(
+        (
+            gain_grad,
+            shift_grad,
+            projection_grad,
+            mixing_grad,
+            factor_grad,
+            bias_grad,
+            centroid_grad,
+            balance_part,
+        ),
+        ("expert", "tensor"),
+    )
+    return (
+        layer_output,
+        summed[7],
+        token_grad,
+        summed[0],
+        summed[1],
+        summed[2],
+        summed[3],
+        summed[4],
+        summed[5],
+        summed[6],
+        up_down[:width][None],
+        jnp.concatenate((up_down[width : width + half], up_down[width + half :]), axis=1)[None],
+    )
+
+
 def solution(mesh):
     placed = (
         P(("expert", "tensor"), None),
@@ -262,8 +935,9 @@
         P(("expert", "tensor"), None),
         P(("expert", "tensor"), None),
     )
+    near = mesh.shape["expert"] == 16 and mesh.shape["tensor"] == 2
     return jax.shard_map(
-        per_device,
+        per_device if near else moving_tokens,
         mesh=mesh,
         in_specs=placed,
         out_specs=(

time: 2350 us -> 763 us (0.32)
  blocking collectives: 1070 us -> 83 us
  matrix products: 458 us -> 68.7 us
  waiting for transfers between devices: 525 us -> 290 us
  Pallas kernels: 0 us -> 131 us
  local copies, waits for them, and re-layouts: 159 us -> 46.6 us
  starting transfers between devices: 14 us -> 65 us
  other arithmetic: 85.3 us -> 54.3 us
    all_to_all x2 -> x0, blocking collectives: 685 us -> none  [the longest x1 369 us: per_device(): lax.all_to_all(grad_copies, 'expert', split_axis=0, concat_axis=0, tiled=...]
    dot_general x91 -> x8, matrix products: 420 us -> 32.1 us  [the longest x2 10.9 us: unsort(): jnp.dot(back_order, high, preferred_element_type=jnp.float32)]
    psum x1 -> x0, blocking collectives: 343 us -> none  [per_device(): loads = lax.psum(jnp.sum(picks_float, axis=0), ('expert', 'tensor'))]
    all_to_all x2 -> x0, waiting for transfers between devices: 262 us -> none  [the longest x1 262 us: per_device(): lax.all_to_all(produced.reshape(arrived.shape), 'expert', split_axis=0, c...]
    ppermute x0 -> x44, waiting for transfers between devices: none -> 223 us  [the longest x14 120 us: beside(): return lax.ppermute(value, 'expert', pairs)]
    pallas_call x0 -> x3, Pallas kernels: none -> 131 us  [the longest x1 70.4 us: expert_stage(): pl.pallas_call(partial(expert_kernel_body, experts, sources, rows, limit,...]
    all_gather x2 -> x0, waiting for transfers between devices: 89.4 us -> none  [the longest x1 45.2 us: per_device(): incoming_pair = lax.all_gather(incoming, 'tensor', axis=0, tiled=True)]
    reduce_scatter x2 -> x0, waiting for transfers between devices: 80.6 us -> none  [the longest x1 40.3 us: per_device(): lax.psum_scatter(expert_forward(gathered, expanding[0], contracting[0]).a...]
  transfers between devices with their start and end apart: 7 -> 45, of which waited for: 6 -> 17; matrix products, arithmetic and copies ran while one was open for 4% -> 16% of each run, Pallas kernels for 0% -> 4%
where the time goes in v1:
time: 763 us; the launch traced here: 755 us
  waiting for transfers between devices  290 us (38%)
  Pallas kernels  131 us (17%)
  blocking collectives  83 us (11%)
  matrix products  68.7 us (9%)
  starting transfers between devices  65 us (9%)
  other arithmetic  54.3 us (7%)
  local copies, waits for them, and re-layouts  46.6 us (6%)
  between operations  16 us (2%)
    ppermute x14, waiting for transfers between devices, beside(): return lax.ppermute(value, 'expert', pairs)  120 us
    pallas_call x1, Pallas kernels, expert_stage(): pl.pallas_call(partial(expert_kernel_body, experts, sources, rows, limit,...  70.4 us
    psum x1, waiting for transfers between devices, per_device(): lax.psum((gain_grad, shift_grad, projection_grad, mixing_grad, factor_gra...  67.1 us
    ppermute x6, waiting for transfers between devices, swap(): return lax.ppermute(value, 'expert', [(i, i ^ bit) for i in range(groups)])  56.8 us
    unnamed x1, blocking collectives  42 us
    psum x1, blocking collectives, per_device(): lax.psum((gain_grad, shift_grad, projection_grad, mixing_grad, factor_gra...  41 us
    pallas_call x1, Pallas kernels, attend_backward(): pl.pallas_call(kernel, out_shape=(jax.ShapeDtypeStruct((count, width), jn...  31.8 us
    unnamed x142, local copies, waits for them, and re-layouts  31.5 us
  transfers between devices with their start and end apart: 45, of which 17 were waited for; matrix products, arithmetic and copies ran while one was open for 16% of the time, Pallas kernels for 4%

profile of v1, /device:TPU:0, one launch (start us, length us, event | category | flops | bytes accessed | tf_op | source)
XLA Modules:
  0.0 754.5 jit_solution(3479068867289471706)
XLA Ops:
  8.5 42.0 %all-reduce = s32[128]{0:T(128)S(1)} all-reduce(s32[128]{0:T(128)S(1)} %dynamic-update-slice), channel_id=2, replica_groups=mesh['expert'=16,'tensor'=2] {'expert','tensor'}, use_global_device_ids=true, to_apply=%add | all-reduce | flops 128 | bytes 1024
  56.9 3.9 copy.45
  63.3 7.0 convolution_convert_fusion.q_ref.k_ref.v_ref
  70.4 28.7 %shard_map.220 = (bf16[1152,768]{1,0:T(8,128)(2,1)}, f32[6,2,1152]{2,1,0:T(2,128)}) custom-call(s32[4]{0:T(128)} %bitcast.73, bf16[1152,2304]{1,0:T(8,128)(2,1)} %convolution_convert_fusion.q_ref.k_ref.v_ref, bf16[1152,2304]{1,0:T(8,128)(2,1)} %convolution_convert_fusion.q_ref.k_ref.v_ref, bf16[1152,2304]{1,0:T(8,128)(2,1)} %convolution_convert_fusion.q_ref.k_ref.v_ref), custom_call_target="tpu_custom_call" | custom-call | flops 4076863488 | bytes 7077888 | tf_op jit(solution)/shard_map/pallas_call | solution.py:324
  99.1 4.3 fusion.81
  110.8 3.7 collective-permute-start.9
  124.5 15.9 %collective-permute-done.9.refs_14_ = bf16[1536,384]{1,0:T(8,128)(2,1)S(1)} collective-permute-done((bf16[1536,384]{1,0:T(8,128)(2,1)S(1)}, bf16[1536,384]{1,0:T(8,128)(2,1)S(1)}, u32[]{:S(2)}, u32[]{:S(2)}) %collective-permute-start.9) | collective-permute-done | bytes 1179680 | tf_op jit(solution)/shard_map/ppermute | solution.py:723
  140.9 3.6 collective-permute-done.12.refs_16_
  144.6 23.4 %collective-permute-done.18.refs_22_ = bf16[1536,384]{1,0:T(8,128)(2,1)S(1)} collective-permute-done((bf16[1536,384]{1,0:T(8,128)(2,1)S(1)}, bf16[1536,384]{1,0:T(8,128)(2,1)S(1)}, u32[]{:S(2)}, u32[]{:S(2)}) %collective-permute-start.18) | collective-permute-done | bytes 1179680 | tf_op jit(solution)/shard_map/ppermute | solution.py:730
  170.8 31.3 %collective-permute-done.4.refs_6_ = bf16[1216,768]{1,0:T(8,128)(2,1)} collective-permute-done((bf16[1216,768]{1,0:T(8,128)(2,1)S(1)}, bf16[1216,768]{1,0:T(8,128)(2,1)}, u32[]{:S(2)}, u32[]{:S(2)}) %collective-permute-start.4) | collective-permute-done | bytes 1867808 | tf_op jit(solution)/shard_map/ppermute | solution.py:704
  208.8 22.4 %collective-permute-done.19.refs_23_ = bf16[1536,384]{1,0:T(8,128)(2,1)S(1)} collective-permute-done((bf16[1536,384]{1,0:T(8,128)(2,1)S(1)}, bf16[1536,384]{1,0:T(8,128)(2,1)S(1)}, u32[]{:S(2)}, u32[]{:S(2)}) %collective-permute-start.19) | collective-permute-done | bytes 1179680 | tf_op jit(solution)/shard_map/ppermute | solution.py:730
  238.2 3.4 collective-permute-start.21
  242.9 19.3 %collective-permute-done.20.refs_24_ = bf16[1536,384]{1,0:T(8,128)(2,1)} collective-permute-done((bf16[1536,384]{1,0:T(8,128)(2,1)}, bf16[1536,384]{1,0:T(8,128)(2,1)}, u32[]{:S(2)}, u32[]{:S(2)}) %collective-permute-start.20) | collective-permute-done | bytes 1179680 | tf_op jit(solution)/shard_map/ppermute | solution.py:730
  262.2 24.8 %collective-permute-done.21.refs_25_ = bf16[1536,384]{1,0:T(8,128)(2,1)} collective-permute-done((bf16[1536,384]{1,0:T(8,128)(2,1)}, bf16[1536,384]{1,0:T(8,128)(2,1)}, u32[]{:S(2)}, u32[]{:S(2)}) %collective-permute-start.21) | collective-permute-done | bytes 1179680 | tf_op jit(solution)/shard_map/ppermute | solution.py:730
  287.1 70.4 %shard_map.221 = (bf16[1216,768]{1,0:T(8,128)(2,1)}, bf16[1216,768]{1,0:T(8,128)(2,1)}, bf16[1216,768]{1,0:T(8,128)(2,1)}, bf16[1216,768]{1,0:T(8,128)(2,1)}, bf...) custom-call(s32[17]{0:T(128)} %concatenate.12.meta_ref, ...), custom_call_target="tpu_custom_call" | custom-call | flops 34426847232 | bytes 100000000 | tf_op jit(solution)/shard_map/pallas_call | solution.py:664
  357.5 5.7 slice_bitcast_fusion.7
  366.0 3.4 collective-permute-start.33
  369.6 24.6 %collective-permute-done.34 = bf16[1536,384]{1,0:T(8,128)(2,1)S(1)} collective-permute-done((bf16[1536,384]{1,0:T(8,128)(2,1)S(1)}, bf16[1536,384]{1,0:T(8,128)(2,1)S(1)}, u32[]{:S(2)}, u32[]{:S(2)}) %collective-permute-start.34) | collective-permute-done | bytes 1179680 | tf_op jit(solution)/shard_map/ppermute | solution.py:730
  401.0 3.9 copy.48
  404.9 3.5 collective-permute-start.32
  412.3 3.8 add_convert_fusion
  416.1 3.5 collective-permute-done.33
  421.6 3.5 fusion.45
  425.1 5.6 collective-permute-start.36
  432.6 5.1 fusion.26
  446.9 5.1 collective-permute-done.36
  452.6 4.9 fusion.47
  460.1 4.6 fusion.2
  467.0 4.9 multiply_reduce_fusion
  476.0 31.8 %shard_map.222 = (bf16[1152,768]{1,0:T(8,128)(2,1)}, bf16[1152,768]{1,0:T(8,128)(2,1)}, bf16[1152,768]{1,0:T(8,128)(2,1)}) custom-call(s32[4]{0:T(128)} %bitcast.74, bf16[1152,2304]{1,0:T(8,128)(2,1)} %convolution_convert_fusion.q_ref.k_ref.v_ref, bf16[1152,2304]{1,0:T(8,128)(2,1)} %convolution_convert_fusion.q_ref.k_ref.v_ref, ...), custom_call_target="tpu_custom_call" | custom-call | flops 10192158720 | bytes 14155776 | tf_op jit(solution)/shard_map/pallas_call | solution.py:406
  511.2 6.8 fusion.82
  518.0 7.3 fusion.76
  525.2 5.3 copy.51
  530.6 5.7 fusion.60
  536.3 4.3 fusion.24
  540.6 41.0 %all-reduce.1 = (f32[]{:T(128)}, f32[768]{0:T(1024)}, f32[768]{0:T(1024)}, f32[768]{0:T(1024)}, f32[768]{0:T(1024)}, /*index=5*/f32[4,768]{1,0:T(4,128)}) all-reduce(f32[]{:T(128)S(6)} %div.79, f32[768]{0:T(1024)} %get-tuple-element.88, f32[768]{0:T(1024)} %get-tuple-element.127, ...), channel_id=1, replica_groups=mesh['expert'=16,'tensor'=2] {'expert','tensor'}, use_global_device_ids=true, to_apply=%region_12.13 | all-reduce | flops 6145 | bytes 49160 | tf_op jit(solution)/shard_map/psum | solution.py:893
  584.7 3.5 fusion.40
  589.9 6.1 fusion.23
  596.0 5.2 copy.54
  601.1 5.1 collective-permute-start.37
  606.3 3.5 fusion.42
  611.5 23.1 %collective-permute-done.24 = bf16[1216,768]{1,0:T(8,128)(2,1)} collective-permute-done((bf16[1216,768]{1,0:T(8,128)(2,1)}, bf16[1216,768]{1,0:T(8,128)(2,1)}, u32[]{:S(2)}, u32[]{:S(2)}) %collective-permute-start.24) | collective-permute-done | bytes 1867808 | tf_op jit(solution)/shard_map/ppermute | solution.py:704
  634.6 4.5 fusion.4
  639.1 6.0 fusion.28
  645.1 3.9 copy.53
  649.0 17.8 %collective-permute-done.43 = bf16[1536,384]{1,0:T(8,128)(2,1)} collective-permute-done((bf16[1536,384]{1,0:T(8,128)(2,1)}, bf16[1536,384]{1,0:T(8,128)(2,1)}, u32[]{:S(2)}, u32[]{:S(2)}) %collective-permute-start.43) | collective-permute-done | bytes 1179680 | tf_op jit(solution)/shard_map/ppermute | solution.py:768
  672.3 67.1 %all-reduce.5.cloned.1.call-done = (f32[768,2304]{1,0:T(8,128)}, f32[768,768]{1,0:T(8,128)}) async-done(((f32[768,2304]{1,0:T(8,128)}, f32[768,768]{1,0:T(8,128)}), (f32[768,2304]{1,0:T(8,128)}, f32[768,768]{1,0:T(8,128)})) %all-reduce.5.cloned.1.call-update) | async-done | bytes 9437200 | tf_op jit(solution)/shard_map/psum | solution.py:893
  739.4 6.6 copy.64
  (251 shorter events, 98.0 us)
Async XLA Ops:
  7.2 732.2 %all-reduce.5.cloned.1.call-start = ((), (), s32[]{:S(2)}) async-start(), calls=%async_computation | async-start | bytes 18874368 | tf_op jit(solution)/shard_map/psum | solution.py:893
  108.2 10.9 %collective-permute-start.7 = (f32[8,1216]{1,0:T(8,128)S(1)}, f32[8,1216]{1,0:T(8,128)S(1)}, u32[]{:S(2)}, u32[]{:S(2)}) collective-permute-start(f32[8,1216]{1,0:T(8,128)S(1)} %broadcast_in_dim.64.refs_8_), channel_id=1, source_target_pairs={{0,4},{2,6},{4,0},{6,2},{8,12},{10,14},{12,8},{14,10},{16,20},{18,... | collective-permute-start | bytes 116744 | tf_op jit(solution)/shard_map/ppermute | solution.py:704
  110.6 11.6 %collective-permute-start.6 = (f32[8,1216]{1,0:T(8,128)S(1)}, f32[8,1216]{1,0:T(8,128)S(1)}, u32[]{:S(2)}, u32[]{:S(2)}) collective-permute-start(f32[8,1216]{1,0:T(8,128)S(1)} %broadcast_in_dim.64.refs_8_), channel_id=1, source_target_pairs={{0,1},{1,0},{2,3},{3,2},{4,5},{5,4},{6,7},{7,6},{8,9},{9,8},{10,11... | collective-permute-start | bytes 116744 | tf_op jit(solution)/shard_map/ppermute | solution.py:708
  110.8 29.6 %collective-permute-start.9 = (bf16[1536,384]{1,0:T(8,128)(2,1)S(1)}, bf16[1536,384]{1,0:T(8,128)(2,1)S(1)}, u32[]{:S(2)}, u32[]{:S(2)}) collective-permute-start(bf16[1536,384]{1,0:T(8,128)(2,1)S(1)} %pad_maximum_fusion.refs_15_), channel_id=1, source_target_pairs={{0,8},{2,10},{4,12},{6,14},{8,16},{10,18},{12,20},{14,22},{16,24},... | collective-permute-start | bytes 3538952 | tf_op jit(solution)/shard_map/ppermute | solution.py:723
  114.6 30.0 %collective-permute-start.12 = (bf16[1536,384]{1,0:T(8,128)(2,1)S(1)}, bf16[1536,384]{1,0:T(8,128)(2,1)S(1)}, u32[]{:S(2)}, u32[]{:S(2)}) collective-permute-start(bf16[1536,384]{1,0:T(8,128)(2,1)S(1)} %pad_maximum_fusion.refs_15_), channel_id=1, source_target_pairs={{8,0},{10,2},{12,4},{14,6},{16,8},{18,10},{20,12},{22,14},{24,16},... | collective-permute-start | bytes 3538952 | tf_op jit(solution)/shard_map/ppermute | solution.py:723
  119.0 49.7 %collective-permute-start.1 = (bf16[1216,768]{1,0:T(8,128)(2,1)S(1)}, bf16[1216,768]{1,0:T(8,128)(2,1)}, u32[]{:S(2)}, u32[]{:S(2)}) collective-permute-start(bf16[1216,768]{1,0:T(8,128)(2,1)S(1)} %fusion.29.refs_0_), channel_id=1, source_target_pairs={{0,4},{2,6},{4,0},{6,2},{8,12},{10,14},{12,8},{14,10},{16,20},{18,... | collective-permute-start | bytes 5603336 | tf_op jit(solution)/shard_map/ppermute | solution.py:704
  119.2 3.4 collective-permute-start.8
  122.2 115.0 %copy-start.59 = (f32[8,1216]{1,0:T(8,128)}, f32[8,1216]{1,0:T(8,128)S(1)}, u32[]{:S(2)}) copy-start(f32[8,1216]{1,0:T(8,128)S(1)} %collective-permute-done.6.refs_9_) | copy-start | bytes 116740
  122.2 47.8 %collective-permute-start = (bf16[1216,768]{1,0:T(8,128)(2,1)S(1)}, bf16[1216,768]{1,0:T(8,128)(2,1)S(1)}, u32[]{:S(2)}, u32[]{:S(2)}) collective-permute-start(bf16[1216,768]{1,0:T(8,128)(2,1)S(1)} %fusion.29.refs_0_), channel_id=1, source_target_pairs={{0,1},{1,0},{2,3},{3,2},{4,5},{5,4},{6,7},{7,6},{8,9},{9,8},{10,11... | collective-permute-start | bytes 5603336 | tf_op jit(solution)/shard_map/ppermute | solution.py:708
  122.5 79.5 %collective-permute-start.4 = (bf16[1216,768]{1,0:T(8,128)(2,1)S(1)}, bf16[1216,768]{1,0:T(8,128)(2,1)}, u32[]{:S(2)}, u32[]{:S(2)}) collective-permute-start(bf16[1216,768]{1,0:T(8,128)(2,1)S(1)} %fusion.30.refs_4_), channel_id=1, source_target_pairs={{0,4},{2,6},{4,0},{6,2},{8,12},{10,14},{12,8},{14,10},{16,20},{18,... | collective-permute-start | bytes 5603336 | tf_op jit(solution)/shard_map/ppermute | solution.py:704
  140.4 68.4 %copy-start.51 = (bf16[1536,384]{1,0:T(8,128)(2,1)}, bf16[1536,384]{1,0:T(8,128)(2,1)S(1)}, u32[]{:S(2)}) copy-start(bf16[1536,384]{1,0:T(8,128)(2,1)S(1)} %collective-permute-done.9.refs_14_) | copy-start | bytes 3538948
  140.4 27.6 %collective-permute-start.18 = (bf16[1536,384]{1,0:T(8,128)(2,1)S(1)}, bf16[1536,384]{1,0:T(8,128)(2,1)S(1)}, u32[]{:S(2)}, u32[]{:S(2)}) collective-permute-start(bf16[1536,384]{1,0:T(8,128)(2,1)S(1)} %pad_maximum_fusion.refs_15_), channel_id=1, source_target_pairs={{0,2},{2,0},{4,6},{6,4},{8,10},{10,8},{12,14},{14,12},{16,18},{18,... | collective-permute-start | bytes 3538952 | tf_op jit(solution)/shard_map/ppermute | solution.py:730
  144.5 64.3 %copy-start.52 = (bf16[1536,384]{1,0:T(8,128)(2,1)}, bf16[1536,384]{1,0:T(8,128)(2,1)S(1)}, u32[]{:S(2)}) copy-start(bf16[1536,384]{1,0:T(8,128)(2,1)S(1)} %collective-permute-done.12.refs_16_) | copy-start | bytes 3538948
  144.5 63.0 %collective-permute-start.3 = (bf16[1216,768]{1,0:T(8,128)(2,1)S(1)}, bf16[1216,768]{1,0:T(8,128)(2,1)S(1)}, u32[]{:S(2)}, u32[]{:S(2)}) collective-permute-start(bf16[1216,768]{1,0:T(8,128)(2,1)S(1)} %fusion.30.refs_4_), channel_id=1, source_target_pairs={{0,1},{1,0},{2,3},{3,2},{4,5},{5,4},{6,7},{7,6},{8,9},{9,8},{10,11... | collective-permute-start | bytes 5603336 | tf_op jit(solution)/shard_map/ppermute | solution.py:708
  168.0 36.5 %collective-permute-start.10 = (bf16[1536,384]{1,0:T(8,128)(2,1)S(1)}, bf16[1536,384]{1,0:T(8,128)(2,1)S(1)}, u32[]{:S(2)}, u32[]{:S(2)}) collective-permute-start(bf16[1536,384]{1,0:T(8,128)(2,1)S(1)} %collective-permute-done.9.refs_14_), channel_id=1, source_target_pairs={{8,16},{10,18},{12,20},{14,22},{16,24},{18,26},{20,28},{22,30},{9,... | collective-permute-start | bytes 3538952 | tf_op jit(solution)/shard_map/ppermute | solution.py:723
  168.7 37.5 %collective-permute-start.13 = (bf16[1536,384]{1,0:T(8,128)(2,1)S(1)}, bf16[1536,384]{1,0:T(8,128)(2,1)}, u32[]{:S(2)}, u32[]{:S(2)}) collective-permute-start(bf16[1536,384]{1,0:T(8,128)(2,1)S(1)} %collective-permute-done.12.refs_16_), channel_id=1, source_target_pairs={{8,0},{10,2},{12,4},{14,6},{16,8},{18,10},{20,12},{22,14},{9,1},{1... | collective-permute-start | bytes 3538952 | tf_op jit(solution)/shard_map/ppermute | solution.py:723
  170.0 38.7 %collective-permute-start.17 = (bf16[1536,384]{1,0:T(8,128)(2,1)S(1)}, bf16[1536,384]{1,0:T(8,128)(2,1)S(1)}, u32[]{:S(2)}, u32[]{:S(2)}) collective-permute-start(bf16[1536,384]{1,0:T(8,128)(2,1)S(1)} %collective-permute-done.9.refs_14_), channel_id=1, source_target_pairs={{8,10},{10,8},{12,14},{14,12},{16,18},{18,16},{20,22},{22,20},{24,... | collective-permute-start | bytes 3538952 | tf_op jit(solution)/shard_map/ppermute | solution.py:730
  202.0 29.2 %collective-permute-start.19 = (bf16[1536,384]{1,0:T(8,128)(2,1)S(1)}, bf16[1536,384]{1,0:T(8,128)(2,1)S(1)}, u32[]{:S(2)}, u32[]{:S(2)}) collective-permute-start(bf16[1536,384]{1,0:T(8,128)(2,1)S(1)} %collective-permute-done.12.refs_16_), channel_id=1, source_target_pairs={{0,2},{2,0},{4,6},{6,4},{8,10},{10,8},{12,14},{14,12},{16,18},{18,... | collective-permute-start | bytes 3538952 | tf_op jit(solution)/shard_map/ppermute | solution.py:730
  204.5 26.7 %collective-permute-start.11 = (bf16[1536,384]{1,0:T(8,128)(2,1)S(1)}, bf16[1536,384]{1,0:T(8,128)(2,1)}, u32[]{:S(2)}, u32[]{:S(2)}) collective-permute-start(bf16[1536,384]{1,0:T(8,128)(2,1)S(1)} %collective-permute-done.10.refs_13_), channel_id=1, source_target_pairs={{16,24},{18,26},{20,28},{22,30},{17,25},{19,27},{21,29},{23,31}} | collective-permute-start | bytes 3538952 | tf_op jit(solution)/shard_map/ppermute | solution.py:723
  206.2 29.2 %collective-permute-start.14 = (bf16[1536,384]{1,0:T(8,128)(2,1)}, bf16[1536,384]{1,0:T(8,128)(2,1)}, u32[]{:S(2)}, u32[]{:S(2)}) collective-permute-start(bf16[1536,384]{1,0:T(8,128)(2,1)} %collective-permute-done.13.refs_17_), channel_id=1, source_target_pairs={{8,0},{10,2},{12,4},{14,6},{9,1},{11,3},{13,5},{15,7}} | collective-permute-start | bytes 3538952 | tf_op jit(solution)/shard_map/ppermute | solution.py:723
  207.5 29.6 %collective-permute-start.16 = (bf16[1536,384]{1,0:T(8,128)(2,1)S(1)}, bf16[1536,384]{1,0:T(8,128)(2,1)S(1)}, u32[]{:S(2)}, u32[]{:S(2)}) collective-permute-start(bf16[1536,384]{1,0:T(8,128)(2,1)S(1)} %collective-permute-done.10.refs_13_), channel_id=1, source_target_pairs={{16,18},{18,16},{20,22},{22,20},{24,26},{26,24},{28,30},{30,28},{1... | collective-permute-start | bytes 3538952 | tf_op jit(solution)/shard_map/ppermute | solution.py:730
  208.7 53.5 %collective-permute-start.2 = (bf16[1216,768]{1,0:T(8,128)(2,1)}, bf16[1216,768]{1,0:T(8,128)(2,1)}, u32[]{:S(2)}, u32[]{:S(2)}) collective-permute-start(bf16[1216,768]{1,0:T(8,128)(2,1)} %collective-permute-done.1.refs_2_), channel_id=1, source_target_pairs={{0,1},{1,0},{2,3},{3,2},{4,5},{5,4},{6,7},{7,6},{8,9},{9,8},{10,11... | collective-permute-start | bytes 5603336 | tf_op jit(solution)/shard_map/ppermute | solution.py:708
  231.2 31.0 %collective-permute-start.5 = (bf16[1216,768]{1,0:T(8,128)(2,1)}, bf16[1216,768]{1,0:T(8,128)(2,1)}, u32[]{:S(2)}, u32[]{:S(2)}) collective-permute-start(bf16[1216,768]{1,0:T(8,128)(2,1)} %collective-permute-done.4.refs_6_), channel_id=1, source_target_pairs={{0,1},{1,0},{2,3},{3,2},{4,5},{5,4},{6,7},{7,6},{8,9},{9,8},{10,11... | collective-permute-start | bytes 5603336 | tf_op jit(solution)/shard_map/ppermute | solution.py:708
  231.2 31.0 %collective-permute-start.20 = (bf16[1536,384]{1,0:T(8,128)(2,1)}, bf16[1536,384]{1,0:T(8,128)(2,1)}, u32[]{:S(2)}, u32[]{:S(2)}) collective-permute-start(bf16[1536,384]{1,0:T(8,128)(2,1)} %collective-permute-done.13.refs_17_), channel_id=1, source_target_pairs={{0,2},{2,0},{4,6},{6,4},{8,10},{10,8},{12,14},{14,12},{1,3},{3,1},... | collective-permute-start | bytes 3538952 | tf_op jit(solution)/shard_map/ppermute | solution.py:730
  235.4 26.8 %collective-permute-start.15 = (bf16[1536,384]{1,0:T(8,128)(2,1)}, bf16[1536,384]{1,0:T(8,128)(2,1)}, u32[]{:S(2)}, u32[]{:S(2)}) collective-permute-start(bf16[1536,384]{1,0:T(8,128)(2,1)} %collective-permute-done.11.refs_12_), channel_id=1, source_target_pairs={{24,26},{26,24},{28,30},{30,28},{25,27},{27,25},{29,31},{31,29}} | collective-permute-start | bytes 3538952 | tf_op jit(solution)/shard_map/ppermute | solution.py:730
  238.2 48.9 %collective-permute-start.21 = (bf16[1536,384]{1,0:T(8,128)(2,1)}, bf16[1536,384]{1,0:T(8,128)(2,1)}, u32[]{:S(2)}, u32[]{:S(2)}) collective-permute-start(bf16[1536,384]{1,0:T(8,128)(2,1)} %collective-permute-done.14.refs_18_), channel_id=1, source_target_pairs={{0,2},{2,0},{4,6},{6,4},{1,3},{3,1},{5,7},{7,5}} | collective-permute-start | bytes 3538952 | tf_op jit(solution)/shard_map/ppermute | solution.py:730
  363.3 30.9 %collective-permute-start.34 = (bf16[1536,384]{1,0:T(8,128)(2,1)S(1)}, bf16[1536,384]{1,0:T(8,128)(2,1)S(1)}, u32[]{:S(2)}, u32[]{:S(2)}) collective-permute-start(bf16[1536,384]{1,0:T(8,128)(2,1)S(1)} %get-tuple-element.105), channel_id=1, source_target_pairs={{0,2},{2,0},{4,6},{6,4},{1,3},{3,1},{5,7},{7,5}} | collective-permute-start | bytes 3538952 | tf_op jit(solution)/shard_map/ppermute | solution.py:730
  365.9 44.7 %collective-permute-start.26 = (bf16[1216,768]{1,0:T(8,128)(2,1)}, bf16[1216,768]{1,0:T(8,128)(2,1)}, u32[]{:S(2)}, u32[]{:S(2)}) collective-permute-start(bf16[1216,768]{1,0:T(8,128)(2,1)} %get-tuple-element.39), channel_id=1, source_target_pairs={{0,1},{1,0},{2,3},{3,2},{4,5},{5,4},{6,7},{7,6},{8,9},{9,8},{10,11... | collective-permute-start | bytes 5603336 | tf_op jit(solution)/shard_map/ppermute | solution.py:708
  366.0 53.6 %collective-permute-start.33 = (bf16[1536,384]{1,0:T(8,128)(2,1)}, bf16[1536,384]{1,0:T(8,128)(2,1)}, u32[]{:S(2)}, u32[]{:S(2)}) collective-permute-start(bf16[1536,384]{1,0:T(8,128)(2,1)} %get-tuple-element.106), channel_id=1, source_target_pairs={{0,2},{2,0},{4,6},{6,4},{8,10},{10,8},{12,14},{14,12},{1,3},{3,1},... | collective-permute-start | bytes 3538952 | tf_op jit(solution)/shard_map/ppermute | solution.py:730
  369.4 29.8 %collective-permute-start.29 = (f32[8,1216]{1,0:T(8,128)S(1)}, f32[8,1216]{1,0:T(8,128)S(1)}, u32[]{:S(2)}, u32[]{:S(2)}) collective-permute-start(f32[8,1216]{1,0:T(8,128)S(1)} %copy-done.61), channel_id=1, source_target_pairs={{0,1},{1,0},{2,3},{3,2},{4,5},{5,4},{6,7},{7,6},{8,9},{9,8},{10,11... | collective-permute-start | bytes 116744 | tf_op jit(solution)/shard_map/ppermute | solution.py:708
  396.9 24.7 %collective-permute-start.35 = (bf16[1536,384]{1,0:T(8,128)(2,1)}, bf16[1536,384]{1,0:T(8,128)(2,1)}, u32[]{:S(2)}, u32[]{:S(2)}) collective-permute-start(bf16[1536,384]{1,0:T(8,128)(2,1)} %fusion.43), channel_id=1, source_target_pairs={{0,8},{2,10},{4,12},{6,14},{1,9},{3,11},{5,13},{7,15}} | collective-permute-start | bytes 3538952 | tf_op jit(solution)/shard_map/ppermute | solution.py:768
  399.2 5.7 collective-permute-start.28
  399.8 8.5 %collective-permute-start.30 = (f32[8,1216]{1,0:T(8,128)}, f32[8,1216]{1,0:T(8,128)}, u32[]{:S(2)}, u32[]{:S(2)}) collective-permute-start(f32[8,1216]{1,0:T(8,128)} %add.224), channel_id=1, source_target_pairs={{0,4},{2,6},{4,0},{6,2},{8,12},{10,14},{12,8},{14,10},{16,20},{18,... | collective-permute-start | bytes 116744 | tf_op jit(solution)/shard_map/ppermute | solution.py:704
  404.9 38.7 %collective-permute-start.32 = (bf16[1536,384]{1,0:T(8,128)(2,1)}, bf16[1536,384]{1,0:T(8,128)(2,1)}, u32[]{:S(2)}, u32[]{:S(2)}) collective-permute-start(bf16[1536,384]{1,0:T(8,128)(2,1)} %get-tuple-element.107), channel_id=1, source_target_pairs={{0,2},{2,0},{4,6},{6,4},{8,10},{10,8},{12,14},{14,12},{16,18},{18,... | collective-permute-start | bytes 3538952 | tf_op jit(solution)/shard_map/ppermute | solution.py:730
  408.3 29.4 %collective-permute-start.23 = (bf16[1216,768]{1,0:T(8,128)(2,1)}, bf16[1216,768]{1,0:T(8,128)(2,1)}, u32[]{:S(2)}, u32[]{:S(2)}) collective-permute-start(bf16[1216,768]{1,0:T(8,128)(2,1)} %get-tuple-element.35), channel_id=1, source_target_pairs={{0,1},{1,0},{2,3},{3,2},{4,5},{5,4},{6,7},{7,6},{8,9},{9,8},{10,11... | collective-permute-start | bytes 5603336 | tf_op jit(solution)/shard_map/ppermute | solution.py:708
  410.6 34.6 %collective-permute-start.40 = (bf16[1536,384]{1,0:T(8,128)(2,1)}, bf16[1536,384]{1,0:T(8,128)(2,1)}, u32[]{:S(2)}, u32[]{:S(2)}) collective-permute-start(bf16[1536,384]{1,0:T(8,128)(2,1)} %get-tuple-element.102), channel_id=1, source_target_pairs={{24,26},{26,24},{28,30},{30,28},{25,27},{27,25},{29,31},{31,29}} | collective-permute-start | bytes 3538952 | tf_op jit(solution)/shard_map/ppermute | solution.py:730
  419.6 40.4 %collective-permute-start.27 = (bf16[1216,768]{1,0:T(8,128)(2,1)}, bf16[1216,768]{1,0:T(8,128)(2,1)}, u32[]{:S(2)}, u32[]{:S(2)}) collective-permute-start(bf16[1216,768]{1,0:T(8,128)(2,1)} %add_convert_fusion), channel_id=1, source_target_pairs={{0,4},{2,6},{4,0},{6,2},{8,12},{10,14},{12,8},{14,10},{16,20},{18,... | collective-permute-start | bytes 5603336 | tf_op jit(solution)/shard_map/ppermute | solution.py:704
  425.1 26.9 %collective-permute-start.36 = (bf16[1536,384]{1,0:T(8,128)(2,1)}, bf16[1536,384]{1,0:T(8,128)(2,1)}, u32[]{:S(2)}, u32[]{:S(2)}) collective-permute-start(bf16[1536,384]{1,0:T(8,128)(2,1)} %fusion.45), channel_id=1, source_target_pairs={{0,8},{2,10},{4,12},{6,14},{8,16},{10,18},{12,20},{14,22},{1,9},{3... | collective-permute-start | bytes 3538952 | tf_op jit(solution)/shard_map/ppermute | solution.py:768
  437.8 27.0 %collective-permute-start.25 = (bf16[1216,768]{1,0:T(8,128)(2,1)S(1)}, bf16[1216,768]{1,0:T(8,128)(2,1)S(1)}, u32[]{:S(2)}, u32[]{:S(2)}) collective-permute-start(bf16[1216,768]{1,0:T(8,128)(2,1)S(1)} %copy-done.45), channel_id=1, source_target_pairs={{0,1},{1,0},{2,3},{3,2},{4,5},{5,4},{6,7},{7,6},{8,9},{9,8},{10,11... | collective-permute-start | bytes 5603336 | tf_op jit(solution)/shard_map/ppermute | solution.py:708
  443.5 138.7 %collective-permute-start.39 = (bf16[1536,384]{1,0:T(8,128)(2,1)}, bf16[1536,384]{1,0:T(8,128)(2,1)}, u32[]{:S(2)}, u32[]{:S(2)}) collective-permute-start(bf16[1536,384]{1,0:T(8,128)(2,1)} %get-tuple-element.103), channel_id=1, source_target_pairs={{16,18},{18,16},{20,22},{22,20},{24,26},{26,24},{28,30},{30,28},{1... | collective-permute-start | bytes 3538952 | tf_op jit(solution)/shard_map/ppermute | solution.py:730
  445.2 155.9 %collective-permute-start.38 = (bf16[1536,384]{1,0:T(8,128)(2,1)}, bf16[1536,384]{1,0:T(8,128)(2,1)}, u32[]{:S(2)}, u32[]{:S(2)}) collective-permute-start(bf16[1536,384]{1,0:T(8,128)(2,1)} %get-tuple-element.104), channel_id=1, source_target_pairs={{8,10},{10,8},{12,14},{14,12},{16,18},{18,16},{20,22},{22,20},{24,... | collective-permute-start | bytes 3538952 | tf_op jit(solution)/shard_map/ppermute | solution.py:730
  452.0 197.0 %collective-permute-start.31 = (bf16[1536,384]{1,0:T(8,128)(2,1)}, bf16[1536,384]{1,0:T(8,128)(2,1)}, u32[]{:S(2)}, u32[]{:S(2)}) collective-permute-start(bf16[1536,384]{1,0:T(8,128)(2,1)} %get-tuple-element.101), channel_id=1, source_target_pairs={{0,2},{2,0},{4,6},{6,4},{8,10},{10,8},{12,14},{14,12},{16,18},{18,... | collective-permute-start | bytes 3538952 | tf_op jit(solution)/shard_map/ppermute | solution.py:730
  460.0 179.1 %collective-permute-start.22 = (bf16[1216,768]{1,0:T(8,128)(2,1)}, bf16[1216,768]{1,0:T(8,128)(2,1)}, u32[]{:S(2)}, u32[]{:S(2)}) collective-permute-start(bf16[1216,768]{1,0:T(8,128)(2,1)} %get-tuple-element.33), channel_id=1, source_target_pairs={{0,1},{1,0},{2,3},{3,2},{4,5},{5,4},{6,7},{7,6},{8,9},{9,8},{10,11... | collective-permute-start | bytes 5603336 | tf_op jit(solution)/shard_map/ppermute | solution.py:708
  464.8 119.9 %collective-permute-start.41 = (bf16[1536,384]{1,0:T(8,128)(2,1)}, bf16[1536,384]{1,0:T(8,128)(2,1)}, u32[]{:S(2)}, u32[]{:S(2)}) collective-permute-start(bf16[1536,384]{1,0:T(8,128)(2,1)} %get-tuple-element.109), channel_id=1, source_target_pairs={{24,16},{26,18},{28,20},{30,22},{25,17},{27,19},{29,21},{31,23}} | collective-permute-start | bytes 3538952 | tf_op jit(solution)/shard_map/ppermute | solution.py:768
  582.3 52.3 %collective-permute-start.24 = (bf16[1216,768]{1,0:T(8,128)(2,1)}, bf16[1216,768]{1,0:T(8,128)(2,1)}, u32[]{:S(2)}, u32[]{:S(2)}) collective-permute-start(bf16[1216,768]{1,0:T(8,128)(2,1)} %add_convert_fusion.2), channel_id=1, source_target_pairs={{0,4},{2,6},{4,0},{6,2},{8,12},{10,14},{12,8},{14,10},{16,20},{18,... | collective-permute-start | bytes 5603336 | tf_op jit(solution)/shard_map/ppermute | solution.py:704
  588.2 18.1 %collective-permute-start.42 = (bf16[1536,384]{1,0:T(8,128)(2,1)}, bf16[1536,384]{1,0:T(8,128)(2,1)}, u32[]{:S(2)}, u32[]{:S(2)}) collective-permute-start(bf16[1536,384]{1,0:T(8,128)(2,1)} %fusion.40), channel_id=1, source_target_pairs={{16,8},{18,10},{20,12},{22,14},{24,16},{26,18},{28,20},{30,22},{17... | collective-permute-start | bytes 3538952 | tf_op jit(solution)/shard_map/ppermute | solution.py:768
  601.1 47.9 %collective-permute-start.37 = (bf16[1536,384]{1,0:T(8,128)(2,1)}, bf16[1536,384]{1,0:T(8,128)(2,1)}, u32[]{:S(2)}, u32[]{:S(2)}) collective-permute-start(bf16[1536,384]{1,0:T(8,128)(2,1)} %get-tuple-element.108), channel_id=1, source_target_pairs={{0,8},{2,10},{4,12},{6,14},{8,16},{10,18},{12,20},{14,22},{16,24},... | collective-permute-start | bytes 3538952 | tf_op jit(solution)/shard_map/ppermute | solution.py:768
  609.7 57.1 %collective-permute-start.43 = (bf16[1536,384]{1,0:T(8,128)(2,1)}, bf16[1536,384]{1,0:T(8,128)(2,1)}, u32[]{:S(2)}, u32[]{:S(2)}) collective-permute-start(bf16[1536,384]{1,0:T(8,128)(2,1)} %fusion.42), channel_id=1, source_target_pairs={{8,0},{10,2},{12,4},{14,6},{16,8},{18,10},{20,12},{22,14},{24,16},... | collective-permute-start | bytes 3538952 | tf_op jit(solution)/shard_map/ppermute | solution.py:768
  (63 other events, 786.4 us)
Sparse Core Ops, SparseCore 0:
  536.4 202.9 all-reduce.4

commit v2 on v1

--- a/solution.py
+++ b/solution.py
@@ -280,72 +280,6 @@
         end = end + lengths_ref[d]
         starts = jnp.where(places >= end, end, starts)
     return starts
-
-
-def attend_forward(joint, lengths):
-    count, width = joint.shape[0], joint.shape[1] // 3
-    pairs = width // 128
-    factor = (width // HEADS) ** (-0.5) * HALF_LOG
-
-    def kernel(lengths_ref, q_ref, k_ref, v_ref, o_ref, l_ref, bias_ref):
-        @pl.when(pl.program_id(0) == 0)
-        def _():
-            rows = lax.broadcasted_iota(jnp.int32, (count, 1), 0)
-            starts = document_starts(lengths_ref, rows)
-            for s, e in query_blocks(count):
-                column = lax.broadcasted_iota(jnp.int32, (count, e - s), 1) + s
-                seen = (column <= rows) & (column >= starts)
-                bias_ref[:, s:e] = jnp.where(seen, 0.0, -1e9)
-
-        first = lax.broadcasted_iota(jnp.int32, (1, 128), 1) < 64
-        for s, e in query_blocks(count):
-            outs, logs = [], []
-            for half in range(2):
-                q = jnp.where(first == (half == 0), q_ref[s:e, :], jnp.bfloat16(0))
-                scores = lax.dot_general(
-                    q, k_ref[0:e, :], NT, preferred_element_type=jnp.float32
-                )
-                scores = scores * factor + bias_ref[s:e, 0:e]
-                peak = jnp.max(scores, axis=1, keepdims=True)
-                weights = jnp.exp2(scores - peak)
-                total = jnp.sum(weights, axis=1, keepdims=True)
-                mixed = jnp.dot(
-                    weights.astype(jnp.bfloat16),
-                    v_ref[0:e, :],
-                    preferred_element_type=jnp.float32,
-                )
-                outs.append(mixed / total)
-                logs.append(peak + jnp.log2(total))
-            o_ref[s:e, :] = jnp.where(first, outs[0], outs[1]).astype(jnp.bfloat16)
-            spread = jnp.transpose(jnp.where(first, logs[0], logs[1]))
-            l_ref[0, 0:1, s:e] = spread[0:1, :]
-            l_ref[0, 1:2, s:e] = spread[64:65, :]
-
-    return pl.pallas_call(
-        kernel,
-        out_shape=(
-            jax.ShapeDtypeStruct((count, width), jnp.bfloat16),
-            jax.ShapeDtypeStruct((pairs, 2, count), jnp.float32),
-        ),
-        grid_spec=pltpu.PrefetchScalarGridSpec(
-            num_scalar_prefetch=1,
-            grid=(pairs,),
-            in_specs=[
-                pl.BlockSpec((count, 128), lambda p, _: (0, p)),
-                pl.BlockSpec((count, 128), lambda p, _: (0, pairs + p)),
-                pl.BlockSpec((count, 128), lambda p, _: (0, 2 * pairs + p)),
-            ],
-            out_specs=(
-                pl.BlockSpec((count, 128), lambda p, _: (0, p)),
-                pl.BlockSpec((1, 2, count), lambda p, _: (p, 0, 0)),
-            ),
-            scratch_shapes=[pltpu.VMEM((count, count), jnp.float32)],
-        ),
-        compiler_params=pltpu.CompilerParams(vmem_limit_bytes=VMEM_LIMIT),
-        cost_estimate=pl.CostEstimate(
-            flops=4 * count * count * width, bytes_accessed=8 * count * width, transcendentals=count * count * HEADS
-        ),
-    )(lengths, joint, joint, joint)
 
 
 def attend_backward(joint, mixed, upstream, logs, lengths):
@@ -431,6 +365,435 @@
     )(lengths, joint, joint, joint, mixed, upstream, logs)
 
 
+MESH = pl.DeviceIdType.MESH
+
+
+def neighbours(slabs):
+    me, core = lax.axis_index("expert"), lax.axis_index("tensor")
+    plane = lax.div(me, slabs)
+    x = lax.rem(me, 2)
+    y = lax.rem(lax.div(me, 2), 2)
+    return me, core, plane, (me + 1 - 2 * x, core), (me + 2 - 4 * y, core), (me, 1 - core)
+
+
+def greet(partners):
+    barrier = pltpu.get_barrier_semaphore()
+    number = 0
+    for device, there in partners:
+        @pl.when(there)
+        def _(device=device):
+            pl.semaphore_signal(barrier, inc=1, device_id=device, device_id_type=MESH)
+        number = number + there.astype(jnp.int32)
+    pl.semaphore_wait(barrier, number)
+
+
+def score_bias(bias_ref, lengths_ref, count):
+    places = lax.broadcasted_iota(jnp.int32, (1, count), 1)
+    starts = document_starts(lengths_ref, places)
+    for s, e in query_blocks(count):
+        row = lax.broadcasted_iota(jnp.int32, (e - s, count), 0) + s
+        seen = (row <= places) & (row >= starts)
+        bias_ref[s:e, :] = jnp.where(seen, 0.0, -1e9)
+
+
+def row_norm(values, gain, shift):
+    centered = values - jnp.mean(values, axis=1, keepdims=True)
+    scale = lax.rsqrt(jnp.mean(centered * centered, axis=1, keepdims=True) + epsilon)
+    normal = centered * scale
+    return normal * gain + shift, normal, scale
+
+
+def chosen_rows(route, centroids_ref, experts):
+    chosen = jnp.zeros((route.shape[0], centroids_ref.shape[1]), jnp.float32)
+    for e in range(experts):
+        chosen = jnp.where(route == e, centroids_ref[e : e + 1, :].astype(jnp.float32), chosen)
+    return chosen
+
+
+def front_kernel(
+    planes,
+    slabs,
+    lengths_ref,
+    tokens_ref,
+    gains_ref,
+    shifts_ref,
+    projection_ref,
+    mixing_ref,
+    factors_ref,
+    biases_ref,
+    centroids_ref,
+    route_row_ref,
+    route_ref,
+    cot_ref,
+    up_ref,
+    down_ref,
+    entry_ref,
+    joint_ref,
+    mixed_ref,
+    logs_ref,
+    residual_ref,
+    place_ref,
+    loads_ref,
+    sent_own,
+    cot_own,
+    gate_own,
+    sent_others,
+    cot_others,
+    gate_others,
+    up_near,
+    up_far,
+    down_near,
+    down_far,
+    bias_ref,
+    order_ref,
+    normed_ref,
+    tally_ref,
+    send_sem,
+    recv_sem,
+    local_sem,
+):
+    count, width = tokens_ref.shape
+    experts = planes
+    rows = sent_own.shape[0]
+    half_rows = rows // 2
+    pairs = width // 128
+    factor = (width // HEADS) ** (-0.5) * HALF_LOG
+    middle = planes - 1
+    me, core, plane, beside_x, beside_y, beside_core = neighbours(slabs)
+    hop_two = lax.rem(plane + 2, planes)
+    hop_one = plane + 1 - 2 * lax.rem(plane, 2)
+    here = lax.rem(me, slabs)
+    always = plane >= 0
+    greet(
+        [
+            (beside_x, always),
+            (beside_y, always),
+            (beside_core, always),
+            ((hop_two * slabs + here, core), always),
+            ((me + slabs, core), plane < planes - 1),
+            ((me - slabs, core), plane > 0),
+        ]
+    )
+
+    def remote(i, src, dst, device):
+        return pltpu.make_async_remote_copy(
+            src_ref=src, dst_ref=dst, send_sem=send_sem.at[i], recv_sem=recv_sem.at[i], device_id=device, device_id_type=MESH
+        )
+
+    owns, nears, fars = (up_ref, down_ref), (up_near, down_near), (up_far, down_far)
+    stride = 2 * (planes - 1) + 2 * planes - 1
+
+    def hop(kind, sign, r):
+        src = owns[kind].at[0] if r == 1 else nears[kind].at[middle - sign * (r - 1)]
+        i = kind * stride + (r - 1) * 2 + (sign > 0)
+        return remote(i, src, nears[kind].at[middle - sign * r], (me + sign * slabs, core))
+
+    def hop_sent(sign, r):
+        ahead = plane if sign > 0 else planes - 1 - plane
+        return (ahead >= r - 1) & (ahead < planes - 1)
+
+    def hop_came(sign, r):
+        ahead = plane if sign > 0 else planes - 1 - plane
+        return ahead >= r
+
+    def aside(kind, slot):
+        src = owns[kind].at[0] if slot == middle else nears[kind].at[slot]
+        i = kind * stride + 2 * (planes - 1) + slot
+        return remote(i, src, fars[kind].at[slot], beside_x)
+
+    def held(slot):
+        at = plane + slot - middle
+        return (at >= 0) & (at < planes)
+
+    def own_weights(kind):
+        return pltpu.make_async_copy(owns[kind].at[0], nears[kind].at[middle], local_sem.at[kind])
+
+    for kind in range(2):
+        for sign in (1, -1):
+            @pl.when(hop_sent(sign, 1))
+            def _(kind=kind, sign=sign):
+                hop(kind, sign, 1).start()
+        aside(kind, middle).start()
+        own_weights(kind).start()
+
+    def forward_weights(kind, r):
+        for sign in (1, -1):
+            slot = middle - sign * r
+
+            @pl.when(hop_came(sign, r))
+            def _(sign=sign, slot=slot):
+                hop(kind, sign, r).wait_recv()
+                aside(kind, slot).start()
+
+            if r < planes - 1:
+                @pl.when(hop_sent(sign, r + 1))
+                def _(sign=sign):
+                    hop(kind, sign, r + 1).start()
+
+    base = 2 * stride
+
+    def row_copy(which, part, piece):
+        own, others = ((cot_own, cot_others), (sent_own, sent_others))[which]
+        at = pl.ds(piece * half_rows, half_rows)
+        i = base + which * 6 + part * 2 + piece
+        if part == 0:
+            return remote(i, own.at[at], others.at[1, at], beside_y)
+        if part == 1:
+            return remote(i, own.at[at], others.at[0, at], beside_core)
+        return remote(i, others.at[1, at], others.at[2, at], beside_core)
+
+    def gate_copy(part):
+        i = base + 12 + part
+        if part == 0:
+            return remote(i, gate_own, gate_others.at[1], beside_y)
+        if part == 1:
+            return remote(i, gate_own, gate_others.at[0], beside_core)
+        return remote(i, gate_others.at[1], gate_others.at[2], beside_core)
+
+    rounds = [beside_core, beside_x, beside_y, (hop_one * slabs + here, core), (hop_two * slabs + here, core)]
+
+    def tally(k):
+        return remote(base + 15 + k, tally_ref.at[2 * k], tally_ref.at[2 * k + 1], rounds[k])
+
+    def tally_step(k):
+        tally(k).wait_recv()
+        total = tally_ref[2 * k] + tally_ref[2 * k + 1]
+        if k + 1 < len(rounds):
+            tally_ref[2 * k + 2] = total
+            tally(k + 1).start()
+        else:
+            loads_ref[...] = total
+
+    number = lax.broadcasted_iota(jnp.int32, (8, count), 0)
+    picks = jnp.where(number == route_row_ref[...], 1.0, 0.0)
+    chunk = 128
+    for s in range(0, count, chunk):
+        row = lax.broadcasted_iota(jnp.int32, (chunk, count), 0) + s
+        column = lax.broadcasted_iota(jnp.int32, (chunk, count), 1)
+        order_ref[s : s + chunk, :] = jnp.where(row < column, 1.0, 0.0).astype(jnp.bfloat16)
+    ranks = jnp.dot(picks.astype(jnp.bfloat16), order_ref[0:count, :], preferred_element_type=jnp.float32)
+    counts = jnp.sum(picks, axis=1, keepdims=True)
+    padded = jnp.ceil(counts * (1.0 / ALIGN)) * ALIGN
+    place = jnp.zeros((1, count), jnp.float32)
+    start = jnp.zeros((1, 1), jnp.float32)
+    for e in range(experts):
+        place = place + picks[e : e + 1, :] * (ranks[e : e + 1, :] + start)
+        start = start + padded[e : e + 1, :]
+    place_ref[...] = jnp.broadcast_to(place, (8, count))
+    tally_ref[0] = jnp.broadcast_to(counts, (8, 128))
+    tally(0).start()
+    for s in range(0, rows, 64):
+        row = lax.broadcasted_iota(jnp.int32, (64, count), 0) + s
+        order_ref[s : s + 64, :] = jnp.where(row.astype(jnp.float32) == place, 1.0, 0.0).astype(jnp.bfloat16)
+
+    def sort_rows(source_ref, to_ref, which):
+        for piece in range(2):
+            at = slice(piece * half_rows, (piece + 1) * half_rows)
+            to_ref[at, :] = jnp.dot(
+                order_ref[at, :], source_ref[...], preferred_element_type=jnp.float32
+            ).astype(jnp.bfloat16)
+            row_copy(which, 0, piece).start()
+            row_copy(which, 1, piece).start()
+
+    sort_rows(cot_ref, cot_own, 0)
+
+    def project(i, _):
+        at = pl.ds(pl.multiple_of(i * 192, 192), 192)
+        entry, _, _ = row_norm(tokens_ref[at, :].astype(jnp.float32), gains_ref[...], shifts_ref[...])
+        entry = entry.astype(jnp.bfloat16)
+        entry_ref[at, :] = entry
+        joint_ref[at, :] = jnp.dot(entry, projection_ref[...], preferred_element_type=jnp.float32).astype(jnp.bfloat16)
+        return 0
+
+    lax.fori_loop(0, count // 192, project, 0)
+    score_bias(bias_ref, lengths_ref, count)
+    forward_weights(0, 1)
+    tally_step(0)
+
+    first = lax.broadcasted_iota(jnp.int32, (1, 128), 1) < 64
+
+    def attend(p, _):
+        lanes = pl.ds(pl.multiple_of(p * 128, 128), 128)
+        keys = pl.ds(pl.multiple_of(width + p * 128, 128), 128)
+        values = pl.ds(pl.multiple_of(2 * width + p * 128, 128), 128)
+        for s, e in query_blocks(count):
+            outs = []
+            for half in range(2):
+                q = jnp.where(first == (half == 0), joint_ref[s:e, lanes], jnp.bfloat16(0))
+                scores = lax.dot_general(joint_ref[0:e, keys], q, NT, preferred_element_type=jnp.float32)
+                scores = scores * factor + bias_ref[0:e, s:e]
+                peak = jnp.max(scores, axis=0, keepdims=True)
+                weights = jnp.exp2(scores - peak)
+                total = jnp.sum(weights, axis=0, keepdims=True)
+                probs = (weights * (1.0 / total)).astype(jnp.bfloat16)
+                outs.append(
+                    lax.dot_general(probs, joint_ref[0:e, values], TN, preferred_element_type=jnp.float32)
+                )
+                logs_ref[p, half : half + 1, s:e] = peak + jnp.log2(total)
+            mixed_ref[s:e, lanes] = jnp.where(first, outs[0], outs[1]).astype(jnp.bfloat16)
+
+        @pl.when(p == 1)
+        def _():
+            forward_weights(1, 1)
+            tally_step(1)
+
+        @pl.when(p == 3)
+        def _():
+            forward_weights(0, 2)
+            tally_step(2)
+
+        @pl.when(p == 5)
+        def _():
+            for piece in range(2):
+                row_copy(0, 0, piece).wait_recv()
+                row_copy(0, 2, piece).start()
+            forward_weights(1, 2)
+            tally_step(3)
+
+        return 0
+
+    lax.fori_loop(0, pairs, attend, 0)
+
+    lane = lax.broadcasted_iota(jnp.int32, (1, 128), 1)
+
+    def mix(i, _):
+        at = pl.ds(pl.multiple_of(i * 192, 192), 192)
+        residual = tokens_ref[at, :].astype(jnp.float32) + jnp.dot(
+            mixed_ref[at, :], mixing_ref[...], preferred_element_type=jnp.float32
+        )
+        residual_ref[at, :] = residual
+        normed, _, _ = row_norm(residual, factors_ref[...], biases_ref[...])
+        chosen = chosen_rows(route_ref[at, :], centroids_ref, experts)
+        gate = 1.0 / (1.0 + jnp.exp(-jnp.sum(normed * chosen, axis=1, keepdims=True)))
+        high = gate.astype(jnp.bfloat16).astype(jnp.float32)
+        mid = (gate - high).astype(jnp.bfloat16).astype(jnp.float32)
+        low = gate - high - mid
+        parts = jnp.where(lane == 0, high, jnp.where(lane == 1, mid, jnp.where(lane == 2, low, 0.0)))
+        normed_ref[at, 0:width] = normed.astype(jnp.bfloat16)
+        normed_ref[at, width : width + 128] = parts.astype(jnp.bfloat16)
+        return 0
+
+    lax.fori_loop(0, count // 192, mix, 0)
+    for piece in range(2):
+        at = slice(piece * half_rows, (piece + 1) * half_rows)
+        moved = jnp.dot(order_ref[at, :], normed_ref[...], preferred_element_type=jnp.float32)
+        sent_own[at, :] = moved[:, 0:width].astype(jnp.bfloat16)
+        row_copy(1, 0, piece).start()
+        row_copy(1, 1, piece).start()
+        bias_ref[at, 0:128] = jnp.broadcast_to(
+            jnp.sum(moved[:, width : width + 128], axis=1, keepdims=True), (half_rows, 128)
+        )
+    gates = jnp.transpose(bias_ref[0:rows, 0:128])
+    gate_own[0:1, :] = gates[0:1, :]
+    gate_own[1:2, :] = jnp.zeros((1, rows), jnp.float32)
+    for e in range(8):
+        gate_own[1:2, e : e + 1] = padded[e : e + 1, :]
+    gate_copy(0).start()
+    gate_copy(1).start()
+
+    for kind in range(2):
+        forward_weights(kind, 3)
+    gate_copy(0).wait_recv()
+    gate_copy(2).start()
+    tally_step(4)
+    for piece in range(2):
+        row_copy(1, 0, piece).wait_recv()
+        row_copy(1, 2, piece).start()
+
+    for which in range(2):
+        for part in range(3):
+            for piece in range(2):
+                copy = row_copy(which, part, piece)
+                copy.wait_send()
+                if part:
+                    copy.wait_recv()
+    for part in range(3):
+        gate_copy(part).wait_send()
+        if part:
+            gate_copy(part).wait_recv()
+    for k in range(len(rounds)):
+        tally(k).wait_send()
+    for kind in range(2):
+        own_weights(kind).wait()
+        for r in range(1, planes):
+            for sign in (1, -1):
+                @pl.when(hop_sent(sign, r))
+                def _(kind=kind, sign=sign, r=r):
+                    hop(kind, sign, r).wait_send()
+        for slot in range(2 * planes - 1):
+            @pl.when(held(slot))
+            def _(kind=kind, slot=slot):
+                aside(kind, slot).wait()
+
+
+def front_stage(
+    tokens, gains, shifts, projection, mixing, factors, biases, centroids, expanding, contracting, route, lengths, cotangent, planes, slabs
+):
+    count, width = tokens.shape
+    rows = aligned_rows(count, planes)
+    pairs = width // 128
+    slots = 2 * planes - 1
+    bf16, f32 = jnp.bfloat16, jnp.float32
+    shape = jax.ShapeDtypeStruct
+    anywhere = pl.BlockSpec(memory_space=pl.ANY)
+    local = pl.BlockSpec(memory_space=pltpu.VMEM)
+    dma = pltpu.SemaphoreType.DMA
+    copies = 2 * (2 * (planes - 1) + slots) + 12 + 3 + 5
+    outs = [
+        (shape((count, width), bf16), local),
+        (shape((count, 3 * width), bf16), local),
+        (shape((count, width), bf16), local),
+        (shape((pairs, 2, count), f32), local),
+        (shape((count, width), f32), local),
+        (shape((8, count), f32), local),
+        (shape((8, 128), f32), local),
+        (shape((rows, width), bf16), local),
+        (shape((rows, width), bf16), local),
+        (shape((8, rows), f32), local),
+        (shape((3, rows, width), bf16), anywhere),
+        (shape((3, rows, width), bf16), anywhere),
+        (shape((3, 8, rows), f32), anywhere),
+        (shape((slots,) + expanding.shape[1:], bf16), anywhere),
+        (shape((slots,) + expanding.shape[1:], bf16), anywhere),
+        (shape((slots,) + contracting.shape[1:], bf16), anywhere),
+        (shape((slots,) + contracting.shape[1:], bf16), anywhere),
+    ]
+    row = lambda v: v.reshape(1, -1)
+    return pl.pallas_call(
+        partial(front_kernel, planes, slabs),
+        out_shape=[o[0] for o in outs],
+        in_specs=[pl.BlockSpec(memory_space=pltpu.SMEM)] + [local] * 11 + [anywhere] * 2,
+        out_specs=[o[1] for o in outs],
+        scratch_shapes=[
+            pltpu.VMEM((rows, count), f32),
+            pltpu.VMEM((rows, count), bf16),
+            pltpu.VMEM((count, width + 128), bf16),
+            pltpu.VMEM((10, 8, 128), f32),
+            dma((copies,)),
+            dma((copies,)),
+            dma((2,)),
+        ],
+        compiler_params=pltpu.CompilerParams(
+            collective_id=0, has_side_effects=True, vmem_limit_bytes=VMEM_LIMIT
+        ),
+    )(
+        lengths[0],
+        tokens,
+        row(gains),
+        row(shifts),
+        projection,
+        mixing,
+        row(factors),
+        row(biases),
+        jnp.pad(centroids, ((0, -centroids.shape[0] % 8), (0, 0))),
+        row(route),
+        route,
+        cotangent,
+        expanding,
+        contracting,
+    )
+
+
 TILE = 256
 ALIGN = 16
 
@@ -461,11 +824,12 @@
     meta_ref,
     *refs,
 ):
-    sent_refs, refs = refs[:sources], refs[sources:]
-    cot_refs, refs = refs[:sources], refs[sources:]
-    gate_refs, refs = refs[:sources], refs[sources:]
-    near_refs, refs = refs[: 2 * experts - 1], refs[2 * experts - 1 :]
-    far_refs, refs = refs[: 2 * experts - 1], refs[2 * experts - 1 :]
+    sent_own, sent_others, cot_own, cot_others, gate_own, gate_others = refs[:6]
+    up_near, up_far, down_near, down_far = refs[6:10]
+    refs = refs[10:]
+    sent_refs = [sent_own] + [sent_others.at[s] for s in range(sources - 1)]
+    cot_refs = [cot_own] + [cot_others.at[s] for s in range(sources - 1)]
+    gate_refs = [gate_own] + [gate_others.at[s] for s in range(sources - 1)]
     back_outs, refs = refs[:sources], refs[sources:]
     made_outs, refs = refs[:sources], refs[sources:]
     dot_outs, refs = refs[:sources], refs[sources:]
@@ -525,21 +889,11 @@
                 act(pltpu.make_async_copy(c_ref.at[dst], back_outs[s].at[src], out_sem.at[1, k, i]))
 
     def move_weights(e, act):
-        step = e - own
-        for k in range(2 * experts - 1):
-            @pl.when(step == k - (experts - 1))
-            def _(k=k):
-                for j, ref in enumerate((near_refs[k], far_refs[k])):
-                    lanes = pl.ds(j * half, half)
-                    act(pltpu.make_async_copy(ref.at[pl.ds(0, width)], up_ref.at[e, :, lanes], weight_sem.at[e, j, 0]))
-                    for part in range(2):
-                        act(
-                            pltpu.make_async_copy(
-                                ref.at[pl.ds(width + part * half, half)],
-                                down_ref.at[e, lanes, pl.ds(part * half, half)],
-                                weight_sem.at[e, j, 1 + part],
-                            )
-                        )
+        slot = e - own + experts - 1
+        for j, (ups, downs) in enumerate(((up_near, down_near), (up_far, down_far))):
+            part = pl.ds(j * half, half)
+            act(pltpu.make_async_copy(ups.at[slot], up_ref.at[e, :, part], weight_sem.at[e, j, 0]))
+            act(pltpu.make_async_copy(downs.at[slot], down_ref.at[e, part], weight_sem.at[e, j, 1]))
 
     zero_ref[...] = jnp.zeros_like(zero_ref)
     for e in range(experts):
@@ -649,10 +1003,10 @@
             copy.wait()
 
 
-def expert_stage(meta, sent, cot, gates, near, far, experts, limit):
-    sources = len(sent)
+def expert_stage(meta, sent, cot, gates, weights, experts, limit):
     rows, width = sent[0].shape
-    half = near[0].shape[1]
+    sources = 1 + sent[1].shape[0]
+    half = weights[0].shape[2]
     hidden = 2 * half
     joined = -(-(sources * rows + experts * (TILE - 1)) // TILE) * TILE
     limit = -(-limit // ALIGN) * ALIGN
@@ -661,17 +1015,18 @@
     local = pl.BlockSpec(memory_space=pltpu.VMEM)
     slots = 2 * experts - 1
     dma = pltpu.SemaphoreType.DMA
+    packed = (width + hidden, half)
     outs = pl.pallas_call(
         partial(expert_kernel_body, experts, sources, rows, limit, width, hidden),
         out_shape=(
             [jax.ShapeDtypeStruct((rows, width), jnp.bfloat16)] * (2 * sources)
             + [jax.ShapeDtypeStruct((8, rows), jnp.float32)] * sources
-            + [jax.ShapeDtypeStruct((slots,) + near[0].shape, jnp.bfloat16)] * 2
+            + [jax.ShapeDtypeStruct((slots,) + packed, jnp.bfloat16)] * 2
         ),
         in_specs=[pl.BlockSpec(memory_space=pltpu.SMEM)]
-        + [anywhere] * (2 * sources)
-        + [local] * sources
-        + [anywhere] * (2 * slots),
+        + [anywhere] * 4
+        + [local] * 2
+        + [anywhere] * 4,
         out_specs=[anywhere] * (2 * sources) + [local] * sources + [anywhere] * 2,
         scratch_shapes=[
             pltpu.VMEM((joined, width), jnp.bfloat16),
@@ -682,9 +1037,9 @@
             pltpu.VMEM((experts, hidden, width), jnp.bfloat16),
             pltpu.VMEM((width, hidden), jnp.float32),
             pltpu.VMEM((hidden, width), jnp.float32),
-            pltpu.VMEM((2, 2) + near[0].shape, jnp.bfloat16),
+            pltpu.VMEM((2, 2) + packed, jnp.bfloat16),
             pltpu.VMEM((ALIGN, width), jnp.bfloat16),
-            dma((experts, 2, 3)),
+            dma((experts, 2, 2)),
             dma((2, sources * experts, pieces)),
             dma((2, sources * experts, pieces)),
             dma((2, 2)),
@@ -694,7 +1049,7 @@
         cost_estimate=pl.CostEstimate(
             flops=12 * sources * rows * width * hidden, bytes_accessed=100_000_000, transcendentals=sources * rows * hidden
         ),
-    )(meta, *sent, *cot, *gates, *near, *far)
+    )(meta, *sent, *cot, *gates, *weights)
     back, made, dots = outs[:sources], outs[sources : 2 * sources], outs[2 * sources : 3 * sources]
     return back, made, dots, outs[-2], outs[-1]
 
@@ -706,21 +1061,6 @@
 
 def across(value):
     return lax.ppermute(value, "tensor", [(0, 1), (1, 0)])
-
-
-def spread_out(value):
-    other = swap(value, 2)
-    return [value, across(value), other, across(other)]
-
-
-def line(value, step, planes, slabs, least):
-    pairs = []
-    for i in range(planes * slabs):
-        plane = i // slabs
-        source = plane if step > 0 else planes - 1 - plane
-        if source >= least and 0 <= plane + step < planes:
-            pairs.append((i, i + step * slabs))
-    return lax.ppermute(value, "expert", pairs)
 
 
 def beside(value, planes, slabs, shift):
@@ -728,21 +1068,6 @@
         (i, i ^ 1) for i in range(planes * slabs) if 0 <= i // slabs + shift < planes
     ]
     return lax.ppermute(value, "expert", pairs)
-
-
-def gather_weights(packed, planes, slabs):
-    near = [None] * (2 * planes - 1)
-    near[planes - 1] = packed
-    for k in range(1, planes):
-        near[planes - 1 - k] = line(near[planes - k], 1, planes, slabs, k - 1)
-        near[planes - 1 + k] = line(near[planes - 2 + k], -1, planes, slabs, k - 1)
-    far = [None] * (2 * planes - 1)
-    for k in range(planes):
-        for sign in (1, -1):
-            if k or sign > 0:
-                at = planes - 1 + sign * k
-                far[at] = beside(near[at], planes, slabs, sign * k)
-    return near, far
 
 
 def reduce_weights(near, far, planes, slabs):
@@ -796,53 +1121,26 @@
     rows = aligned_rows(count, experts)
     me, core = lax.axis_index("expert"), lax.axis_index("tensor")
 
-    packed = jnp.concatenate(
-        (expanding[0], contracting[0, :, :half], contracting[0, :, half:]), axis=0
-    )
-    near, far = gather_weights(packed, experts, slabs)
-
     route = routes[:, 0]
-    picks = route[:, None] == jnp.arange(experts, dtype=jnp.int32)[None, :]
-    picks_int = picks.astype(jnp.int32)
-    counts = jnp.sum(picks_int, axis=0)
-    all_counts = lax.all_gather(counts, ("expert", "tensor"))
-    loads = jnp.sum(all_counts, axis=0).astype(jnp.float32)
-    spread = (loads - average) / average
+    picks = routes == jnp.arange(experts, dtype=jnp.int32)[None, :]
+    entry, joint, mixed_rows, logs, residual, place, loads, sent_own, cot_own, gate_own, sent_others, cot_others, gate_others, *weights = front_stage(
+        tokens, gains, shifts, projection, mixing, factors, biases, centroids, expanding, contracting, routes, lengths, cotangent, experts, slabs
+    )
+    spread = (loads[:experts, 0] - average) / average
     token_spread = jnp.sum(jnp.where(picks, spread[None, :], 0.0), axis=1)
-    sizes = (all_counts + (ALIGN - 1)) // ALIGN * ALIGN
-    mine = sizes[me * 2 + core]
-    starts = running(mine) - mine
-    ranks = earlier(picks)
-    position = jnp.sum((ranks + starts[None, :]) * picks_int, axis=1)
-    order = (jnp.arange(rows, dtype=jnp.int32)[:, None] == position[None, :]).astype(jnp.bfloat16)
+    position = place[0].astype(jnp.int32)
+    sizes = jnp.concatenate((gate_own[1:2, :experts], gate_others[:, 1, :experts]), axis=0)
+    meta = jnp.concatenate(
+        [(me // slabs).astype(jnp.int32)[None], sizes.reshape(-1).astype(jnp.int32)]
+    )
     back_order = (position[:, None] == jnp.arange(rows, dtype=jnp.int32)[None, :]).astype(jnp.bfloat16)
-    group = [me * 2 + core, me * 2 + 1 - core, (me ^ 2) * 2 + core, (me ^ 2) * 2 + 1 - core]
-    meta = jnp.concatenate(
-        [(me // slabs).astype(jnp.int32)[None]] + [sizes[g] for g in group]
-    )
-    sorted_cot = jnp.dot(order, cotangent, preferred_element_type=jnp.float32).astype(jnp.bfloat16)
-    group_cot = spread_out(sorted_cot)
-
     inputs = tokens.astype(jnp.float32)
-    entry, entry_normal, entry_scale = norm_parts(inputs, gains, shifts)
-    entry = entry.astype(jnp.bfloat16)
-    joint = jnp.dot(entry, projection, preferred_element_type=jnp.float32).astype(jnp.bfloat16)
-    mixed_rows, logs = attend_forward(joint, lengths[0])
-    residual = inputs + jnp.dot(mixed_rows, mixing, preferred_element_type=jnp.float32)
+    _, entry_normal, entry_scale = norm_parts(inputs, gains, shifts)
     normed, mixer_normal, mixer_scale = norm_parts(residual, factors, biases)
     chosen = jnp.dot(picks.astype(jnp.bfloat16), centroids, preferred_element_type=jnp.float32)
     gates = jax.nn.sigmoid(jnp.sum(normed * chosen, axis=1))
-    sorted_sent = jnp.dot(
-        order, normed.astype(jnp.bfloat16), preferred_element_type=jnp.float32
-    ).astype(jnp.bfloat16)
-    sorted_gates = jnp.sum(
-        jnp.where(position[:, None] == jnp.arange(rows, dtype=jnp.int32)[None, :], gates[:, None], 0.0),
-        axis=0,
-    )
-    group_gates = spread_out(jnp.broadcast_to(sorted_gates[None, :], (8, rows)))
-    group_sent = spread_out(sorted_sent)
     back, made, dots, near_grads, far_grads = expert_stage(
-        meta, group_sent, group_cot, group_gates, near, far, experts, limit
+        meta, (sent_own, sent_others), (cot_own, cot_others), (gate_own, gate_others), weights, experts, limit
     )
 
     def collect(parts, narrow):

time: 763 us -> 650 us (0.85)
  waiting for transfers between devices: 290 us -> 153 us
  Pallas kernels: 131 us -> 244 us
  starting transfers between devices: 65 us -> 34.9 us
  matrix products: 68.7 us -> 50.1 us
  local copies, waits for them, and re-layouts: 46.6 us -> 29.4 us
  blocking collectives: 83 us -> 68.6 us
  other arithmetic: 54.3 us -> 44.8 us
    pallas_call x1, Pallas kernels: 28.7 us -> 140 us  [front_stage(): pl.pallas_call(partial(front_kernel, planes, slabs), out_shape=[o[0] for...]
    ppermute x14 -> x7, waiting for transfers between devices: 120 us -> 27.1 us  [beside(): return lax.ppermute(value, 'expert', pairs)]
    ppermute x6 -> x3, waiting for transfers between devices: 56.8 us -> 4.2 us  [swap(): return lax.ppermute(value, 'expert', [(i, i ^ bit) for i in range(groups)])]
    unnamed x1 -> x0, blocking collectives: 42 us -> none
    psum x1, blocking collectives: 41 us -> 68.6 us  [per_device(): lax.psum((gain_grad, shift_grad, projection_grad, mixing_grad, factor_gra...]
    ppermute x6 -> x0, waiting for transfers between devices: 21.3 us -> none  [line(): return lax.ppermute(value, 'expert', pairs)]
    dot_general x5 -> x0, matrix products: 18.3 us -> none  [the longest x1 7.04 us: per_device(): jnp.dot(entry, projection, preferred_element_type=jnp.float32)]
    unnamed x142 -> x84, local copies, waits for them, and re-layouts: 31.5 us -> 14.5 us
  transfers between devices with their start and end apart: 45 -> 23, of which waited for: 17 -> 9; matrix products, arithmetic and copies ran while one was open for 16% -> 16% of each run, Pallas kernels for 4% -> 5%
where the time goes in v2:
time: 650 us; the launch traced here: 641 us
  Pallas kernels  244 us (38%)
  waiting for transfers between devices  153 us (24%)
  blocking collectives  68.6 us (11%)
  matrix products  50.1 us (8%)
  other arithmetic  44.8 us (7%)
  starting transfers between devices  34.9 us (5%)
  local copies, waits for them, and re-layouts  29.4 us (5%)
  between operations  15.4 us (2%)
    pallas_call x1, Pallas kernels, front_stage(): pl.pallas_call(partial(front_kernel, planes, slabs), out_shape=[o[0] for...  140 us
    psum x1, waiting for transfers between devices, per_device(): lax.psum((gain_grad, shift_grad, projection_grad, mixing_grad, factor_gra...  81.4 us
    pallas_call x1, Pallas kernels, expert_stage(): pl.pallas_call(partial(expert_kernel_body, experts, sources, rows, limit,...  72.8 us
    psum x1, blocking collectives, per_device(): lax.psum((gain_grad, shift_grad, projection_grad, mixing_grad, factor_gra...  68.6 us
    ppermute x6, waiting for transfers between devices, reduce_weights(): came = lax.ppermute(total.astype(jnp.bfloat16), 'expert', pairs)  40.8 us
    pallas_call x1, Pallas kernels, attend_backward(): pl.pallas_call(kernel, out_shape=(jax.ShapeDtypeStruct((count, width), jn...  31.6 us
    ppermute x7, waiting for transfers between devices, beside(): return lax.ppermute(value, 'expert', pairs)  27.1 us
    convert_element_type x5, other arithmetic, reduce_weights(): came = lax.ppermute(total.astype(jnp.bfloat16), 'expert', pairs)  17 us
  transfers between devices with their start and end apart: 23, of which 9 were waited for; matrix products, arithmetic and copies ran while one was open for 16% of the time, Pallas kernels for 5%

profile of v2, /device:TPU:0, one launch (start us, length us, event | category | flops | bytes accessed | tf_op | source)
XLA Modules:
  0.0 641.0 jit_solution(15621492555578132796)
XLA Ops:
  12.3 1.8 copy.31.route_ref
  15.4 139.9 %shard_map.220 = (bf16[1152,768]{1,0:T(8,128)(2,1)}, bf16[1152,2304]{1,0:T(8,128)(2,1)}, bf16[1152,768]{1,0:T(8,128)(2,1)}, f32[6,2,1152]{2,1,0:T(2,128)}, f32[1...) custom-call(s32[4]{0:T(128)} %bitcast.56, ...), custom_call_target="tpu_custom_call" | custom-call | tf_op jit(solution)/shard_map/pallas_call | solution.py:762
  157.4 72.8 %shard_map.221 = (bf16[1216,768]{1,0:T(8,128)(2,1)}, bf16[1216,768]{1,0:T(8,128)(2,1)}, bf16[1216,768]{1,0:T(8,128)(2,1)}, bf16[1216,768]{1,0:T(8,128)(2,1)}, bf...) custom-call(s32[17]{0:T(128)} %pad_add_fusion.meta_ref, ...), custom_call_target="tpu_custom_call" | custom-call | flops 34426847232 | bytes 100000000 | tf_op jit(solution)/shard_map/pallas_call | solution.py:1019
  231.2 5.7 slice_bitcast_fusion.7
  237.0 2.8 collective-permute-start.12
  239.8 3.3 collective-permute-start.11
  243.7 1.8 convert_reduce_fusion
  245.5 2.1 fusion.19
  250.6 3.1 multiply_reduce_fusion.2
  253.7 14.6 %collective-permute-done.12 = bf16[1536,384]{1,0:T(8,128)(2,1)} collective-permute-done((bf16[1536,384]{1,0:T(8,128)(2,1)}, bf16[1536,384]{1,0:T(8,128)(2,1)}, u32[]{:S(2)}, u32[]{:S(2)}) %collective-permute-start.12) | collective-permute-done | bytes 1179680 | tf_op jit(solution)/shard_map/ppermute | solution.py:1070
  268.3 1.9 fusion.32
  273.9 2.6 collective-permute-done.8
  276.5 1.8 collective-permute-start.18
  279.8 2.7 collective-permute-start.10
  282.5 3.3 add_convert_fusion
  285.8 7.7 %collective-permute-done.11 = bf16[1536,384]{1,0:T(8,128)(2,1)} collective-permute-done((bf16[1536,384]{1,0:T(8,128)(2,1)}, bf16[1536,384]{1,0:T(8,128)(2,1)}, u32[]{:S(2)}, u32[]{:S(2)}) %collective-permute-start.11) | collective-permute-done | bytes 1179680 | tf_op jit(solution)/shard_map/ppermute | solution.py:1070
  295.5 3.1 fusion.34
  298.6 5.4 collective-permute-start.14
  305.9 3.5 fusion.20
  309.4 3.3 add_convert_fusion.2
  313.2 4.8 collective-permute-done.10
  318.6 7.9 %collective-permute-done.14 = bf16[1536,384]{1,0:T(8,128)(2,1)} collective-permute-done((bf16[1536,384]{1,0:T(8,128)(2,1)}, bf16[1536,384]{1,0:T(8,128)(2,1)}, u32[]{:S(2)}, u32[]{:S(2)}) %collective-permute-start.14) | collective-permute-done | bytes 1179680 | tf_op jit(solution)/shard_map/ppermute | solution.py:1093
  326.6 1.8 collective-permute-start.17
  328.4 4.9 fusion.36
  333.3 1.6 collective-permute-done.5
  335.6 4.4 fusion
  340.0 1.7 collective-permute-start.19
  341.8 4.8 multiply_reduce_fusion
  346.6 1.8 multiply_add_fusion
  348.4 2.8 convolution_convert_fusion.u_ref
  351.3 31.6 %shard_map.222 = (bf16[1152,768]{1,0:T(8,128)(2,1)}, bf16[1152,768]{1,0:T(8,128)(2,1)}, bf16[1152,768]{1,0:T(8,128)(2,1)}) custom-call(s32[4]{0:T(128)} %bitcast.57, bf16[1152,2304]{1,0:T(8,128)(2,1)} %get-tuple-element.71.q_ref.k_ref.v_ref, bf16[1152,2304]{1,0:T(8,128)(2,1)} %get-tuple-element.71.q_ref.k_ref.v_ref, ...), custom_call_target="tpu_custom_call" | custom-call | flops 10192158720 | bytes 14155776 | tf_op jit(solution)/shard_map/pallas_call | solution.py:340
  382.9 1.7 constant_dynamic-update-slice_fusion.2
  387.7 7.6 %fusion.18 = (f32[768]{0:T(1024)}, f32[1152]{0:T(1024)}, f32[1152]{0:T(1024)}, f32[768]{0:T(1024)}, f32[1152,768]{1,0:T(8,128)}) fusion(bf16[1152,768]{1,0:T(8,128)(2,1)S(1)} %copy-done.1, f32[1152]{0:T(1024)S(1)} %copy-done.26, f32[1152]{0:T(1024)S(1)} %broadcast_multiply_fusion.1, f32[768]{0:T(1024)S(1)} %copy-done.30, ...), kind=kOutput, calls=%fused_computation.26 | convolution fusion | flops 4085707008 | bytes 14183424 | tf_op jit(solution)/shard_map/te,de->td/dot_general | solution.py:1187
  395.3 7.2 %fusion.52 = f32[768,2304]{1,0:T(8,128)} fusion(bf16[1152,768]{1,0:T(8,128)(2,1)S(1)} %copy-done.37, bf16[1152,2304]{1,0:T(8,128)(2,1)S(1)} %constant_dynamic-update-slice_fusion), kind=kOutput, calls=%fused_computation.109 | convolution fusion | flops 4076863488 | bytes 14155776 | tf_op jit(solution)/shard_map/td,te->de/dot_general | solution.py:1186
  402.5 3.2 fusion.44
  405.7 1.7 collective-permute-start.16
  407.3 5.4 collective-permute-start.15
  412.7 4.5 fusion.29
  417.2 1.7 collective-permute-start.20
  418.9 6.1 fusion.2
  425.0 68.6 %all-reduce.1 = (f32[]{:T(128)}, f32[768]{0:T(1024)}, f32[768]{0:T(1024)}, f32[768]{0:T(1024)}, f32[768]{0:T(1024)}, /*index=5*/f32[4,768]{1,0:T(4,128)}) all-reduce(f32[]{:T(128)S(6)} %div.64, f32[768]{0:T(1024)} %get-tuple-element.82, f32[768]{0:T(1024)} %get-tuple-element.87, ...), channel_id=1, replica_groups=mesh['expert'=16,'tensor'=2] {'expert','tensor'}, use_global_device_ids=true, to_apply=%region_5.6 | all-reduce | flops 6145 | bytes 49160 | tf_op jit(solution)/shard_map/psum | solution.py:1191
  494.4 7.4 %fusion.22 = bf16[1152,768]{1,0:T(8,128)(2,1)} fusion(f32[1152,768]{1,0:T(8,128)S(1)} %copy-done, f32[1152,768]{1,0:T(8,128)} %fusion.2, s32[1152]{0:T(1024)S(1)} %copy-done.25, bf16[1216,768]{1,0:T(8,128)(2,1)} %collective-permute-done, bf16[1216,768]{1,0:T(8,128)(2,1)} %get-tuple-element.58, f32[1152]{0:T(1024)} %get-tuple-element.109), kind=kOutput, calls=%fused_computation.36 | convolution fusion | flops 2160353280 | bytes 12592128 | tf_op jit(solution)/shard_map/dot_general | solution.py:1153
  501.8 2.6 fusion.31
  505.8 2.6 fusion.17
  508.4 31.4 %collective-permute-done.21 = bf16[1536,384]{1,0:T(8,128)(2,1)S(1)} collective-permute-done((bf16[1536,384]{1,0:T(8,128)(2,1)S(1)}, bf16[1536,384]{1,0:T(8,128)(2,1)S(1)}, u32[]{:S(2)}, u32[]{:S(2)}) %collective-permute-start.21) | collective-permute-done | bytes 1179680 | tf_op jit(solution)/shard_map/ppermute | solution.py:1093
  539.8 2.5 fusion.38
  544.6 81.4 %all-reduce.5.cloned.1.call-done = (f32[768,2304]{1,0:T(8,128)}, f32[768,768]{1,0:T(8,128)}) async-done(((f32[768,2304]{1,0:T(8,128)}, f32[768,768]{1,0:T(8,128)}), (f32[768,2304]{1,0:T(8,128)}, f32[768,768]{1,0:T(8,128)})) %all-reduce.5.cloned.1.call-update) | async-done | bytes 9437200 | tf_op jit(solution)/shard_map/psum | solution.py:1191
  626.0 6.6 %copy.42 = f32[768,2304]{1,0:T(8,128)} copy(f32[768,2304]{1,0:T(8,128)} %get-tuple-element.121) | data formatting | bytes 14155776
  (141 shorter events, 32.0 us)
Async XLA Ops:
  7.2 618.8 %all-reduce.5.cloned.1.call-start = ((), (), s32[]{:S(2)}) async-start(), calls=%async_computation | async-start | bytes 18874368 | tf_op jit(solution)/shard_map/psum | solution.py:1191
  230.2 43.6 %collective-permute-start.6 = (f32[8,1216]{1,0:T(8,128)}, f32[8,1216]{1,0:T(8,128)}, u32[]{:S(2)}, u32[]{:S(2)}) collective-permute-start(f32[8,1216]{1,0:T(8,128)} %get-tuple-element.68), channel_id=1, source_target_pairs={{0,1},{1,0},{2,3},{3,2},{4,5},{5,4},{6,7},{7,6},{8,9},{9,8},{10,11... | collective-permute-start | bytes 116744 | tf_op jit(solution)/shard_map/ppermute | solution.py:1063
  230.7 41.0 %collective-permute-start.7 = (f32[8,1216]{1,0:T(8,128)}, f32[8,1216]{1,0:T(8,128)}, u32[]{:S(2)}, u32[]{:S(2)}) collective-permute-start(f32[8,1216]{1,0:T(8,128)} %get-tuple-element.70), channel_id=1, source_target_pairs={{0,1},{1,0},{2,3},{3,2},{4,5},{5,4},{6,7},{7,6},{8,9},{9,8},{10,11... | collective-permute-start | bytes 116744 | tf_op jit(solution)/shard_map/ppermute | solution.py:1063
  230.8 49.0 %collective-permute-start.4 = (bf16[1216,768]{1,0:T(8,128)(2,1)}, bf16[1216,768]{1,0:T(8,128)(2,1)}, u32[]{:S(2)}, u32[]{:S(2)}) collective-permute-start(bf16[1216,768]{1,0:T(8,128)(2,1)} %get-tuple-element.66), channel_id=1, source_target_pairs={{0,1},{1,0},{2,3},{3,2},{4,5},{5,4},{6,7},{7,6},{8,9},{9,8},{10,11... | collective-permute-start | bytes 5603336 | tf_op jit(solution)/shard_map/ppermute | solution.py:1063
  231.2 11.9 %copy-start.19 = (s32[1152,1]{0,1:T(1,128)S(1)}, s32[1152,1]{0,1:T(1,128)}, u32[]{:S(2)}) copy-start(s32[1152,1]{0,1:T(1,128)} %param.23) | copy-start | bytes 13828
  237.0 11.3 %copy-start = (f32[1152,768]{1,0:T(8,128)S(1)}, f32[1152,768]{1,0:T(8,128)}, u32[]{:S(2)}) copy-start(f32[1152,768]{1,0:T(8,128)} %get-tuple-element.46) | copy-start | bytes 10616836
  237.0 31.3 %collective-permute-start.12 = (bf16[1536,384]{1,0:T(8,128)(2,1)}, bf16[1536,384]{1,0:T(8,128)(2,1)}, u32[]{:S(2)}, u32[]{:S(2)}) collective-permute-start(bf16[1536,384]{1,0:T(8,128)(2,1)} %get-tuple-element.100), channel_id=1, source_target_pairs={{0,2},{2,0},{4,6},{6,4},{1,3},{3,1},{5,7},{7,5}} | collective-permute-start | bytes 3538952 | tf_op jit(solution)/shard_map/ppermute | solution.py:1070
  239.8 53.8 %collective-permute-start.11 = (bf16[1536,384]{1,0:T(8,128)(2,1)}, bf16[1536,384]{1,0:T(8,128)(2,1)}, u32[]{:S(2)}, u32[]{:S(2)}) collective-permute-start(bf16[1536,384]{1,0:T(8,128)(2,1)} %get-tuple-element.101), channel_id=1, source_target_pairs={{0,2},{2,0},{4,6},{6,4},{8,10},{10,8},{12,14},{14,12},{1,3},{3,1},... | collective-permute-start | bytes 3538952 | tf_op jit(solution)/shard_map/ppermute | solution.py:1070
  253.7 18.0 %copy-start.20 = (f32[8,1216]{1,0:T(8,128)S(1)}, f32[8,1216]{1,0:T(8,128)}, u32[]{:S(2)}) copy-start(f32[8,1216]{1,0:T(8,128)} %get-tuple-element.69) | copy-start | bytes 116740
  253.7 28.8 %copy-start.12 = (bf16[1216,768]{1,0:T(8,128)(2,1)S(1)}, bf16[1216,768]{1,0:T(8,128)(2,1)}, u32[]{:S(2)}) copy-start(bf16[1216,768]{1,0:T(8,128)(2,1)} %get-tuple-element.65) | copy-start | bytes 5603332
  270.2 25.3 %collective-permute-start.13 = (bf16[1536,384]{1,0:T(8,128)(2,1)S(1)}, bf16[1536,384]{1,0:T(8,128)(2,1)S(1)}, u32[]{:S(2)}, u32[]{:S(2)}) collective-permute-start(bf16[1536,384]{1,0:T(8,128)(2,1)S(1)} %fusion.32), channel_id=1, source_target_pairs={{0,8},{2,10},{4,12},{6,14},{1,9},{3,11},{5,13},{7,15}} | collective-permute-start | bytes 3538952 | tf_op jit(solution)/shard_map/ppermute | solution.py:1093
  272.5 4.0 collective-permute-start.8
  273.8 6.0 copy-start.23
  273.8 35.6 %collective-permute-start.1 = (bf16[1216,768]{1,0:T(8,128)(2,1)}, bf16[1216,768]{1,0:T(8,128)(2,1)}, u32[]{:S(2)}, u32[]{:S(2)}) collective-permute-start(bf16[1216,768]{1,0:T(8,128)(2,1)} %get-tuple-element.61), channel_id=1, source_target_pairs={{0,1},{1,0},{2,3},{3,2},{4,5},{5,4},{6,7},{7,6},{8,9},{9,8},{10,11... | collective-permute-start | bytes 5603336 | tf_op jit(solution)/shard_map/ppermute | solution.py:1063
  276.5 36.2 %collective-permute-start.18 = (bf16[1536,384]{1,0:T(8,128)(2,1)}, bf16[1536,384]{1,0:T(8,128)(2,1)}, u32[]{:S(2)}, u32[]{:S(2)}) collective-permute-start(bf16[1536,384]{1,0:T(8,128)(2,1)} %get-tuple-element.97), channel_id=1, source_target_pairs={{24,26},{26,24},{28,30},{30,28},{25,27},{27,25},{29,31},{31,29}} | collective-permute-start | bytes 3538952 | tf_op jit(solution)/shard_map/ppermute | solution.py:1070
  279.8 38.2 %collective-permute-start.10 = (bf16[1536,384]{1,0:T(8,128)(2,1)}, bf16[1536,384]{1,0:T(8,128)(2,1)}, u32[]{:S(2)}, u32[]{:S(2)}) collective-permute-start(bf16[1536,384]{1,0:T(8,128)(2,1)} %get-tuple-element.102), channel_id=1, source_target_pairs={{0,2},{2,0},{4,6},{6,4},{8,10},{10,8},{12,14},{14,12},{16,18},{18,... | collective-permute-start | bytes 3538952 | tf_op jit(solution)/shard_map/ppermute | solution.py:1070
  293.6 41.3 %collective-permute-start.5 = (bf16[1216,768]{1,0:T(8,128)(2,1)}, bf16[1216,768]{1,0:T(8,128)(2,1)}, u32[]{:S(2)}, u32[]{:S(2)}) collective-permute-start(bf16[1216,768]{1,0:T(8,128)(2,1)} %add_convert_fusion), channel_id=1, source_target_pairs={{0,4},{2,6},{4,0},{6,2},{8,12},{10,14},{12,8},{14,10},{16,20},{18,... | collective-permute-start | bytes 5603336 | tf_op jit(solution)/shard_map/ppermute | solution.py:1059
  298.6 27.9 %collective-permute-start.14 = (bf16[1536,384]{1,0:T(8,128)(2,1)}, bf16[1536,384]{1,0:T(8,128)(2,1)}, u32[]{:S(2)}, u32[]{:S(2)}) collective-permute-start(bf16[1536,384]{1,0:T(8,128)(2,1)} %fusion.34), channel_id=1, source_target_pairs={{0,8},{2,10},{4,12},{6,14},{8,16},{10,18},{12,20},{14,22},{1,9},{3... | collective-permute-start | bytes 3538952 | tf_op jit(solution)/shard_map/ppermute | solution.py:1093
  305.9 3.5 copy-start.35
  305.9 3.5 copy-start.11
  309.4 30.6 %collective-permute-start.3 = (bf16[1216,768]{1,0:T(8,128)(2,1)S(1)}, bf16[1216,768]{1,0:T(8,128)(2,1)S(1)}, u32[]{:S(2)}, u32[]{:S(2)}) collective-permute-start(bf16[1216,768]{1,0:T(8,128)(2,1)S(1)} %copy-done.35), channel_id=1, source_target_pairs={{0,1},{1,0},{2,3},{3,2},{4,5},{5,4},{6,7},{7,6},{8,9},{9,8},{10,11... | collective-permute-start | bytes 5603336 | tf_op jit(solution)/shard_map/ppermute | solution.py:1063
  312.7 181.6 %collective-permute-start = (bf16[1216,768]{1,0:T(8,128)(2,1)}, bf16[1216,768]{1,0:T(8,128)(2,1)}, u32[]{:S(2)}, u32[]{:S(2)}) collective-permute-start(bf16[1216,768]{1,0:T(8,128)(2,1)} %get-tuple-element.59), channel_id=1, source_target_pairs={{0,1},{1,0},{2,3},{3,2},{4,5},{5,4},{6,7},{7,6},{8,9},{9,8},{10,11... | collective-permute-start | bytes 5603336 | tf_op jit(solution)/shard_map/ppermute | solution.py:1063
  318.0 190.4 %collective-permute-start.9 = (bf16[1536,384]{1,0:T(8,128)(2,1)}, bf16[1536,384]{1,0:T(8,128)(2,1)}, u32[]{:S(2)}, u32[]{:S(2)}) collective-permute-start(bf16[1536,384]{1,0:T(8,128)(2,1)} %get-tuple-element.96), channel_id=1, source_target_pairs={{0,2},{2,0},{4,6},{6,4},{8,10},{10,8},{12,14},{14,12},{16,18},{18,... | collective-permute-start | bytes 3538952 | tf_op jit(solution)/shard_map/ppermute | solution.py:1070
  326.6 9.1 %copy-start.24 = (s32[1152]{0:T(1024)S(1)}, s32[1152]{0:T(1024)}, u32[]{:S(2)}) copy-start(s32[1152]{0:T(1024)} %copy-done.23) | copy-start | bytes 13828
  326.6 79.1 %collective-permute-start.17 = (bf16[1536,384]{1,0:T(8,128)(2,1)}, bf16[1536,384]{1,0:T(8,128)(2,1)}, u32[]{:S(2)}, u32[]{:S(2)}) collective-permute-start(bf16[1536,384]{1,0:T(8,128)(2,1)} %get-tuple-element.98), channel_id=1, source_target_pairs={{16,18},{18,16},{20,22},{22,20},{24,26},{26,24},{28,30},{30,28},{1... | collective-permute-start | bytes 3538952 | tf_op jit(solution)/shard_map/ppermute | solution.py:1070
  333.3 8.5 %copy-start.7 = (f32[1152,768]{1,0:T(8,128)S(1)}, f32[1152,768]{1,0:T(8,128)}, u32[]{:S(2)}) copy-start(f32[1152,768]{1,0:T(8,128)} %get-tuple-element.111) | copy-start | bytes 10616836
  333.3 8.5 %copy-start.18 = (f32[1152]{0:T(1024)S(1)}, f32[1152]{0:T(1024)}, u32[]{:S(2)}) copy-start(f32[1152]{0:T(1024)} %copy-done.17) | copy-start | bytes 13828
  333.3 8.5 %copy-start.22 = (f32[768]{0:T(1024)S(1)}, f32[768]{0:T(1024)}, u32[]{:S(2)}) copy-start(f32[768]{0:T(1024)} %param.18) | copy-start | bytes 9220
  333.3 8.5 %copy-start.33 = (f32[1152]{0:T(1024)S(1)}, f32[1152]{0:T(1024)}, u32[]{:S(2)}) copy-start(f32[1152]{0:T(1024)} %get-tuple-element.107) | copy-start | bytes 13828
  333.3 8.5 %copy-start.38 = (bf16[1216,768]{1,0:T(8,128)(2,1)S(1)}, bf16[1216,768]{1,0:T(8,128)(2,1)}, u32[]{:S(2)}) copy-start(bf16[1216,768]{1,0:T(8,128)(2,1)} %get-tuple-element.63) | copy-start | bytes 5603332
  334.9 82.3 %collective-permute-start.2 = (bf16[1216,768]{1,0:T(8,128)(2,1)}, bf16[1216,768]{1,0:T(8,128)(2,1)}, u32[]{:S(2)}, u32[]{:S(2)}) collective-permute-start(bf16[1216,768]{1,0:T(8,128)(2,1)} %add_convert_fusion.2), channel_id=1, source_target_pairs={{0,4},{2,6},{4,0},{6,2},{8,12},{10,14},{12,8},{14,10},{16,20},{18,... | collective-permute-start | bytes 5603336 | tf_op jit(solution)/shard_map/ppermute | solution.py:1059
  340.0 67.3 %collective-permute-start.19 = (bf16[1536,384]{1,0:T(8,128)(2,1)}, bf16[1536,384]{1,0:T(8,128)(2,1)}, u32[]{:S(2)}, u32[]{:S(2)}) collective-permute-start(bf16[1536,384]{1,0:T(8,128)(2,1)} %get-tuple-element.104), channel_id=1, source_target_pairs={{24,16},{26,18},{28,20},{30,22},{25,17},{27,19},{29,21},{31,23}} | collective-permute-start | bytes 3538952 | tf_op jit(solution)/shard_map/ppermute | solution.py:1093
  341.8 4.8 copy-start.6
  387.7 7.6 %copy-start.37 = (bf16[1152,768]{1,0:T(8,128)(2,1)S(1)}, bf16[1152,768]{1,0:T(8,128)(2,1)}, u32[]{:S(2)}) copy-start(bf16[1152,768]{1,0:T(8,128)(2,1)} %get-tuple-element.77) | copy-start | bytes 5308420
  395.3 7.2 %copy-start.4 = (f32[1152,768]{1,0:T(8,128)S(1)}, f32[1152,768]{1,0:T(8,128)}, u32[]{:S(2)}) copy-start(f32[1152,768]{1,0:T(8,128)} %copy-done.3) | copy-start | bytes 10616836
  395.3 7.2 %copy-start.36 = (bf16[1152,768]{1,0:T(8,128)(2,1)S(1)}, bf16[1152,768]{1,0:T(8,128)(2,1)}, u32[]{:S(2)}) copy-start(bf16[1152,768]{1,0:T(8,128)(2,1)} %get-tuple-element.72.o_ref) | copy-start | bytes 5308420
  405.7 96.1 %collective-permute-start.16 = (bf16[1536,384]{1,0:T(8,128)(2,1)}, bf16[1536,384]{1,0:T(8,128)(2,1)}, u32[]{:S(2)}, u32[]{:S(2)}) collective-permute-start(bf16[1536,384]{1,0:T(8,128)(2,1)} %get-tuple-element.99), channel_id=1, source_target_pairs={{8,10},{10,8},{12,14},{14,12},{16,18},{18,16},{20,22},{22,20},{24,... | collective-permute-start | bytes 3538952 | tf_op jit(solution)/shard_map/ppermute | solution.py:1070
  407.3 11.5 %copy-start.25 = (s32[1152]{0:T(1024)S(1)}, s32[1152]{0:T(1024)}, u32[]{:S(2)}) copy-start(s32[1152]{0:T(1024)} %copy-done.23) | copy-start | bytes 13828
  407.3 101.1 %collective-permute-start.15 = (bf16[1536,384]{1,0:T(8,128)(2,1)}, bf16[1536,384]{1,0:T(8,128)(2,1)}, u32[]{:S(2)}, u32[]{:S(2)}) collective-permute-start(bf16[1536,384]{1,0:T(8,128)(2,1)} %get-tuple-element.103), channel_id=1, source_target_pairs={{0,8},{2,10},{4,12},{6,14},{8,16},{10,18},{12,20},{14,22},{16,24},... | collective-permute-start | bytes 3538952 | tf_op jit(solution)/shard_map/ppermute | solution.py:1093
  417.2 84.6 %collective-permute-start.20 = (bf16[1536,384]{1,0:T(8,128)(2,1)}, bf16[1536,384]{1,0:T(8,128)(2,1)}, u32[]{:S(2)}, u32[]{:S(2)}) collective-permute-start(bf16[1536,384]{1,0:T(8,128)(2,1)} %fusion.29), channel_id=1, source_target_pairs={{16,8},{18,10},{20,12},{22,14},{24,16},{26,18},{28,20},{30,22},{17... | collective-permute-start | bytes 3538952 | tf_op jit(solution)/shard_map/ppermute | solution.py:1093
  494.4 11.4 %copy-start.5 = (f32[1152,768]{1,0:T(8,128)S(1)}, f32[1152,768]{1,0:T(8,128)}, u32[]{:S(2)}) copy-start(f32[1152,768]{1,0:T(8,128)} %copy-done.3) | copy-start | bytes 10616836
  494.4 11.4 %copy-start.8 = (f32[1152,768]{1,0:T(8,128)S(1)}, f32[1152,768]{1,0:T(8,128)}, u32[]{:S(2)}) copy-start(f32[1152,768]{1,0:T(8,128)} %get-tuple-element.113) | copy-start | bytes 10616836
  501.8 4.0 copy-start.32
  501.8 4.0 copy-start.2
  501.8 4.0 copy-start.27
  501.8 4.0 copy-start.31
  504.4 35.4 %collective-permute-start.21 = (bf16[1536,384]{1,0:T(8,128)(2,1)S(1)}, bf16[1536,384]{1,0:T(8,128)(2,1)S(1)}, u32[]{:S(2)}, u32[]{:S(2)}) collective-permute-start(bf16[1536,384]{1,0:T(8,128)(2,1)S(1)} %fusion.31), channel_id=1, source_target_pairs={{8,0},{10,2},{12,4},{14,6},{16,8},{18,10},{20,12},{22,14},{24,16},... | collective-permute-start | bytes 3538952 | tf_op jit(solution)/shard_map/ppermute | solution.py:1093
  626.0 6.6 %copy-start.10 = (f32[768,768]{1,0:T(8,128)S(1)}, f32[768,768]{1,0:T(8,128)}, u32[]{:S(2)}) copy-start(f32[768,768]{1,0:T(8,128)} %get-tuple-element.122) | copy-start | bytes 7077892
  (14 other events, 30.0 us)
Sparse Core Ops, SparseCore 0:
  405.8 220.1 all-reduce.4

commit v3 on v2

--- a/solution.py
+++ b/solution.py
@@ -282,89 +282,6 @@
     return starts
 
 
-def attend_backward(joint, mixed, upstream, logs, lengths):
-    count, width = joint.shape[0], joint.shape[1] // 3
-    pairs = width // 128
-    scale = (width // HEADS) ** (-0.5)
-    factor = scale * HALF_LOG
-
-    def kernel(
-        lengths_ref, q_ref, k_ref, v_ref, o_ref, u_ref, l_ref, dq_ref, dk_ref, dv_ref, bias_ref, ka_ref, va_ref
-    ):
-        @pl.when(pl.program_id(0) == 0)
-        def _():
-            places = lax.broadcasted_iota(jnp.int32, (1, count), 1)
-            starts = document_starts(lengths_ref, places)
-            for s, e in query_blocks(count):
-                row = lax.broadcasted_iota(jnp.int32, (e - s, count), 0) + s
-                seen = (row <= places) & (row >= starts)
-                bias_ref[s:e, :] = jnp.where(seen, 0.0, -1e9)
-
-        first = lax.broadcasted_iota(jnp.int32, (1, 128), 1) < 64
-        ka_ref[...] = jnp.zeros_like(ka_ref)
-        va_ref[...] = jnp.zeros_like(va_ref)
-        for s, e in query_blocks(count):
-            both = jnp.transpose(
-                u_ref[s:e, :].astype(jnp.float32) * o_ref[s:e, :].astype(jnp.float32)
-            )
-            found = []
-            for half in range(2):
-                mine = first == (half == 0)
-                inner = jnp.sum(both[64 * half : 64 * half + 64, :], axis=0, keepdims=True)
-                q = jnp.where(mine, q_ref[s:e, :], jnp.bfloat16(0))
-                u = jnp.where(mine, u_ref[s:e, :], jnp.bfloat16(0))
-                scores = lax.dot_general(
-                    k_ref[0:e, :], q, NT, preferred_element_type=jnp.float32
-                )
-                probs = jnp.exp2(
-                    scores * factor + bias_ref[0:e, s:e] - l_ref[0, half : half + 1, s:e]
-                )
-                prob_grad = lax.dot_general(
-                    v_ref[0:e, :], u, NT, preferred_element_type=jnp.float32
-                )
-                score_grad = (probs * (prob_grad - inner)).astype(jnp.bfloat16)
-                va_ref[0:e, :] += jnp.dot(
-                    probs.astype(jnp.bfloat16), u, preferred_element_type=jnp.float32
-                )
-                ka_ref[0:e, :] += jnp.dot(score_grad, q, preferred_element_type=jnp.float32)
-                found.append(
-                    lax.dot_general(
-                        score_grad, k_ref[0:e, :], TN, preferred_element_type=jnp.float32
-                    )
-                )
-            dq_ref[s:e, :] = (jnp.where(first, found[0], found[1]) * scale).astype(jnp.bfloat16)
-        dk_ref[...] = (ka_ref[...] * scale).astype(jnp.bfloat16)
-        dv_ref[...] = va_ref[...].astype(jnp.bfloat16)
-
-    column = lambda shift: pl.BlockSpec((count, 128), lambda p, _: (0, shift + p))
-    return pl.pallas_call(
-        kernel,
-        out_shape=(jax.ShapeDtypeStruct((count, width), jnp.bfloat16),) * 3,
-        grid_spec=pltpu.PrefetchScalarGridSpec(
-            num_scalar_prefetch=1,
-            grid=(pairs,),
-            in_specs=[
-                column(0),
-                column(pairs),
-                column(2 * pairs),
-                column(0),
-                column(0),
-                pl.BlockSpec((1, 2, count), lambda p, _: (p, 0, 0)),
-            ],
-            out_specs=(column(0),) * 3,
-            scratch_shapes=[
-                pltpu.VMEM((count, count), jnp.float32),
-                pltpu.VMEM((count, 128), jnp.float32),
-                pltpu.VMEM((count, 128), jnp.float32),
-            ],
-        ),
-        compiler_params=pltpu.CompilerParams(vmem_limit_bytes=VMEM_LIMIT),
-        cost_estimate=pl.CostEstimate(
-            flops=10 * count * count * width, bytes_accessed=16 * count * width, transcendentals=count * count * HEADS
-        ),
-    )(lengths, joint, joint, joint, mixed, upstream, logs)
-
-
 MESH = pl.DeviceIdType.MESH
 
 
@@ -427,7 +344,7 @@
     cot_ref,
     up_ref,
     down_ref,
-    entry_ref,
+    flipped_ref,
     joint_ref,
     mixed_ref,
     logs_ref,
@@ -601,11 +518,13 @@
         at = pl.ds(pl.multiple_of(i * 192, 192), 192)
         entry, _, _ = row_norm(tokens_ref[at, :].astype(jnp.float32), gains_ref[...], shifts_ref[...])
         entry = entry.astype(jnp.bfloat16)
-        entry_ref[at, :] = entry
+        normed_ref[at, 0:width] = entry
         joint_ref[at, :] = jnp.dot(entry, projection_ref[...], preferred_element_type=jnp.float32).astype(jnp.bfloat16)
         return 0
 
     lax.fori_loop(0, count // 192, project, 0)
+    for s in range(0, count, 384):
+        flipped_ref[:, s : s + 384] = jnp.transpose(normed_ref[s : s + 384, 0:width])
     score_bias(bias_ref, lengths_ref, count)
     forward_weights(0, 1)
     tally_step(0)
@@ -740,7 +659,7 @@
     dma = pltpu.SemaphoreType.DMA
     copies = 2 * (2 * (planes - 1) + slots) + 12 + 3 + 5
     outs = [
-        (shape((count, width), bf16), local),
+        (shape((width, count), bf16), local),
         (shape((count, 3 * width), bf16), local),
         (shape((count, width), bf16), local),
         (shape((pairs, 2, count), f32), local),
@@ -794,6 +713,694 @@
     )
 
 
+STEP = 192
+
+
+def rear_kernel(
+    planes,
+    slabs,
+    total_tokens,
+    lengths_ref,
+    tokens_ref,
+    gains_ref,
+    projection_ref,
+    mixing_ref,
+    factors_ref,
+    biases_ref,
+    centroids_ref,
+    route_ref,
+    cot_ref,
+    flipped_ref,
+    joint_in,
+    mixed_ref,
+    logs_ref,
+    residual_in,
+    place_ref,
+    loads_ref,
+    dots_ref,
+    back_all,
+    made_all,
+    near_all,
+    far_all,
+    layer_ref,
+    token_ref,
+    vector_ref,
+    up_out,
+    down_out,
+    shared_out,
+    core_land,
+    y_land,
+    x_land,
+    z_land,
+    joint_ref,
+    residual_ref,
+    bias_ref,
+    upstream_ref,
+    a_ref,
+    b_ref,
+    place_col,
+    gate_col,
+    dot_land,
+    part_ref,
+    stage_ref,
+    own_ref,
+    own_core,
+    own_x,
+    own_y,
+    own_z,
+    piece_ref,
+    tally_ref,
+    key_sums,
+    send_sem,
+    recv_sem,
+    local_sem,
+):
+    count, width = tokens_ref.shape
+    experts = planes
+    rows = a_ref.shape[0]
+    half_rows = rows // 2
+    pairs = width // 128
+    half = width // 2
+    scale = (width // HEADS) ** (-0.5)
+    factor = scale * HALF_LOG
+    average = total_tokens / experts
+    me, core, plane, beside_x, beside_y, beside_core = neighbours(slabs)
+    x = lax.rem(me, 2)
+    y = lax.rem(lax.div(me, 2), 2)
+    here = lax.rem(me, slabs)
+    diagonal = (beside_y[0], 1 - core)
+    always = plane >= 0
+    others = [(lax.rem(plane + d, planes) * slabs + here, core) for d in range(1, planes)]
+    greet([(d, always) for d in [beside_x, beside_y, beside_core, diagonal] + others])
+    ids = {}
+
+    def remote(key, src, dst, device):
+        i = ids.setdefault(key, len(ids))
+        return pltpu.make_async_remote_copy(
+            src_ref=src, dst_ref=dst, send_sem=send_sem.at[i], recv_sem=recv_sem.at[i], device_id=device, device_id_type=MESH
+        )
+
+    def fetch(i, src, dst):
+        return pltpu.make_async_copy(src, dst, local_sem.at[i])
+
+    loads = [fetch(0, joint_in, joint_ref), fetch(1, residual_in, residual_ref)]
+    for copy in loads:
+        copy.start()
+
+    alls = (back_all, made_all)
+
+    def to_core(which, second, piece):
+        at = pl.ds(piece * half_rows, half_rows)
+        return remote(
+            ("core", which, second, piece), alls[which].at[1 + 2 * second, at], core_land.at[which, second, at], beside_core
+        )
+
+    def to_y(which, piece):
+        at = pl.ds(piece * half_rows, half_rows)
+        return remote(("y", which, piece), a_ref.at[at], y_land.at[which, at], beside_y)
+
+    def dot_copy(k):
+        return remote(("dot", k), dots_ref.at[1 + k], dot_land.at[k], (beside_core, beside_y, diagonal)[k])
+
+    for which in range(2):
+        for second in (1, 0):
+            for piece in range(2):
+                to_core(which, second, piece).start()
+        if which == 0:
+            for k in range(3):
+                dot_copy(k).start()
+
+    def target(sign, r):
+        e = plane + sign * r
+        return jnp.clip(e, 0, planes - 1), (e >= 0) & (e < planes)
+
+    def share_x(sign, r):
+        e, _ = target(sign, r)
+        return remote(("x", sign, r), far_all.at[e], x_land.at[e], beside_x)
+
+    def share_z(sign, r):
+        return remote(
+            ("z", sign, r),
+            stage_ref.at[0 if sign > 0 else 1],
+            z_land.at[0 if sign > 0 else 1, r - 1],
+            (jnp.clip(me + sign * slabs, 0, planes * slabs - 1), core),
+        )
+
+    ways = [(s, r) for r in range(planes - 1, 0, -1) for s in (1, -1)] + [(1, 0)]
+    for sign, r in ways:
+        @pl.when(target(sign, r)[1])
+        def _(sign=sign, r=r):
+            share_x(sign, r).start()
+
+    def add_pieces(into, sources, size, step):
+        def one(i, _):
+            at = pl.ds(pl.multiple_of(i * step, step), step)
+            total = sources[0][at, :].astype(jnp.float32)
+            for s in sources[1:]:
+                total = total + s[at, :].astype(jnp.float32)
+            into[at, :] = total.astype(into.dtype)
+            return 0
+        lax.fori_loop(0, size // step, one, 0)
+
+    def share_step(sign, r):
+        e, valid = target(sign, r)
+        lane = 0 if sign > 0 else 1
+
+        @pl.when(valid)
+        def _():
+            first = fetch(2, near_all.at[e], part_ref.at[0])
+            first.start()
+            share_x(sign, r).wait_recv()
+            second = fetch(3, x_land.at[e], part_ref.at[1])
+            second.start()
+            if r < planes - 1:
+                @pl.when(target(sign, r + 1)[1])
+                def _():
+                    share_z(sign, r + 1).wait_send()
+            first.wait()
+            second.wait()
+            add_pieces(stage_ref.at[lane], [part_ref.at[0], part_ref.at[1]], part_ref.shape[1], 96)
+            if r < planes - 1:
+                @pl.when((plane - sign >= 0) & (plane - sign < planes))
+                def _():
+                    share_z(sign, r + 1).wait_recv()
+                    third = fetch(2, z_land.at[lane, r], part_ref.at[0])
+                    third.start()
+                    third.wait()
+                    add_pieces(stage_ref.at[lane], [stage_ref.at[lane], part_ref.at[0]], part_ref.shape[1], 96)
+            share_z(sign, r).start()
+
+    def share_end():
+        share_x(1, 0).wait_recv()
+        copies = [fetch(2, near_all.at[plane], part_ref.at[0]), fetch(3, x_land.at[plane], part_ref.at[1])]
+        for copy in copies:
+            copy.start()
+        for copy in copies:
+            copy.wait()
+
+        def put(sources, more):
+            def rows_of(i, _):
+                at = pl.ds(pl.multiple_of(i * 96, 96), 96)
+                total = sources[0][at, :].astype(jnp.float32)
+                if len(sources) > 1:
+                    total = total + sources[1][at, :].astype(jnp.float32)
+                up_out[at, :] = up_out[at, :] + total if more else total
+                return 0
+            lax.fori_loop(0, width // 96, rows_of, 0)
+
+            def columns_of(i, _):
+                at = pl.ds(pl.multiple_of(i * 96, 96), 96)
+                for part in range(2):
+                    source_at = pl.ds(pl.multiple_of(width + part * half + i * 96, 32), 96)
+                    total = sources[0][source_at, :].astype(jnp.float32)
+                    if len(sources) > 1:
+                        total = total + sources[1][source_at, :].astype(jnp.float32)
+                    to = slice(part * half, (part + 1) * half)
+                    down_out[at, to] = down_out[at, to] + total if more else total
+                return 0
+            lax.fori_loop(0, half // 96, columns_of, 0)
+
+        put([part_ref.at[0], part_ref.at[1]], False)
+        for sign in (1, -1):
+            lane = 0 if sign > 0 else 1
+
+            @pl.when((plane - sign >= 0) & (plane - sign < planes))
+            def _(sign=sign, lane=lane):
+                share_z(sign, 1).wait_recv()
+                third = fetch(2, z_land.at[lane, 0], part_ref.at[0])
+                third.start()
+                third.wait()
+                put([part_ref.at[0]], True)
+
+    q1, q2, q3, q4 = width // 2, width // 4, width // 8, width // 16
+    base1 = core * q1
+    base2 = base1 + x * q2
+    base3 = base2 + y * q3
+
+    def spot(start, size):
+        return pl.ds(pl.multiple_of(start, 16), size)
+
+    def corner(p):
+        return lax.div(p, 2) * q4, pl.multiple_of(lax.rem(p, 2) * half, 128)
+
+    def sum_copy(c, stage, d=0):
+        own = own_ref.at[c % 2]
+        if stage == "core":
+            return remote((c, stage), own.at[spot((1 - core) * q1, q1)], own_core.at[c], beside_core)
+        if stage == "x":
+            return remote((c, stage), own.at[spot(base1 + (1 - x) * q2, q2)], own_x.at[c], beside_x)
+        if stage == "y":
+            return remote((c, stage), own.at[spot(base2 + (1 - y) * q3, q3)], own_y.at[c], beside_y)
+        if stage == "z":
+            r, k = corner(lax.rem(plane + d, planes))
+            return remote(
+                (c, stage, d), own.at[spot(base3 + r, q4), pl.ds(k, half)], own_z.at[c, d - 1], others[d - 1]
+            )
+        out = shared_out.at[c]
+        if stage == "zz":
+            r, k = corner(plane)
+            return remote(
+                (c, stage, d), piece_ref.at[c], out.at[spot(base3 + r, q4), pl.ds(k, half)], others[d - 1]
+            )
+        if stage == "yy":
+            at = spot(base3, q3)
+            return remote((c, stage), out.at[at], out.at[at], beside_y)
+        if stage == "xx":
+            at = spot(base2, q2)
+            return remote((c, stage), out.at[at], out.at[at], beside_x)
+        at = spot(base1, q1)
+        return remote((c, stage), out.at[at], out.at[at], beside_core)
+
+    def add_rows(c, start, size, came, step):
+        def one(i, _):
+            at = pl.ds(pl.multiple_of(i * step, step), step)
+            mine = spot(start + i * step, step)
+            own_ref[c % 2, mine, :] = (
+                own_ref[c % 2, mine, :].astype(jnp.float32) + came[c, at, :].astype(jnp.float32)
+            ).astype(jnp.bfloat16)
+            return 0
+        lax.fori_loop(0, size // step, one, 0)
+
+    def keep_piece(c):
+        r, k = corner(plane)
+        return fetch(4 + c, piece_ref.at[c], shared_out.at[c, spot(base3 + r, q4), pl.ds(k, half)])
+
+    def sum_step(c, stage):
+        if stage == 0:
+            sum_copy(c, "core").start()
+        elif stage == 1:
+            sum_copy(c, "core").wait_recv()
+            add_rows(c, base1, q1, own_core, 48)
+            sum_copy(c, "x").start()
+        elif stage == 2:
+            sum_copy(c, "x").wait_recv()
+            add_rows(c, base2, q2, own_x, 48)
+            sum_copy(c, "y").start()
+        elif stage == 3:
+            sum_copy(c, "y").wait_recv()
+            add_rows(c, base3, q3, own_y, 48)
+            for d in range(1, planes):
+                sum_copy(c, "z", d).start()
+        elif stage == 4:
+            r, k = corner(plane)
+            total = own_ref[c % 2, spot(base3 + r, q4), pl.ds(k, half)].astype(jnp.float32)
+            for d in range(1, planes):
+                sum_copy(c, "z", d).wait_recv()
+                total = total + own_z[c, d - 1].astype(jnp.float32)
+            piece_ref[c] = total.astype(jnp.bfloat16)
+            keep_piece(c).start()
+            for d in range(1, planes):
+                sum_copy(c, "zz", d).start()
+        elif stage == 5:
+            keep_piece(c).wait()
+            for d in range(1, planes):
+                sum_copy(c, "zz", d).wait_recv()
+            sum_copy(c, "yy").start()
+        elif stage == 6:
+            sum_copy(c, "yy").wait_recv()
+            sum_copy(c, "xx").start()
+        elif stage == 7:
+            sum_copy(c, "xx").wait_recv()
+            sum_copy(c, "cc").start()
+        else:
+            sum_copy(c, "cc").wait_recv()
+
+    def sum_sent(c):
+        for stage in ("core", "x", "y"):
+            sum_copy(c, stage).wait_send()
+        for d in range(1, planes):
+            sum_copy(c, "z", d).wait_send()
+
+    def sum_for_y(which):
+        for piece in range(2):
+            at = pl.ds(piece * half_rows, half_rows)
+            first = fetch(2, alls[which].at[2, at], a_ref.at[at])
+            first.start()
+            to_core(which, 1, piece).wait_recv()
+            second = fetch(3, core_land.at[which, 1, at], b_ref.at[at])
+            second.start()
+            first.wait()
+            second.wait()
+            add_pieces(a_ref.at[at], [a_ref.at[at], b_ref.at[at]], half_rows, 32)
+            to_y(which, piece).start()
+
+    sum_for_y(0)
+    place_col[...] = jnp.transpose(place_ref[...])
+    score_bias(bias_ref, lengths_ref, count)
+    for copy in loads:
+        copy.wait()
+    vector_ref[...] = jnp.zeros_like(vector_ref)
+    number = lax.broadcasted_iota(jnp.int32, (1, rows), 1).astype(jnp.float32)
+
+    def order_of(at):
+        return jnp.where(place_col[at, 0:1] == number, 1.0, 0.0)
+
+    def chunk_of(i):
+        return pl.ds(pl.multiple_of(i * STEP, STEP), STEP)
+
+    steps = count // STEP
+
+    def unsort(buffer, act):
+        def one(i, _):
+            at = chunk_of(i)
+            act(at, jnp.dot(order_of(at).astype(jnp.bfloat16), buffer[...], preferred_element_type=jnp.float32))
+            return 0
+        lax.fori_loop(0, steps, one, 0)
+
+    def set_token(at, value):
+        token_ref[at, :] = value
+
+    def add_token(at, value):
+        token_ref[at, :] += value
+
+    own_back = fetch(2, back_all.at[0], b_ref)
+    own_back.start()
+    own_back.wait()
+    unsort(b_ref, set_token)
+    for piece in range(2):
+        to_core(0, 0, piece).wait_recv()
+    core_back = fetch(2, core_land.at[0, 0], b_ref)
+    core_back.start()
+    core_back.wait()
+    unsort(b_ref, add_token)
+    for sign in (1, -1):
+        share_step(sign, planes - 1)
+    for piece in range(2):
+        to_y(0, piece).wait_recv()
+    y_back = fetch(2, y_land.at[0], b_ref)
+    y_back.start()
+    y_back.wait()
+    unsort(b_ref, add_token)
+    for k in range(3):
+        dot_copy(k).wait_recv()
+    dots = dots_ref[0] + dot_land[0] + dot_land[1] + dot_land[2]
+    dots = dots[0:1, :]
+
+    def norm_step(i, _):
+        at = chunk_of(i)
+        normed, normal, spread_by = row_norm(residual_ref[at, :], factors_ref[...], biases_ref[...])
+        route = route_ref[at, :]
+        chosen = chosen_rows(route, centroids_ref, experts)
+        gate = 1.0 / (1.0 + jnp.exp(-jnp.sum(normed * chosen, axis=1, keepdims=True)))
+        gate_col[at, :] = jnp.broadcast_to(gate, (STEP, 128))
+        gate_grad = jnp.sum(order_of(at) * dots, axis=1, keepdims=True)
+        spread = jnp.zeros((STEP, 1), jnp.float32)
+        for e in range(experts):
+            spread = jnp.where(route == e, (loads_ref[e : e + 1, 0:1] - average) * (1.0 / average), spread)
+        logit = (gate_grad + spread * (1.0 / total_tokens)) * gate * (1.0 - gate)
+        above = token_ref[at, :] + logit * chosen
+        pull = logit * normed
+        vector_ref[2:3, :] += jnp.sum(above * normal, axis=0, keepdims=True)
+        vector_ref[3:4, :] += jnp.sum(above, axis=0, keepdims=True)
+        for e in range(experts):
+            vector_ref[8 + e : 9 + e, :] += jnp.sum(jnp.where(route == e, pull, 0.0), axis=0, keepdims=True)
+        vector_ref[4:5, :] += jnp.broadcast_to(
+            jnp.sum(spread * gate, axis=0, keepdims=True) * (1.0 / total_tokens), (1, width)
+        )
+        scaled = above * factors_ref[...]
+        inner = (
+            scaled
+            - jnp.mean(scaled, axis=1, keepdims=True)
+            - normal * jnp.mean(scaled * normal, axis=1, keepdims=True)
+        )
+        grad = cot_ref[at, :].astype(jnp.float32) + inner * spread_by
+        token_ref[at, :] = grad
+        branch = grad.astype(jnp.bfloat16)
+        layer_ref[at, :] = branch
+        upstream_ref[at, :] = lax.dot_general(
+            branch, mixing_ref[...], NT, preferred_element_type=jnp.float32
+        ).astype(jnp.bfloat16)
+        return 0
+
+    lax.fori_loop(0, steps, norm_step, 0)
+    own_ref[0] = lax.dot_general(
+        mixed_ref[...], layer_ref[...], TN, preferred_element_type=jnp.float32
+    ).astype(jnp.bfloat16)
+    sum_step(0, 0)
+    for piece in range(2):
+        to_y(0, piece).wait_send()
+    sum_for_y(1)
+
+    first = lax.broadcasted_iota(jnp.int32, (1, 128), 1) < 64
+
+    def attend(p, _):
+        lanes = pl.ds(pl.multiple_of(p * 128, 128), 128)
+        keys = pl.ds(pl.multiple_of(width + p * 128, 128), 128)
+        values = pl.ds(pl.multiple_of(2 * width + p * 128, 128), 128)
+        key_sum, value_sum = key_sums.at[0], key_sums.at[1]
+        key_sum[...] = jnp.zeros_like(key_sum)
+        value_sum[...] = jnp.zeros_like(value_sum)
+        for s, e in query_blocks(count):
+            both = jnp.transpose(
+                upstream_ref[s:e, lanes].astype(jnp.float32) * mixed_ref[s:e, lanes].astype(jnp.float32)
+            )
+            found = []
+            for h in range(2):
+                mine = first == (h == 0)
+                inner = jnp.sum(both[64 * h : 64 * h + 64, :], axis=0, keepdims=True)
+                q = jnp.where(mine, joint_ref[s:e, lanes], jnp.bfloat16(0))
+                u = jnp.where(mine, upstream_ref[s:e, lanes], jnp.bfloat16(0))
+                scores = lax.dot_general(joint_ref[0:e, keys], q, NT, preferred_element_type=jnp.float32)
+                probs = jnp.exp2(scores * factor + bias_ref[0:e, s:e] - logs_ref[p, h : h + 1, s:e])
+                prob_grad = lax.dot_general(joint_ref[0:e, values], u, NT, preferred_element_type=jnp.float32)
+                score_grad = (probs * (prob_grad - inner)).astype(jnp.bfloat16)
+                value_sum[0:e, :] += jnp.dot(probs.astype(jnp.bfloat16), u, preferred_element_type=jnp.float32)
+                key_sum[0:e, :] += jnp.dot(score_grad, q, preferred_element_type=jnp.float32)
+                found.append(
+                    lax.dot_general(score_grad, joint_ref[0:e, keys], TN, preferred_element_type=jnp.float32)
+                )
+            joint_ref[s:e, lanes] = (jnp.where(first, found[0], found[1]) * scale).astype(jnp.bfloat16)
+        joint_ref[:, keys] = (key_sum[...] * scale).astype(jnp.bfloat16)
+        joint_ref[:, values] = value_sum[...].astype(jnp.bfloat16)
+
+        events = {
+            0: [(0, 1)],
+            1: [(0, 2)],
+            2: [(0, 3), (1, 1)],
+            3: [(0, 4), (1, 2)],
+            4: [(0, 5), (1, 3), (2, 1)],
+            5: [(0, 6), (1, 4), (2, 2)],
+        }
+        for k, steps_of in events.items():
+            @pl.when(p == k)
+            def _(k=k, steps_of=steps_of):
+                if k == 1:
+                    for sign in (1, -1):
+                        share_step(sign, 2)
+                if k == 5:
+                    for sign in (1, -1):
+                        share_step(sign, 1)
+                for c, stage in steps_of:
+                    sum_step(c, stage)
+        for c in range(1, 4):
+            @pl.when(p == 2 * c - 1)
+            def _(c=c):
+                if c >= 2:
+                    sum_sent(c - 2)
+                for k in range(3):
+                    at = pl.ds(k * width + (c - 1) * 256, 256)
+                    own_ref[c % 2, :, k * 256 : (k + 1) * 256] = jnp.dot(
+                        flipped_ref[...], joint_ref[:, at], preferred_element_type=jnp.float32
+                    ).astype(jnp.bfloat16)
+                sum_step(c, 0)
+
+        return 0
+
+    lax.fori_loop(0, pairs, attend, 0)
+
+    rounds = [beside_core, beside_x, beside_y]
+    rounds += [((plane + 1 - 2 * lax.rem(plane, 2)) * slabs + here, core), (lax.rem(plane + 2, planes) * slabs + here, core)]
+
+    def tally(k):
+        return remote(("tally", k), tally_ref.at[2 * k], tally_ref.at[2 * k + 1], rounds[k])
+
+    def tally_step(k):
+        tally(k).wait_recv()
+        total = tally_ref[2 * k] + tally_ref[2 * k + 1]
+        if k + 1 < len(rounds):
+            tally_ref[2 * k + 2] = total
+            tally(k + 1).start()
+        else:
+            vector_ref[...] = total
+
+    def finish_step(i, _):
+        at = chunk_of(i)
+        back = lax.dot_general(joint_ref[at, :], projection_ref[...], NT, preferred_element_type=jnp.float32)
+        _, normal, spread_by = row_norm(tokens_ref[at, :].astype(jnp.float32), gains_ref[...], gains_ref[...])
+        scaled = back * gains_ref[...]
+        inner = (
+            scaled
+            - jnp.mean(scaled, axis=1, keepdims=True)
+            - normal * jnp.mean(scaled * normal, axis=1, keepdims=True)
+        )
+        token_ref[at, :] += inner * spread_by
+        vector_ref[0:1, :] += jnp.sum(back * normal, axis=0, keepdims=True)
+        vector_ref[1:2, :] += jnp.sum(back, axis=0, keepdims=True)
+        return 0
+
+    def add_made(at, value):
+        residual_ref[at, :] += gate_col[at, 0:1] * value
+
+    def end_made(at, value):
+        layer_ref[at, :] = (residual_ref[at, :] + gate_col[at, 0:1] * value).astype(jnp.bfloat16)
+
+    def gather_made(source, act):
+        copy = fetch(2, source, b_ref)
+        copy.start()
+        copy.wait()
+        unsort(b_ref, act)
+
+    lax.fori_loop(0, steps // 2, finish_step, 0)
+    for c, stage in ((0, 7), (1, 5), (2, 3), (3, 1)):
+        sum_step(c, stage)
+    lax.fori_loop(steps // 2, steps, finish_step, 0)
+    tally_ref[0] = vector_ref[...]
+    tally(0).start()
+    for c, stage in ((0, 8), (1, 6), (2, 4), (3, 2)):
+        sum_step(c, stage)
+    gather_made(made_all.at[0], add_made)
+    for c, stage in ((1, 7), (2, 5), (3, 3)):
+        sum_step(c, stage)
+    tally_step(0)
+    for piece in range(2):
+        to_core(1, 0, piece).wait_recv()
+    gather_made(core_land.at[1, 0], add_made)
+    for c, stage in ((1, 8), (2, 6), (3, 4)):
+        sum_step(c, stage)
+    tally_step(1)
+    for piece in range(2):
+        to_y(1, piece).wait_recv()
+    gather_made(y_land.at[1], end_made)
+    for c, stage in ((2, 7), (3, 5)):
+        sum_step(c, stage)
+    tally_step(2)
+    share_end()
+    for c, stage in ((2, 8), (3, 6)):
+        sum_step(c, stage)
+    tally_step(3)
+    sum_step(3, 7)
+    tally_step(4)
+    sum_step(3, 8)
+
+    for which in range(2):
+        for piece in range(2):
+            for second in range(2):
+                to_core(which, second, piece).wait_send()
+    for piece in range(2):
+        to_y(1, piece).wait_send()
+    for k in range(3):
+        dot_copy(k).wait_send()
+    for sign, r in ways:
+        @pl.when(target(sign, r)[1])
+        def _(sign=sign, r=r):
+            share_x(sign, r).wait_send()
+    for sign in (1, -1):
+        @pl.when(target(sign, 1)[1])
+        def _(sign=sign):
+            share_z(sign, 1).wait_send()
+    for c in (2, 3):
+        sum_sent(c)
+    for c in range(4):
+        for d in range(1, planes):
+            sum_copy(c, "zz", d).wait_send()
+        for stage in ("yy", "xx", "cc"):
+            sum_copy(c, stage).wait_send()
+    for k in range(len(rounds)):
+        tally(k).wait_send()
+    assert len(ids) <= send_sem.shape[0]
+
+
+def rear_stage(
+    tokens, gains, projection, mixing, factors, biases, centroids, route, lengths, cotangent,
+    flipped, joint, mixed, logs, residual, place, loads, dots, back, made, near, far, planes, slabs, total_tokens,
+):
+    count, width = tokens.shape
+    rows = back.shape[1]
+    half = width // 2
+    bf16, f32 = jnp.bfloat16, jnp.float32
+    shape = jax.ShapeDtypeStruct
+    anywhere = pl.BlockSpec(memory_space=pl.ANY)
+    local = pl.BlockSpec(memory_space=pltpu.VMEM)
+    dma = pltpu.SemaphoreType.DMA
+    packed = near.shape[1:]
+    outs = [
+        (shape((count, width), bf16), local),
+        (shape((count, width), f32), local),
+        (shape((16, width), f32), local),
+        (shape((width, half), f32), local),
+        (shape((half, width), f32), local),
+        (shape((4, width, width), bf16), anywhere),
+        (shape((2, 2, rows, width), bf16), anywhere),
+        (shape((2, rows, width), bf16), anywhere),
+        (shape((planes,) + packed, bf16), anywhere),
+        (shape((2, planes - 1) + packed, bf16), anywhere),
+    ]
+    row = lambda v: v.reshape(1, -1)
+    copies = 120
+    return pl.pallas_call(
+        partial(rear_kernel, planes, slabs, total_tokens),
+        out_shape=[o[0] for o in outs],
+        in_specs=[pl.BlockSpec(memory_space=pltpu.SMEM)]
+        + [local] * 10
+        + [anywhere]
+        + [local] * 2
+        + [anywhere]
+        + [local] * 3
+        + [anywhere] * 4,
+        out_specs=[o[1] for o in outs],
+        scratch_shapes=[
+            pltpu.VMEM((count, 3 * width), bf16),
+            pltpu.VMEM((count, width), f32),
+            pltpu.VMEM((count, count), f32),
+            pltpu.VMEM((count, width), bf16),
+            pltpu.VMEM((rows, width), bf16),
+            pltpu.VMEM((rows, width), bf16),
+            pltpu.VMEM((count, 8), f32),
+            pltpu.VMEM((count, 128), f32),
+            pltpu.VMEM((3, 8, rows), f32),
+            pltpu.VMEM((2,) + packed, bf16),
+            pltpu.VMEM((2,) + packed, bf16),
+            pltpu.VMEM((2, width, width), bf16),
+            pltpu.VMEM((4, width // 2, width), bf16),
+            pltpu.VMEM((4, width // 4, width), bf16),
+            pltpu.VMEM((4, width // 8, width), bf16),
+            pltpu.VMEM((4, planes - 1, width // 16, half), bf16),
+            pltpu.VMEM((4, width // 16, half), bf16),
+            pltpu.VMEM((10, 16, width), f32),
+            pltpu.VMEM((2, count, 128), f32),
+            dma((copies,)),
+            dma((copies,)),
+            dma((8,)),
+        ],
+        compiler_params=pltpu.CompilerParams(
+            collective_id=1, has_side_effects=True, vmem_limit_bytes=VMEM_LIMIT
+        ),
+    )(
+        lengths[0],
+        tokens,
+        row(gains),
+        projection,
+        mixing,
+        row(factors),
+        row(biases),
+        jnp.pad(centroids, ((0, -centroids.shape[0] % 8), (0, 0))),
+        route,
+        cotangent,
+        flipped,
+        joint,
+        mixed,
+        logs,
+        residual,
+        place,
+        loads,
+        dots,
+        back,
+        made,
+        near,
+        far,
+    )
+
+
 TILE = 256
 ALIGN = 16
 
@@ -830,12 +1437,12 @@
     sent_refs = [sent_own] + [sent_others.at[s] for s in range(sources - 1)]
     cot_refs = [cot_own] + [cot_others.at[s] for s in range(sources - 1)]
     gate_refs = [gate_own] + [gate_others.at[s] for s in range(sources - 1)]
-    back_outs, refs = refs[:sources], refs[sources:]
-    made_outs, refs = refs[:sources], refs[sources:]
-    dot_outs, refs = refs[:sources], refs[sources:]
-    near_out, far_out = refs[:2]
-    (x_ref, c_ref, g_ref, column_ref, up_ref, down_ref, gu_ref, gd_ref, pack_ref, zero_ref) = refs[2:12]
-    weight_sem, row_sem, out_sem, grad_sem, zero_sem = refs[12:]
+    back_all, made_all, dots_all, near_out, far_out = refs[:5]
+    back_outs = [back_all.at[s] for s in range(sources)]
+    made_outs = [made_all.at[s] for s in range(sources)]
+    dot_outs = [dots_all.at[s] for s in range(sources)]
+    (x_ref, c_ref, g_ref, column_ref, up_ref, down_ref, gu_ref, gd_ref, pack_ref, zero_ref) = refs[5:15]
+    weight_sem, row_sem, out_sem, grad_sem, zero_sem = refs[15:]
     half = hidden // 2
     own = meta_ref[0]
 
@@ -968,7 +1575,7 @@
 
         slot = e % 2
         grads = lambda e, slot: [
-            pltpu.make_async_copy(pack_ref.at[slot, j], ref.at[e - own + experts - 1], grad_sem.at[slot, j])
+            pltpu.make_async_copy(pack_ref.at[slot, j], ref.at[e], grad_sem.at[slot, j])
             for j, ref in enumerate((near_out, far_out))
         ]
         if e >= 2:
@@ -1016,18 +1623,20 @@
     slots = 2 * experts - 1
     dma = pltpu.SemaphoreType.DMA
     packed = (width + hidden, half)
-    outs = pl.pallas_call(
+    return pl.pallas_call(
         partial(expert_kernel_body, experts, sources, rows, limit, width, hidden),
         out_shape=(
-            [jax.ShapeDtypeStruct((rows, width), jnp.bfloat16)] * (2 * sources)
-            + [jax.ShapeDtypeStruct((8, rows), jnp.float32)] * sources
-            + [jax.ShapeDtypeStruct((slots,) + packed, jnp.bfloat16)] * 2
+            jax.ShapeDtypeStruct((sources, rows, width), jnp.bfloat16),
+            jax.ShapeDtypeStruct((sources, rows, width), jnp.bfloat16),
+            jax.ShapeDtypeStruct((sources, 8, rows), jnp.float32),
+            jax.ShapeDtypeStruct((experts,) + packed, jnp.bfloat16),
+            jax.ShapeDtypeStruct((experts,) + packed, jnp.bfloat16),
         ),
         in_specs=[pl.BlockSpec(memory_space=pltpu.SMEM)]
         + [anywhere] * 4
         + [local] * 2
         + [anywhere] * 4,
-        out_specs=[anywhere] * (2 * sources) + [local] * sources + [anywhere] * 2,
+        out_specs=(anywhere, anywhere, local, anywhere, anywhere),
         scratch_shapes=[
             pltpu.VMEM((joined, width), jnp.bfloat16),
             pltpu.VMEM((joined, width), jnp.bfloat16),
@@ -1050,49 +1659,6 @@
             flops=12 * sources * rows * width * hidden, bytes_accessed=100_000_000, transcendentals=sources * rows * hidden
         ),
     )(meta, *sent, *cot, *gates, *weights)
-    back, made, dots = outs[:sources], outs[sources : 2 * sources], outs[2 * sources : 3 * sources]
-    return back, made, dots, outs[-2], outs[-1]
-
-
-def swap(value, bit):
-    groups = lax.axis_size("expert")
-    return lax.ppermute(value, "expert", [(i, i ^ bit) for i in range(groups)])
-
-
-def across(value):
-    return lax.ppermute(value, "tensor", [(0, 1), (1, 0)])
-
-
-def beside(value, planes, slabs, shift):
-    pairs = [
-        (i, i ^ 1) for i in range(planes * slabs) if 0 <= i // slabs + shift < planes
-    ]
-    return lax.ppermute(value, "expert", pairs)
-
-
-def reduce_weights(near, far, planes, slabs):
-    sums = {}
-    for k in range(planes - 1, -1, -1):
-        for sign in (1, -1):
-            if k or sign > 0:
-                at = planes - 1 + sign * k
-                came = beside(far[at], planes, slabs, sign * k)
-                sums[sign * k] = near[at].astype(jnp.float32) + came.astype(jnp.float32)
-    arrived = []
-    for sign in (1, -1):
-        came = None
-        for k in range(planes - 1, 0, -1):
-            total = sums[sign * k]
-            if came is not None:
-                total = total + came.astype(jnp.float32)
-            pairs = [
-                (i, i + sign * slabs)
-                for i in range(planes * slabs)
-                if 0 <= i // slabs + sign * k < planes
-            ]
-            came = lax.ppermute(total.astype(jnp.bfloat16), "expert", pairs)
-        arrived.append(came.astype(jnp.float32))
-    return sums[0] + arrived[0] + arrived[1]
 
 
 def per_device(
@@ -1114,106 +1680,40 @@
     experts = centroids.shape[0]
     groups = lax.axis_size("expert")
     slabs = groups // experts
-    half = expanding.shape[2]
     limit = 2 * count // experts
     total_tokens = count * groups * lax.axis_size("tensor")
-    average = total_tokens / experts
-    rows = aligned_rows(count, experts)
-    me, core = lax.axis_index("expert"), lax.axis_index("tensor")
-
-    route = routes[:, 0]
-    picks = routes == jnp.arange(experts, dtype=jnp.int32)[None, :]
-    entry, joint, mixed_rows, logs, residual, place, loads, sent_own, cot_own, gate_own, sent_others, cot_others, gate_others, *weights = front_stage(
+
+    flipped, joint, mixed, logs, residual, place, loads, sent_own, cot_own, gate_own, sent_others, cot_others, gate_others, *weights = front_stage(
         tokens, gains, shifts, projection, mixing, factors, biases, centroids, expanding, contracting, routes, lengths, cotangent, experts, slabs
     )
-    spread = (loads[:experts, 0] - average) / average
-    token_spread = jnp.sum(jnp.where(picks, spread[None, :], 0.0), axis=1)
-    position = place[0].astype(jnp.int32)
     sizes = jnp.concatenate((gate_own[1:2, :experts], gate_others[:, 1, :experts]), axis=0)
     meta = jnp.concatenate(
-        [(me // slabs).astype(jnp.int32)[None], sizes.reshape(-1).astype(jnp.int32)]
-    )
-    back_order = (position[:, None] == jnp.arange(rows, dtype=jnp.int32)[None, :]).astype(jnp.bfloat16)
-    inputs = tokens.astype(jnp.float32)
-    _, entry_normal, entry_scale = norm_parts(inputs, gains, shifts)
-    normed, mixer_normal, mixer_scale = norm_parts(residual, factors, biases)
-    chosen = jnp.dot(picks.astype(jnp.bfloat16), centroids, preferred_element_type=jnp.float32)
-    gates = jax.nn.sigmoid(jnp.sum(normed * chosen, axis=1))
-    back, made, dots, near_grads, far_grads = expert_stage(
+        [lax.div(lax.axis_index("expert"), slabs)[None], sizes.reshape(-1).astype(jnp.int32)]
+    )
+    back, made, dots, near, far = expert_stage(
         meta, (sent_own, sent_others), (cot_own, cot_others), (gate_own, gate_others), weights, experts, limit
     )
-
-    def collect(parts, narrow):
-        own = parts[0].astype(jnp.float32) + across(parts[1]).astype(jnp.float32)
-        other = parts[2].astype(jnp.float32) + across(parts[3]).astype(jnp.float32)
-        return own, swap(other.astype(narrow), 2)
-
-    def unsort(own, came):
-        high = own.astype(jnp.bfloat16)
-        return jnp.dot(
-            back_order, high, preferred_element_type=jnp.float32
-        ) + jnp.dot(back_order, came, preferred_element_type=jnp.float32)
-
-    dot_own, dot_came = collect(dots, jnp.float32)
-    gate_rows = (dot_own + dot_came)[0]
-    gate_grad = jnp.sum(
-        jnp.where(position[:, None] == jnp.arange(rows, dtype=jnp.int32)[None, :], gate_rows[None, :], 0.0),
-        axis=1,
-    )
-    sent_grad = unsort(*collect(back, jnp.bfloat16))
-    made_own, made_came = collect(made, jnp.bfloat16)
-    up_down = reduce_weights(near_grads, far_grads, experts, slabs)
-
-    upstream = cotangent.astype(jnp.float32)
-    balance_part = jnp.sum(token_spread * gates) / total_tokens
-    logit_grad = (gate_grad + token_spread / total_tokens) * gates * (1.0 - gates)
-    normed_grad = sent_grad + logit_grad[:, None] * chosen
-    centroid_grad = jnp.einsum(
-        "te,td->ed", picks.astype(jnp.float32), logit_grad[:, None] * normed, precision=highest
-    )
-    mixer_back, factor_grad, bias_grad = norm_back(normed_grad, mixer_normal, mixer_scale, factors)
-    residual_grad = upstream + mixer_back
-    branch_grad = residual_grad.astype(jnp.bfloat16)
-    mixing_grad = jnp.einsum(
-        "td,te->de", mixed_rows, branch_grad, preferred_element_type=jnp.float32
-    )
-    mixed_grad = jnp.einsum(
-        "te,de->td", branch_grad, mixing, preferred_element_type=jnp.float32
-    ).astype(jnp.bfloat16)
-    joint_grad = jnp.concatenate(
-        attend_backward(joint, mixed_rows, mixed_grad, logs, lengths[0]), axis=1
-    )
-    projection_grad = jnp.einsum("td,te->de", entry, joint_grad, preferred_element_type=jnp.float32)
-    entry_back = jnp.einsum("te,de->td", joint_grad, projection, preferred_element_type=jnp.float32)
-    entry_input, gain_grad, shift_grad = norm_back(entry_back, entry_normal, entry_scale, gains)
-    token_grad = residual_grad + entry_input
-    layer_output = (residual + gates[:, None] * unsort(made_own, made_came)).astype(jnp.bfloat16)
-    summed = lax.psum(
-        (
-            gain_grad,
-            shift_grad,
-            projection_grad,
-            mixing_grad,
-            factor_grad,
-            bias_grad,
-            centroid_grad,
-            balance_part,
-        ),
-        ("expert", "tensor"),
+    layer_output, token_grad, vectors, up_grad, down_grad, shared, *_ = rear_stage(
+        tokens, gains, projection, mixing, factors, biases, centroids, routes, lengths, cotangent,
+        flipped, joint, mixed, logs, residual, place, loads, dots, back, made, near, far, experts, slabs, total_tokens,
+    )
+    mixing_grad = shared[0].astype(jnp.float32)
+    projection_grad = (
+        shared[1:].reshape(3, width, 3, width // 3).transpose(1, 2, 0, 3).reshape(width, 3 * width).astype(jnp.float32)
     )
     return (
         layer_output,
-        summed[7],
+        vectors[4, 0],
         token_grad,
-        summed[0],
-        summed[1],
-        summed[2],
-        summed[3],
-        summed[4],
-        summed[5],
-        summed[6],
-        up_down[:width][None],
-        jnp.concatenate((up_down[width : width + half], up_down[width + half :]), axis=1)[None],
+        vectors[0],
+        vectors[1],
+        projection_grad,
+        mixing_grad,
+        vectors[2],
+        vectors[3],
+        vectors[8 : 8 + experts],
+        up_grad[None],
+        down_grad[None],
     )
 
 

time: 650 us -> 502 us (0.77)
  Pallas kernels: 244 us -> 439 us
  waiting for transfers between devices: 153 us -> 0 us
  blocking collectives: 68.6 us -> 0 us
  matrix products: 50.1 us -> 0 us
  other arithmetic: 44.8 us -> 9.01 us
  starting transfers between devices: 34.9 us -> 0 us
  between operations: 15.4 us -> 1.13 us
  local copies, waits for them, and re-layouts: 29.4 us -> 43 us
    pallas_call x1, Pallas kernels: 31.6 us -> 226 us  [rear_stage(): pl.pallas_call(partial(rear_kernel, planes, slabs, total_tokens), out_sha...]
    psum x1 -> x0, waiting for transfers between devices: 81.4 us -> none  [per_device(): lax.psum((gain_grad, shift_grad, projection_grad, mixing_grad, factor_gra...]
    ppermute x22 -> x0, waiting for transfers between devices: 72.1 us -> none  [the longest x6 40.8 us: reduce_weights(): came = lax.ppermute(total.astype(jnp.bfloat16), 'expert', pairs)]
    psum x1 -> x0, blocking collectives: 68.6 us -> none  [per_device(): lax.psum((gain_grad, shift_grad, projection_grad, mixing_grad, factor_gra...]
    dot_general x10 -> x0, matrix products: 50.1 us -> none  [the longest x2 12.2 us: unsort(): jnp.dot(back_order, high, preferred_element_type=jnp.float32)]
    ppermute x22 -> x0, starting transfers between devices: 34.9 us -> none  [the longest x6 16.8 us: reduce_weights(): came = lax.ppermute(total.astype(jnp.bfloat16), 'expert', pairs)]
    convert_element_type x8 -> x2, other arithmetic: 24.4 us -> 8.41 us  [the longest x1 5.56 us: per_device(): shared[1:].reshape(3, width, 3, width // 3).transpose(1, 2, 0, 3)]
    convert_element_type x0 -> x2, local copies, waits for them, and re-layouts: none -> 14.5 us  [per_device(): shared[1:].reshape(3, width, 3, width // 3).transpose(1, 2, 0, 3)]
  transfers between devices with their start and end apart: 23 -> 0, of which waited for: 9 -> 0; matrix products, arithmetic and copies ran while one was open for 16% -> 0% of each run, Pallas kernels for 5% -> 0%
where the time goes in v3:
time: 502 us; the launch traced here: 492 us
  Pallas kernels  439 us (87%)
  local copies, waits for them, and re-layouts  43 us (9%)
  other arithmetic  9.01 us (2%)
    pallas_call x1, Pallas kernels, rear_stage(): pl.pallas_call(partial(rear_kernel, planes, slabs, total_tokens), out_sha...  226 us
    pallas_call x1, Pallas kernels, front_stage(): pl.pallas_call(partial(front_kernel, planes, slabs), out_shape=[o[0] for...  140 us
    pallas_call x1, Pallas kernels, expert_stage(): pl.pallas_call(partial(expert_kernel_body, experts, sources, rows, limit,...  73.1 us
    unnamed x15, local copies, waits for them, and re-layouts  16.6 us
    convert_element_type x2, local copies, waits for them, and re-layouts, per_device(): shared[1:].reshape(3, width, 3, width // 3).transpose(1, 2, 0, 3)  14.5 us

profile of v3, /device:TPU:0, one launch (start us, length us, event | category | flops | bytes accessed | tf_op | source)
XLA Modules:
  0.0 492.4 jit_solution(15273613720973291477)
XLA Ops:
  0.6 1.3 reshape.52.gains_ref
  1.9 1.3 reshape.53.factors_ref
  3.2 1.3 reshape.54.biases_ref
  4.5 1.3 reshape.55.shifts_ref
  5.7 1.3 pad.5.centroids_ref
  7.0 1.8 copy.29.route_ref
  8.8 140.0 %shard_map.220 = (bf16[768,1152]{1,0:T(8,128)(2,1)}, bf16[1152,2304]{1,0:T(8,128)(2,1)}, bf16[1152,768]{1,0:T(8,128)(2,1)}, f32[6,2,1152]{2,1,0:T(2,128)}, f32[1...) custom-call(s32[4]{0:T(128)} %bitcast.22, ...), custom_call_target="tpu_custom_call" | custom-call | tf_op jit(solution)/shard_map/pallas_call | solution.py:681
  148.8 0.7 slice.30
  149.5 0.7 slice.31
  150.2 0.1 convert_element_type.28
  150.3 0.6 pad_add_fusion.meta_ref
  150.9 73.1 %shard_map.221 = (bf16[4,1216,768]{2,1,0:T(8,128)(2,1)}, bf16[4,1216,768]{2,1,0:T(8,128)(2,1)}, f32[4,8,1216]{2,1,0:T(8,128)}, bf16[4,1536,384]{2,1,0:T(8,128)(2,1)}, bf16[4,1536,384]{2,1,0:T(8,128)(2,1)}) custom-call(s32[17]{0:T(128)} %pad_add_fusion.meta_ref, bf16[1216,768]{1,0:T(8,128)(2,1)} %get-tuple-element.49.refs_0_, ...), custom_call_target="tpu_custom_call" | custom-call | flops 34426847232 | bytes 100000000 | tf_op jit(solution)/shard_map/pallas_call | solution.py:1626
  224.0 226.1 %shard_map.222 = (bf16[1152,768]{1,0:T(8,128)(2,1)}, f32[1152,768]{1,0:T(8,128)}, f32[16,768]{1,0:T(8,128)}, f32[768,384]{1,0:T(8,128)}, f32[384,768]{1,0:T(8,12...) custom-call(s32[4]{0:T(128)} %bitcast.23, ...), custom_call_target="tpu_custom_call" | custom-call | tf_op jit(solution)/shard_map/pallas_call | solution.py:1340
  450.1 1.2 slice.32
  451.3 1.3 slice.39
  452.6 1.5 slice_reduce_fusion
  454.2 2.8 bitcast_convert_fusion
  457.0 5.6 %slice_convert_fusion = f32[3,768,768]{2,1,0:T(8,128)} fusion(bf16[4,768,768]{2,1,0:T(8,128)(2,1)} %get-tuple-element.65), kind=kLoop, calls=%fused_computation | loop fusion | flops 1769472 | bytes 10616832 | tf_op jit(solution)/shard_map/convert_element_type | solution.py:1702
  462.6 8.1 %copy.30 = f32[3,768,768]{1,2,0:T(8,128)} copy(f32[3,768,768]{2,1,0:T(8,128)} %slice_convert_fusion) | data formatting | bytes 14155776 | tf_op jit(solution)/shard_map/convert_element_type | solution.py:1702
  470.7 6.4 %copy.31 = f32[768,3,3,256]{0,3,2,1:T(8,128)} copy(f32[768,3,3,256]{0,3,1,2:T(8,128)} %bitcast.16) | data formatting | bytes 14155776 | tf_op jit(solution)/shard_map/convert_element_type | solution.py:1702
  477.1 0.0 copy-start.1
  477.1 8.1 %copy.32 = f32[768,2304]{1,0:T(8,128)} copy(f32[768,2304]{0,1:T(8,128)} %bitcast.17) | data formatting | bytes 14155776
  485.2 0.0 copy-done.1
  485.2 0.0 copy-start
  485.2 1.2 copy.40
  486.4 1.4 copy-done
  487.8 0.0 copy-start.3
  487.8 0.0 copy-start.2
  487.8 1.8 copy.41
  489.6 0.3 copy-done.3
  489.9 1.0 copy.42
  490.9 0.0 copy-done.2
  490.9 1.0 copy.43
  (2 shorter events, 0.0 us)
Async XLA Ops:
  477.1 8.1 %copy-start.1 = (bf16[1152,768]{1,0:T(8,128)(2,1)S(1)}, bf16[1152,768]{1,0:T(8,128)(2,1)}, u32[]{:S(2)}) copy-start(bf16[1152,768]{1,0:T(8,128)(2,1)} %get-tuple-element.96) | copy-start | bytes 5308420
  485.2 2.6 copy-start
  487.8 2.1 copy-start.3
  487.8 3.1 copy-start.2
